TPU v7x, 256 devices: a whole 4x4x8 slice. The times are simulated.
256 devices in a mesh: blk: 8 (over y, x_lo), cross: 32 (over x_hi, z, core).
Axes of the slice: x: 4 (x_hi: 2, x_lo: 2; x = x_hi * 2 + x_lo), y: 4, z: 8, core: 2. Of those that a mesh axis runs over, the one named last changes fastest.
Arguments:
- right_side: float32 [16, 32, 512, 256], P('blk', 'cross'), may hold values from -6 to 6
- schur_inverse: bfloat16 [16, 32, 1024, 1024], P('blk', 'cross'), may hold values from -1 to 3, as said below
- schur: bfloat16 [16, 32, 1024, 1024], P('blk', 'cross'), may hold values from -1 to 3, as said below
- coarse_basis: float32 [16, 32, 4, 512], P('blk', 'cross'), may hold values from -1.25 to 1.25
- occupancy: int32 [16, 32, 512], P('blk', 'cross'), may hold values 0 or 1
- perm_left: int32 [16, 32, 256], P('blk', 'cross'), may hold values from 0 to 255, each once within a row
- perm_down: int32 [16, 32, 256], P('blk', 'cross'), may hold values from 0 to 255, each once within a row
- corner_number: int32 [512], replicated, may hold values from 0 to 511, each once
- coarse_inverse: float32 [512, 512], replicated, may hold values from -1 to 3, as said below
Outputs:
- multipliers: float32 [16, 32, 512, 256], P('blk', 'cross')
Inputs may be any that keep to these rules, and one draw needn't show every extreme that they name: `perm_left`: each row holds every number 0 to 255 once. `perm_down`: each row holds every number 0 to 255 once. `corner_number`: holds every number 0 to 511 once. `schur_inverse`: every block is symmetric positive definite. `schur`: every block is symmetric positive definite. `coarse_inverse`: symmetric positive definite.
All inputs are finite; a program needn't handle non-finite values. No bound on the sum of `occupancy` on one device may be relied on, other than what follows from the above.
Results may differ from a plain program's by a relative error of at most 0.0023.
The roundings to bfloat16 on the way count: a program that leaves them out, or rounds other values in their place, can miss the bound.
Values sent between devices are 32-bit elements; how exact they have to be, the bound alone decides.
No kernel may reach another device: no remote copies, remote signals or barrier semaphores. Data moves between devices by JAX's collectives and lax.ppermute only.
A program may use at most 64 MiB of HBM per device.

v0:
```python
import jax
import jax.numpy as jnp
from jax import lax
from jax.sharding import PartitionSpec as P

ITERS = 2


exact_mode = lax.Precision.HIGHEST


def from_behind(block, axis, distance):
    devices = range(lax.axis_size(axis))
    route = [((i - distance) % len(devices), i) for i in devices]
    return lax.ppermute(block, axis, route)


def rows_by(face, order):
    return jax.vmap(lambda block, chosen: jnp.take(block, chosen, axis=0))(face, order)


def spread(multiplier, left_order, down_order):
    faces = multiplier.shape[1] // 2
    right = multiplier[:, :faces]
    upper = multiplier[:, faces:]
    from_left = from_behind(right, "cross", 1)
    below_first = from_behind(upper[-1], "blk", 1)
    from_down = jnp.concatenate([below_first[None], upper[:-1]], axis=0)
    left = -rows_by(from_left, left_order)
    down = -rows_by(from_down, down_order)
    return jnp.concatenate([left, right, down, upper], axis=1)


def jump(image, left_inverse, down_inverse):
    faces = image.shape[1] // 4
    left = rows_by(image[:, :faces], left_inverse)
    down = rows_by(image[:, 2 * faces : 3 * faces], down_inverse)
    from_right = from_behind(left, "cross", -1)
    above_last = from_behind(down[0], "blk", -1)
    from_up = jnp.concatenate([down[1:], above_last[None]], axis=0)
    return jnp.concatenate(
        [image[:, faces : 2 * faces] - from_right, image[:, 3 * faces :] - from_up], axis=1
    )


def inner_progress(residual, smoothed):
    return lax.psum(jnp.sum(residual * smoothed, axis=(0, 1)), ("blk", "cross"))


def inner_curvature(direction, image):
    return lax.psum(jnp.sum(direction * image, axis=(0, 1)), ("blk", "cross"))


def on_device(
    right_side,
    schur_inverse,
    schur,
    coarse_basis,
    occupancy,
    perm_left,
    perm_down,
    corner_number,
    coarse_inverse,
):
    residual = right_side[:, 0]
    inverse_blocks = schur_inverse[:, 0]
    schur_blocks = schur[:, 0]
    basis_rows = coarse_basis[:, 0]
    weight = (1.0 / (1.0 + occupancy[:, 0].astype(jnp.float32)))[:, :, None]
    left_order = perm_left[:, 0]
    down_order = perm_down[:, 0]
    left_inverse = jnp.argsort(left_order, axis=-1)
    down_inverse = jnp.argsort(down_order, axis=-1)
    blocks = residual.shape[0]
    columns_rhs = residual.shape[2]
    axial_groups = lax.axis_size("blk")
    sector_count = lax.axis_size("cross")
    axial_count = blocks * axial_groups
    corner_count = coarse_inverse.shape[0]
    numbers = corner_number.reshape(axial_count, sector_count)
    group_index = lax.axis_index("blk")
    sector_index = lax.axis_index("cross")
    axial_rows = (group_index * blocks + jnp.arange(blocks, dtype=jnp.int32)) % axial_count
    axial_next = (axial_rows + 1) % axial_count
    sector_next = (sector_index + 1) % sector_count
    corner_ids = jnp.stack(
        [
            numbers[axial_rows, sector_index],
            numbers[axial_rows, sector_next],
            numbers[axial_next, sector_index],
            numbers[axial_next, sector_next],
        ],
        axis=1,
    ).reshape(-1)
    coarse_rows = jnp.take(coarse_inverse, corner_ids, axis=0)

    def coarse_values(loads):
        flat_loads = loads.reshape(-1, columns_rhs)
        onehot = (corner_ids[:, None] == jnp.arange(corner_count, dtype=jnp.int32)[None, :]).astype(
            jnp.float32
        )
        partial_sums = jnp.einsum("kc,kr->cr", onehot, flat_loads, precision=exact_mode)
        corner_sums = lax.psum(partial_sums, ("blk", "cross"))
        values = jnp.dot(
            coarse_rows, corner_sums, precision=exact_mode, preferred_element_type=jnp.float32
        )
        return values.reshape(loads.shape)

    def precondition(current):
        operand = spread(weight * current, left_order, down_order).astype(jnp.bfloat16)
        image = jnp.einsum(
            "kmn,knr->kmr", schur_blocks, operand, preferred_element_type=jnp.float32
        )
        local = weight * jump(image, left_inverse, down_inverse)
        loads = jnp.einsum("kcm,kmr->kcr", basis_rows, current, precision=exact_mode)
        values = coarse_values(loads)
        return local + jnp.einsum("kcm,kcr->kmr", basis_rows, values, precision=exact_mode)

    multipliers = jnp.zeros_like(residual)
    smoothed = precondition(residual)
    progress_now = inner_progress(residual, smoothed)
    direction = smoothed
    spread_field = spread(smoothed, left_order, down_order)
    for step in range(ITERS):
        operate_image = jnp.einsum(
            "kmn,knr->kmr",
            inverse_blocks,
            spread_field.astype(jnp.bfloat16),
            preferred_element_type=jnp.float32,
        )
        image = jump(operate_image, left_inverse, down_inverse)
        alpha = progress_now / inner_curvature(direction, image)
        multipliers = multipliers + alpha * direction
        if step + 1 < ITERS:
            residual = residual - alpha * image
            smoothed = precondition(residual)
            progress_next = inner_progress(residual, smoothed)
            ratio = progress_next / progress_now
            direction = smoothed + ratio * direction
            spread_field = spread(direction, left_order, down_order)
            progress_now = progress_next
    return multipliers[:, None]


def solution(mesh):
    placed = (
        P("blk", "cross", None, None),
        P("blk", "cross", None, None),
        P("blk", "cross", None, None),
        P("blk", "cross", None, None),
        P("blk", "cross", None),
        P("blk", "cross", None),
        P("blk", "cross", None),
        P(),
        P(),
    )
    return jax.shard_map(
        on_device,
        mesh=mesh,
        in_specs=placed,
        out_specs=P("blk", "cross", None, None),
        check_vma=False,
    )
```

profile of v0, /device:TPU:1, one launch (start us, length us, event | category | flops | bytes accessed | tf_op | source)
XLA Modules:
  0.0 925.8 jit_solution(309517824946467220)
XLA Ops:
  28.9 3.9 gather_fusion.6
  35.0 3.9 gather_fusion.5
  45.6 3.9 gather_fusion.7
  51.2 7.8 collective-permute-done.2
  61.3 3.9 gather_fusion.8
  70.4 206.6 %all-reduce.8.cloned.1.call-done = f32[512,256]{1,0:T(8,128)} async-done(((f32[512,256]{1,0:T(8,128)}), f32[512,256]{1,0:T(8,128)}) %all-reduce.8.cloned.1.call-update) | async-done | bytes 524304 | tf_op jit(solution)/shard_map/psum | solution.py:103
  289.7 3.9 gather_fusion.10
  295.1 3.9 gather_fusion.9
  299.3 3.6 fusion.14
  304.6 3.9 gather_fusion.11
  308.8 4.9 collective-permute-start.6
  313.7 6.2 collective-permute-done.6
  323.2 6.4 gather_fusion.12
  331.0 5.2 collective-permute-done.7
  337.6 80.6 %all-reduce.4 = (f32[256]{0:T(256)S(1)}, f32[256]{0:T(256)S(1)}) all-reduce(f32[256]{0:T(256)S(1)} %get-tuple-element.11, f32[256]{0:T(256)S(1)} %get-tuple-element.10), channel_id=1, replica_groups=mesh['blk'=8,'cross'=32] {'blk','cross'}, use_global_device_ids=true, to_apply=%region_4.6 | all-reduce | flops 512 | bytes 4096 | tf_op jit(solution)/shard_map/psum | solution.py:47
  421.3 12.7 %collective-permute-done.9 = f32[256,256]{0,1:T(8,128)S(1)} collective-permute-done((f32[256,256]{0,1:T(8,128)S(1)}, f32[256,256]{0,1:T(8,128)S(1)}, u32[]{:S(2)}, u32[]{:S(2)}) %collective-permute-start.9) | collective-permute-done | bytes 262176 | tf_op jit(solution)/shard_map/ppermute | solution.py:15
  434.2 3.9 gather_fusion.14
  438.6 3.9 gather_fusion.13
  447.9 3.9 gather_fusion.15
  456.5 4.2 collective-permute-done.10
  464.1 6.4 gather_fusion.16
  472.1 225.9 %all-reduce.10.cloned.1.call-done = f32[512,256]{1,0:T(8,128)} async-done(((f32[512,256]{1,0:T(8,128)}), f32[512,256]{1,0:T(8,128)}) %all-reduce.10.cloned.1.call-update) | async-done | bytes 524304 | tf_op jit(solution)/shard_map/psum | solution.py:103
  703.4 77.3 %psum.46 = f32[256]{0:T(256)S(1)} all-reduce(f32[256]{0:T(256)S(1)} %get-tuple-element.48), channel_id=1, replica_groups=mesh['blk'=8,'cross'=32] {'blk','cross'}, use_global_device_ids=true, to_apply=%region_9.11 | all-reduce | flops 256 | bytes 2048 | tf_op jit(solution)/shard_map/psum | solution.py:47
  784.8 6.9 collective-permute-done.13
  791.9 3.9 gather_fusion.18
  797.3 3.9 gather_fusion.17
  801.5 3.7 fusion.17
  806.8 3.9 gather_fusion.19
  811.0 7.1 collective-permute-start.14
  821.9 3.9 gather_fusion.20
  826.3 5.2 collective-permute-done.15
  832.8 81.7 %psum.47 = f32[256]{0:T(256)S(1)} all-reduce(f32[256]{0:T(256)S(1)} %fusion.50), channel_id=1, replica_groups=mesh['blk'=8,'cross'=32] {'blk','cross'}, use_global_device_ids=true, to_apply=%region_11.13 | all-reduce | flops 256 | bytes 2048 | tf_op jit(solution)/shard_map/psum | solution.py:51
  (202 shorter events, 102.5 us)
Async XLA Ops:
  7.4 62.4 %copy-start = (f32[512,512]{1,0:T(8,128)S(1)}, f32[512,512]{1,0:T(8,128)}, u32[]{:S(2)}) copy-start(f32[512,512]{1,0:T(8,128)} %param.19) | copy-start | bytes 3145732
  7.4 18.9 %sort.30.cloned.1.call-start = ((), (), s32[]{:S(2)}) async-start(), calls=%async_computation.2 | async-start | bytes 12320 | tf_op jit(solution)/shard_map/jit(argsort)/sort | solution.py:72
  9.3 40.5 %sort.32.cloned.1.call-start = ((), (), s32[]{:S(2)}) async-start(), calls=%async_computation.3 | async-start | bytes 12320 | tf_op jit(solution)/shard_map/jit(argsort)/sort | solution.py:73
  11.7 6.3 copy-start.14
  11.7 7.6 copy-start.15
  11.8 10.2 %copy-start.8 = (f32[2,1,4,512]{3,2,1,0:T(4,128)S(1)}, f32[2,1,4,512]{3,2,1,0:T(4,128)}, u32[]{:S(2)}) copy-start(f32[2,1,4,512]{3,2,1,0:T(4,128)} %param.14) | copy-start | bytes 49156
  12.6 15.1 %collective-permute-start.1 = (f32[256,256]{0,1:T(8,128)}, f32[256,256]{0,1:T(8,128)}, u32[]{:S(2)}, u32[]{:S(2)}) collective-permute-start(f32[256,256]{0,1:T(8,128)} %get-tuple-element.38), channel_id=1, source_target_pairs={{224,0},{0,32},{32,64},{64,96},{96,128},{128,160},{160,192},{192,2... | collective-permute-start | bytes 786440 | tf_op jit(solution)/shard_map/ppermute | solution.py:15
  15.4 18.4 %collective-permute-start = (f32[2,256,256]{1,2,0:T(8,128)}, f32[2,256,256]{1,2,0:T(8,128)}, u32[]{:S(2)}, u32[]{:S(2)}) collective-permute-start(f32[2,256,256]{1,2,0:T(8,128)} %slice.214), channel_id=1, source_target_pairs={{31,0},{0,1},{1,2},{2,3},{3,4},{4,5},{5,6},{6,7},{7,8},{8,9},{9,10... | collective-permute-start | bytes 1572872 | tf_op jit(solution)/shard_map/ppermute | solution.py:15
  19.1 257.9 %all-reduce.8.cloned.1.call-start = ((), (), s32[]{:S(2)}) async-start(), calls=%async_computation | async-start | bytes 1048576 | tf_op jit(solution)/shard_map/psum | solution.py:103
  19.3 5.9 copy-start.13
  25.2 672.8 %all-reduce.10.cloned.1.call-start = ((), (), s32[]{:S(2)}) async-start(), calls=%async_computation.1 | async-start | bytes 1048576 | tf_op jit(solution)/shard_map/psum | solution.py:103
  39.0 1.4 copy-start.9
  44.0 1.4 copy-start.3
  49.7 9.3 %collective-permute-start.2 = (f32[2,256,256]{1,2,0:T(8,128)S(1)}, f32[2,256,256]{1,2,0:T(8,128)S(1)}, u32[]{:S(2)}, u32[]{:S(2)}) collective-permute-start(f32[2,256,256]{1,2,0:T(8,128)S(1)} %broadcast_select_fusion.7), channel_id=1, source_target_pairs={{1,0},{2,1},{3,2},{4,3},{5,4},{6,5},{7,6},{8,7},{9,8},{10,9},{11,1... | collective-permute-start | bytes 1572872 | tf_op jit(solution)/shard_map/ppermute | solution.py:15
  67.4 211.1 %collective-permute-start.3 = (f32[256,256]{0,1:T(8,128)S(1)}, f32[256,256]{0,1:T(8,128)S(1)}, u32[]{:S(2)}, u32[]{:S(2)}) collective-permute-start(f32[256,256]{0,1:T(8,128)S(1)} %get-tuple-element.47), channel_id=1, source_target_pairs={{32,0},{64,32},{96,64},{128,96},{160,128},{192,160},{224,192},{0,2... | collective-permute-start | bytes 786440 | tf_op jit(solution)/shard_map/ppermute | solution.py:15
  281.7 7.7 collective-permute-start.5
  283.6 10.3 %collective-permute-start.4 = (f32[2,256,256]{1,2,0:T(8,128)}, f32[2,256,256]{1,2,0:T(8,128)}, u32[]{:S(2)}, u32[]{:S(2)}) collective-permute-start(f32[2,256,256]{1,2,0:T(8,128)} %slice.224), channel_id=1, source_target_pairs={{31,0},{0,1},{1,2},{2,3},{3,4},{4,5},{5,6},{6,7},{7,8},{8,9},{9,10... | collective-permute-start | bytes 1572872 | tf_op jit(solution)/shard_map/ppermute | solution.py:15
  308.8 11.1 %collective-permute-start.6 = (f32[2,256,256]{1,2,0:T(8,128)S(1)}, f32[2,256,256]{1,2,0:T(8,128)S(1)}, u32[]{:S(2)}, u32[]{:S(2)}) collective-permute-start(f32[2,256,256]{1,2,0:T(8,128)S(1)} %broadcast_select_fusion.5), channel_id=1, source_target_pairs={{1,0},{2,1},{3,2},{4,3},{5,4},{6,5},{7,6},{8,7},{9,8},{10,9},{11,1... | collective-permute-start | bytes 1572872 | tf_op jit(solution)/shard_map/ppermute | solution.py:15
  330.9 5.3 collective-permute-start.7
  419.4 14.5 %collective-permute-start.9 = (f32[256,256]{0,1:T(8,128)S(1)}, f32[256,256]{0,1:T(8,128)S(1)}, u32[]{:S(2)}, u32[]{:S(2)}) collective-permute-start(f32[256,256]{0,1:T(8,128)S(1)} %get-tuple-element.30), channel_id=1, source_target_pairs={{224,0},{0,32},{32,64},{64,96},{96,128},{128,160},{160,192},{192,2... | collective-permute-start | bytes 786440 | tf_op jit(solution)/shard_map/ppermute | solution.py:15
  419.6 18.8 %collective-permute-start.8 = (f32[2,256,256]{1,2,0:T(8,128)S(1)}, f32[2,256,256]{1,2,0:T(8,128)S(1)}, u32[]{:S(2)}, u32[]{:S(2)}) collective-permute-start(f32[2,256,256]{1,2,0:T(8,128)S(1)} %slice.234), channel_id=1, source_target_pairs={{31,0},{0,1},{1,2},{2,3},{3,4},{4,5},{5,6},{6,7},{7,8},{8,9},{9,10... | collective-permute-start | bytes 1572872 | tf_op jit(solution)/shard_map/ppermute | solution.py:15
  438.6 4.2 copy-start.10
  438.6 4.2 copy-start.11
  451.8 2.4 copy-start.2
  452.1 8.7 collective-permute-start.10
  471.8 227.6 %collective-permute-start.11 = (f32[256,256]{0,1:T(8,128)S(1)}, f32[256,256]{0,1:T(8,128)S(1)}, u32[]{:S(2)}, u32[]{:S(2)}) collective-permute-start(f32[256,256]{0,1:T(8,128)S(1)} %get-tuple-element.43), channel_id=1, source_target_pairs={{32,0},{64,32},{96,64},{128,96},{160,128},{192,160},{224,192},{0,2... | collective-permute-start | bytes 786440 | tf_op jit(solution)/shard_map/ppermute | solution.py:15
  782.2 9.5 %collective-permute-start.13 = (f32[256,256]{0,1:T(8,128)S(1)}, f32[256,256]{0,1:T(8,128)S(1)}, u32[]{:S(2)}, u32[]{:S(2)}) collective-permute-start(f32[256,256]{0,1:T(8,128)S(1)} %get-tuple-element.26), channel_id=1, source_target_pairs={{224,0},{0,32},{32,64},{64,96},{96,128},{128,160},{160,192},{192,2... | collective-permute-start | bytes 786440 | tf_op jit(solution)/shard_map/ppermute | solution.py:15
  783.8 12.3 %collective-permute-start.12 = (f32[2,256,256]{1,2,0:T(8,128)}, f32[2,256,256]{1,2,0:T(8,128)}, u32[]{:S(2)}, u32[]{:S(2)}) collective-permute-start(f32[2,256,256]{1,2,0:T(8,128)} %slice.244), channel_id=1, source_target_pairs={{31,0},{0,1},{1,2},{2,3},{3,4},{4,5},{5,6},{6,7},{7,8},{8,9},{9,10... | collective-permute-start | bytes 1572872 | tf_op jit(solution)/shard_map/ppermute | solution.py:15
  811.0 8.7 collective-permute-start.14
  826.1 6.5 copy-start.7
  826.2 5.3 collective-permute-start.15
  914.5 3.7 copy-start.1
  (4 other events, 4.8 us)
Sparse Core Ops, SparseCore 0:
  10.5 2.5 sort.34.cloned.1.call-done
  19.3 2.6 sort.36.cloned.1.call-done
  (2 shorter events, 0.0 us)
Sparse Core Ops, SparseCore 1:
  25.3 251.7 all-reduce.7
  456.6 241.3 all-reduce.9
where the time goes:
time: 936 us; the launch traced here: 926 us
  waiting for transfers between devices  486 us (52%)
  blocking collectives  240 us (26%)
  local copies, waits for them, and re-layouts  107 us (11%)
  matrix products  26.7 us (3%)
  starting transfers between devices  26 us (3%)
  other arithmetic  24.8 us (3%)
  between operations  16.1 us (2%)
    psum x2, waiting for transfers between devices, coarse_values(): corner_sums = lax.psum(partial_sums, ('blk', 'cross'))  433 us
    psum x2, blocking collectives, inner_progress(): return lax.psum(jnp.sum(residual * smoothed, axis=(0, 1)), ('blk', 'cross'))  158 us
    psum x1, blocking collectives, inner_curvature(): return lax.psum(jnp.sum(direction * image, axis=(0, 1)), ('blk', 'cross'))  81.7 us
    gather x32, local copies, waits for them, and re-layouts, rows_by(): jnp.take(block, chosen, axis=0)  74.4 us
    ppermute x16, waiting for transfers between devices, from_behind(): return lax.ppermute(block, axis, route)  53.3 us
    ppermute x16, starting transfers between devices, from_behind(): return lax.ppermute(block, axis, route)  25.9 us
  transfers between devices with their start and end apart: 18, of which 11 were waited for; matrix products, arithmetic and copies ran while one was open for 8% of the time, Pallas kernels for 0%

commit v1 on v0

v1 whole, which is shorter than its diff:
```python
import functools

import jax
import jax.numpy as jnp
import numpy as np
from jax import lax
from jax.experimental import pallas as pl
from jax.experimental.pallas import tpu as pltpu
from jax.sharding import Mesh
from jax.sharding import PartitionSpec as P

SPLIT = {"y": 4, "xl": 2, "xh": 2, "z": 8, "c": 2}
BLK = ("y", "xl")
CROSS = ("xh", "z", "c")
NEAR = ("z", "c")
FAR = ("y", "xl", "xh")
F = 256
R = 256
CORNERS = 512
EXACT = lax.Precision.HIGHEST
F32 = jnp.float32
BF16 = jnp.bfloat16

FACES = 7
SIDES = ((4, 0, 6, 2), (5, 1, 2, 3))
OWNER = ((0, 0), (1, 0), (0, 0), (1, 0), (0, -1), (1, -1), (-1, 0))


def slot(axial, sector):
    return (axial + 1) * 3 + sector + 1


SLOTS = 16


def face_slots(face):
    axial, sector = OWNER[face]
    return [slot(axial + da, sector + ds) for da in (0, 1) for ds in (0, 1)]


def call(kernel, outs, *args, flops=0, smem=()):
    size = sum(int(np.prod(a.shape)) * a.dtype.itemsize for a in args)
    size += sum(int(np.prod(s)) * jnp.dtype(d).itemsize for s, d in outs)
    return pl.pallas_call(
        kernel,
        out_shape=[jax.ShapeDtypeStruct(s, d) for s, d in outs],
        in_specs=[
            pl.BlockSpec(memory_space=pltpu.SMEM if i in smem else pltpu.VMEM)
            for i in range(len(args))
        ],
        out_specs=[pl.BlockSpec(memory_space=pltpu.VMEM)] * len(outs),
        compiler_params=pltpu.CompilerParams(vmem_limit_bytes=40 * 1024 * 1024),
        cost_estimate=pl.CostEstimate(flops=flops, bytes_accessed=size, transcendentals=0),
    )(*args)


def thirds(value):
    high = value.astype(BF16)
    rest = value - high.astype(F32)
    middle = rest.astype(BF16)
    return high, middle, (rest - middle.astype(F32)).astype(BF16)


def nt(left, right):
    return lax.dot_general(left, right, (((1,), (1,)), ((), ())), preferred_element_type=F32)


def tn(left, right):
    return lax.dot_general(left, right, (((0,), (0,)), ((), ())), preferred_element_type=F32)


def nn(left, right):
    return lax.dot_general(left, right, (((1,), (0,)), ((), ())), preferred_element_type=F32)


def pack_kernel(r_ref, occ_ref, basis_ref, right_ref, up_ref, small_right_ref, small_up_ref):
    for k in range(2):
        right_ref[k] = r_ref[k, :F, :]
    up_ref[...] = r_ref[1, F:, :]
    weight = 1.0 / (1.0 + occ_ref[...].astype(F32))
    small_right_ref[...] = jnp.zeros_like(small_right_ref)
    small_up_ref[...] = jnp.zeros_like(small_up_ref)
    for k in range(2):
        small_right_ref[k, 0:4, :] = basis_ref[k, :, :F]
        small_right_ref[k, 4:5, :] = weight[k : k + 1, :F]
    small_up_ref[0:4, :] = basis_ref[1, :, F:]
    small_up_ref[4:5, :] = weight[1:2, F:]


def loads_kernel(r_ref, basis_ref, out_ref):
    out_ref[...] = jnp.zeros_like(out_ref)
    first = jnp.dot(basis_ref[0], r_ref[0], precision=EXACT, preferred_element_type=F32)
    second = jnp.dot(basis_ref[1], r_ref[1], precision=EXACT, preferred_element_type=F32)
    here = slot(0, 0)
    out_ref[here : here + 2, :] = first[0:2]
    here = slot(1, 0)
    out_ref[here : here + 2, :] = first[2:4] + second[0:2]
    here = slot(2, 0)
    out_ref[here : here + 2, :] = second[2:4]


def placed(order_row, scale_row):
    rows = lax.broadcasted_iota(jnp.int32, (F, F), 0)
    onehot = order_row == rows
    if scale_row is None:
        return jnp.where(onehot, -1.0, 0.0).astype(BF16)
    eye = lax.broadcasted_iota(jnp.int32, (F, F), 1) == rows
    column = jnp.sum(jnp.where(eye, scale_row, 0.0), axis=1, keepdims=True)
    return jnp.where(onehot, -column, 0.0).astype(BF16)


def scale_column(row):
    eye = lax.broadcasted_iota(jnp.int32, (F, F), 1) == lax.broadcasted_iota(jnp.int32, (F, F), 0)
    return jnp.sum(jnp.where(eye, row, 0.0), axis=1, keepdims=True)


def reorder_block(s_ref, out_ref, work_ref, k, left_t, down_t, rows_weights):
    work_ref[:, 0:F] = nt(s_ref[k, :, 0:F], left_t).astype(BF16)
    work_ref[:, 2 * F : 3 * F] = nt(s_ref[k, :, 2 * F : 3 * F], down_t).astype(BF16)
    for side in (1, 3):
        part = s_ref[k, :, side * F : (side + 1) * F]
        if rows_weights is not None:
            part = (part.astype(F32) * rows_weights[side]).astype(BF16)
        work_ref[:, side * F : (side + 1) * F] = part
    out_ref[k, 0:F, :] = nn(left_t, work_ref[0:F, :]).astype(BF16)
    out_ref[k, 2 * F : 3 * F, :] = nn(down_t, work_ref[2 * F : 3 * F, :]).astype(BF16)
    for side in (1, 3):
        part = work_ref[side * F : (side + 1) * F, :]
        if rows_weights is not None:
            part = (part.astype(F32) * scale_column(rows_weights[side])).astype(BF16)
        out_ref[k, side * F : (side + 1) * F, :] = part


def reorder_plain_kernel(s_ref, left_ref, down_ref, out_ref):
    def run(work_ref):
        for k in range(2):
            left_t = placed(left_ref[k : k + 1, :], None)
            down_t = placed(down_ref[k : k + 1, :], None)
            reorder_block(s_ref, out_ref, work_ref, k, left_t, down_t, None)

    pl.run_scoped(run, pltpu.VMEM((4 * F, 4 * F), BF16))


def reorder_weighted_kernel(
    s_ref, left_ref, down_ref, occ_ref, basis_ref, from_left_ref, from_down_ref, out_ref, spread_basis_ref
):
    weight = 1.0 / (1.0 + occ_ref[...].astype(F32))
    down_weight = (from_down_ref[4:5, :], weight[0:1, F:])

    def run(work_ref):
        for k in range(2):
            left_t = placed(left_ref[k : k + 1, :], from_left_ref[k, 4:5, :])
            down_t = placed(down_ref[k : k + 1, :], down_weight[k])
            rows = {1: weight[k : k + 1, :F], 3: weight[k : k + 1, F:]}
            reorder_block(s_ref, out_ref, work_ref, k, left_t, down_t, rows)

    pl.run_scoped(run, pltpu.VMEM((4 * F, 4 * F), BF16))
    spread_basis_ref[...] = jnp.zeros_like(spread_basis_ref)
    sources = (
        basis_ref[0, :, :F],
        basis_ref[1, :, :F],
        basis_ref[0, :, F:],
        basis_ref[1, :, F:],
        from_left_ref[0, 0:4, :],
        from_left_ref[1, 0:4, :],
        from_down_ref[0:4, :],
    )
    for face in range(FACES):
        for k, row in enumerate(face_slots(face)):
            spread_basis_ref[face, row : row + 1, :] = sources[face][k : k + 1, :]


def corner_onehot(numbers_t, axial, sector, spare):
    wanted = (axial & 15) * 32 + (sector & 31)
    columns = lax.broadcasted_iota(jnp.int32, (wanted.shape[0], CORNERS), 1)
    picks = jnp.where((columns == wanted) & jnp.logical_not(spare), 1.0, 0.0).astype(BF16)
    return nt(picks, numbers_t).astype(BF16)


def coarse_block_kernel(place_ref, numbers_ref, inverse_ref, out_ref):
    blk, xh, near = place_ref[0], place_ref[1], place_ref[2]
    ids = lax.broadcasted_iota(jnp.int32, (CORNERS, CORNERS), 0)
    numbers_t = jnp.where(numbers_ref[...] == ids, 1.0, 0.0).astype(BF16)
    rows = lax.broadcasted_iota(jnp.int32, (16 * SLOTS, 1), 0)
    peer = rows >> 4
    entry = rows & 15
    third = (entry >= 3).astype(jnp.int32) + (entry >= 6).astype(jnp.int32) + (entry >= 9).astype(jnp.int32)
    da = third - 1
    ds = entry - 3 * third - 1
    spare = entry >= 12
    far_rows = corner_onehot(numbers_t, 2 * (peer >> 1) + da, (peer & 1) * 16 + near + ds, spare)
    near_rows = corner_onehot(numbers_t, 2 * blk + da, xh * 16 + peer + ds, spare)
    picked = sum(nn(far_rows, part) for part in thirds(inverse_ref[...])[::-1])
    block = sum(nt(part, near_rows) for part in thirds(picked)[::-1])
    columns = lax.broadcasted_iota(jnp.int32, (16 * SLOTS, 16 * SLOTS), 1) & 15
    passed = (columns == entry) & spare
    out_ref[...] = jnp.where(passed, 1.0, block)


HALVES = [((2, F, R), F32), ((2, F, R), F32), ((F, R), F32), ((F, R), F32), ((F, R), F32)]


def apply_block(s_ref, operand_ref, left_ref, right_ref, up_ref, down_ref, mid_ref):
    for k in range(2):
        sides = [nn(s_ref[k, side * F : (side + 1) * F, :], operand_ref[k]) for side in range(4)]
        left_ref[k] = sides[0]
        right_ref[k] = sides[1]
        if k == 0:
            down_ref[...] = sides[2]
            mid_ref[...] = sides[3]
        else:
            mid_ref[...] += sides[2]
            up_ref[...] = sides[3]


def set_operand(operand_ref, face, value):
    value = value.astype(BF16)
    for k in range(2):
        for side in range(4):
            if SIDES[k][side] == face:
                operand_ref[k, side * F : (side + 1) * F, :] = value


def first_kernel(s_ref, r_ref, from_left_ref, from_down_ref, left_ref, right_ref, up_ref, down_ref, mid_ref):
    def run(operand_ref):
        for k in range(2):
            set_operand(operand_ref, k, r_ref[k, :F, :])
            set_operand(operand_ref, 2 + k, r_ref[k, F:, :])
            set_operand(operand_ref, 4 + k, from_left_ref[k])
        set_operand(operand_ref, 6, from_down_ref[...])
        apply_block(s_ref, operand_ref, left_ref, right_ref, up_ref, down_ref, mid_ref)

    pl.run_scoped(run, pltpu.VMEM((2, 4 * F, R), BF16))


def faces_of(left_ref, right_ref, up_ref, down_ref, mid_ref):
    return (
        right_ref.at[0],
        right_ref.at[1],
        mid_ref,
        up_ref,
        left_ref.at[0],
        left_ref.at[1],
        down_ref,
    )


def others_of(from_left_ref, from_right_ref, from_up_ref, from_down_ref):
    return (
        from_right_ref.at[0],
        from_right_ref.at[1],
        None,
        from_up_ref,
        from_left_ref.at[0],
        from_left_ref.at[1],
        from_down_ref,
    )


def corner_part(spread_basis_ref, face, values):
    return lax.dot_general(
        spread_basis_ref[face], values, (((0,), (0,)), ((), ())), precision=EXACT, preferred_element_type=F32
    )


def own_face(r_ref, face):
    return r_ref[face % 2, (face // 2) * F : (face // 2 + 1) * F, :]


def total(value):
    return jnp.sum(value, axis=0, keepdims=True)


def operate_first_kernel(
    s_ref, basis_ref, r_ref, values_ref, l_ref, r2_ref, u_ref, d_ref, m_ref, fl_ref, fr_ref, fu_ref, fd_ref,
    z_ref, left_ref, right_ref, up_ref, down_ref, mid_ref, message_ref, corners_ref,
):
    corners = jnp.sum(values_ref[...], axis=0)
    corners_ref[...] = corners
    mine = faces_of(l_ref, r2_ref, u_ref, d_ref, m_ref)
    theirs = others_of(fl_ref, fr_ref, fu_ref, fd_ref)

    def run(operand_ref):
        progress = jnp.zeros((1, R), F32)
        for face in range(FACES):
            value = mine[face][...]
            if theirs[face] is not None:
                value = value + theirs[face][...]
            value = value + corner_part(basis_ref, face, corners)
            z_ref[face] = value
            set_operand(operand_ref, face, value)
            if face < 4:
                progress = progress + total(own_face(r_ref, face) * value)
        apply_block(s_ref, operand_ref, left_ref, right_ref, up_ref, down_ref, mid_ref)
        images = faces_of(left_ref, right_ref, up_ref, down_ref, mid_ref)
        loads = jnp.zeros((SLOTS, R), F32)
        curvature = jnp.zeros((1, R), F32)
        for face in range(FACES):
            image = images[face][...]
            loads = loads + jnp.dot(basis_ref[face], image, precision=EXACT, preferred_element_type=F32)
            curvature = curvature + total(z_ref[face] * image)
        message_ref[...] = loads
        message_ref[12:13, :] = progress
        message_ref[13:14, :] = curvature

    pl.run_scoped(run, pltpu.VMEM((2, 4 * F, R), BF16))


def second_kernel(
    s_ref, r_ref, r_left_ref, r_down_ref, values_ref, corners_ref,
    l_ref, r2_ref, u_ref, d_ref, m_ref, fl_ref, fr_ref, fu_ref, fd_ref,
    residual_ref, image_ref, left_ref, right_ref, up_ref, down_ref, mid_ref, next_ref, scalars_ref,
):
    sums = jnp.sum(values_ref[...], axis=0)
    progress, curvature = sums[12:13, :], sums[13:14, :]
    alpha = progress / curvature
    next_ref[...] = corners_ref[...] - alpha * sums
    scalars_ref[...] = jnp.zeros_like(scalars_ref)
    scalars_ref[0:1, :] = progress
    scalars_ref[1:2, :] = curvature
    scalars_ref[2:3, :] = alpha
    mine = faces_of(l_ref, r2_ref, u_ref, d_ref, m_ref)
    theirs = others_of(fl_ref, fr_ref, fu_ref, fd_ref)

    def run(operand_ref):
        for face in range(FACES):
            image = mine[face][...]
            if theirs[face] is not None:
                image = image + theirs[face][...]
            if face < 4:
                start = own_face(r_ref, face)
            elif face < 6:
                start = r_left_ref[face - 4]
            else:
                start = r_down_ref[...]
            value = start - alpha * image
            if face < 4:
                image_ref[face] = image
                residual_ref[face] = value
            set_operand(operand_ref, face, value)
        apply_block(s_ref, operand_ref, left_ref, right_ref, up_ref, down_ref, mid_ref)

    pl.run_scoped(run, pltpu.VMEM((2, 4 * F, R), BF16))


def operate_last_kernel(
    s_ref, basis_ref, corners_ref, z0_ref, residual_ref, image_ref,
    l_ref, r2_ref, u_ref, d_ref, m_ref, fl_ref, fr_ref, fu_ref, fd_ref,
    z_ref, message_ref,
):
    corners = corners_ref[...]
    rows = lax.broadcasted_iota(jnp.int32, corners.shape, 0)
    corners = jnp.where(rows < 12, corners, 0.0)
    mine = faces_of(l_ref, r2_ref, u_ref, d_ref, m_ref)
    theirs = others_of(fl_ref, fr_ref, fu_ref, fd_ref)

    def run(operand_ref, z7_ref, left_ref, right_ref, up_ref, down_ref, mid_ref):
        progress = jnp.zeros((1, R), F32)
        mixed = jnp.zeros((1, R), F32)
        for face in range(FACES):
            value = mine[face][...]
            if theirs[face] is not None:
                value = value + theirs[face][...]
            value = value + corner_part(basis_ref, face, corners)
            z7_ref[face] = value
            set_operand(operand_ref, face, value)
            if face < 4:
                z_ref[face] = value
                progress = progress + total(residual_ref[face] * value)
                mixed = mixed + total(image_ref[face] * value)
        apply_block(s_ref, operand_ref, left_ref, right_ref, up_ref, down_ref, mid_ref)
        images = faces_of(left_ref, right_ref, up_ref, down_ref, mid_ref)
        curvature = jnp.zeros((1, R), F32)
        for face in range(FACES):
            image = images[face][...]
            curvature = curvature + total(z7_ref[face] * image)
            mixed = mixed + total(z0_ref[face] * image)
        message_ref[...] = jnp.zeros_like(message_ref)
        message_ref[0:1, :] = progress
        message_ref[1:2, :] = curvature
        message_ref[2:3, :] = mixed

    pl.run_scoped(
        run,
        pltpu.VMEM((2, 4 * F, R), BF16),
        pltpu.VMEM((FACES, F, R), F32),
        *[pltpu.VMEM(s, d) for s, d in HALVES],
    )


def finish_kernel(z0_ref, z1_ref, scalars_ref, sums_ref, out_ref):
    sums = jnp.sum(sums_ref[...], axis=0)
    progress, curvature, mixed = sums[0:1, :], sums[1:2, :], sums[2:3, :]
    first_progress, first_curvature, alpha = scalars_ref[0:1, :], scalars_ref[1:2, :], scalars_ref[2:3, :]
    ratio = progress / first_progress
    last = progress / (curvature + ratio * (mixed + ratio * first_curvature))
    scale0 = alpha + last * ratio
    for face in range(4):
        out_ref[face % 2, (face // 2) * F : (face // 2 + 1) * F, :] = scale0 * z0_ref[face] + last * z1_ref[face]


def partial_kernel(block_ref, message_ref, out_ref):
    flat = jnp.concatenate([message_ref[i] for i in range(16)], axis=0)
    out = jnp.dot(block_ref[...], flat, precision=EXACT, preferred_element_type=F32)
    for i in range(16):
        out_ref[i] = out[i * SLOTS : (i + 1) * SLOTS]


def sum_kernel(in_ref, out_ref):
    total_rows = jnp.sum(in_ref[...], axis=0)
    for i in range(16):
        out_ref[i] = total_rows


def moved(block, axes, count, distance):
    return lax.ppermute(block, axes, [(i, (i + distance) % count) for i in range(count)])


def exchanged(left, right, up, down):
    return (
        moved(right, CROSS, 32, 1),
        moved(left, CROSS, 32, -1),
        moved(down, BLK, 8, -1),
        moved(up, BLK, 8, 1),
    )


MATMUL_FLOPS = 2 * 2 * (4 * F) * (4 * F) * R


def on_device(r, s_inverse, s, basis, occ, left_order, down_order, numbers, coarse_inverse):
    r, s_inverse, s = r[:, 0], s_inverse[:, 0], s[:, 0]
    basis, occ, left_order, down_order = basis[:, 0], occ[:, 0], left_order[:, 0], down_order[:, 0]
    place = jnp.stack([lax.axis_index(BLK), lax.axis_index("xh"), lax.axis_index(NEAR)]).astype(jnp.int32)

    right, up, small_right, small_up = call(
        pack_kernel,
        [((2, F, R), F32), ((F, R), F32), ((2, 8, F), F32), ((8, F), F32)],
        r, occ, basis,
    )
    small_left = moved(small_right, CROSS, 32, 1)
    small_down = moved(small_up, BLK, 8, 1)
    r_left = moved(right, CROSS, 32, 1)
    r_down = moved(up, BLK, 8, 1)
    (loads,) = call(loads_kernel, [((SLOTS, R), F32)], r, basis)
    (inverse_block,) = call(
        reorder_plain_kernel, [(s_inverse.shape, BF16)], s_inverse, left_order, down_order, flops=2 * MATMUL_FLOPS
    )
    (coarse_block,) = call(
        coarse_block_kernel,
        [((16 * SLOTS, 16 * SLOTS), F32)],
        place, numbers[None, :], coarse_inverse,
        smem=(0,),
    )

    def coarse(message):
        near = lax.all_gather(message, NEAR)
        (partial,) = call(partial_kernel, [((16, SLOTS, R), F32)], coarse_block, near)
        return lax.all_to_all(partial, FAR, 0, 0)

    schur_block, spread_basis = call(
        reorder_weighted_kernel,
        [(s.shape, BF16), ((FACES, SLOTS, F), F32)],
        s, left_order, down_order, occ, basis, small_left, small_down,
        flops=2 * MATMUL_FLOPS,
    )
    values = coarse(loads)

    halves = call(first_kernel, HALVES, schur_block, r, r_left, r_down, flops=MATMUL_FLOPS)
    others = exchanged(*halves[:4])
    z0, *halves, message, corners = call(
        operate_first_kernel,
        [((FACES, F, R), F32), *HALVES, ((SLOTS, R), F32), ((SLOTS, R), F32)],
        inverse_block, spread_basis, r, values, *halves, *others,
        flops=MATMUL_FLOPS,
    )
    others = exchanged(*halves[:4])
    values = coarse(message)
    residual, image, *halves, corners, scalars = call(
        second_kernel,
        [((4, F, R), F32), ((4, F, R), F32), *HALVES, ((SLOTS, R), F32), ((8, R), F32)],
        schur_block, r, r_left, r_down, values, corners, *halves, *others,
        flops=MATMUL_FLOPS,
    )
    others = exchanged(*halves[:4])
    z1, message = call(
        operate_last_kernel,
        [((4, F, R), F32), ((8, R), F32)],
        inverse_block, spread_basis, corners, z0, residual, image, *halves, *others,
        flops=MATMUL_FLOPS,
    )
    near = lax.all_gather(message, NEAR)
    (spread_sums,) = call(sum_kernel, [((16, 8, R), F32)], near)
    sums = lax.all_to_all(spread_sums, FAR, 0, 0)
    (out,) = call(finish_kernel, [((2, 2 * F, R), F32)], z0, z1, scalars, sums)
    return out[:, None]


def solution(mesh):
    split = Mesh(mesh.devices.reshape(tuple(SPLIT.values())), tuple(SPLIT))
    four = P(BLK, CROSS, None, None)
    three = P(BLK, CROSS, None)
    return jax.shard_map(
        on_device,
        mesh=split,
        in_specs=(four, four, four, four, three, three, three, P(), P()),
        out_specs=four,
        check_vma=False,
    )
```

time: 936 us -> 167 us (0.18); the launches traced: 926 us -> 167 us
  waiting for transfers between devices: 486 us -> 26.9 us
  blocking collectives: 240 us -> 73.7 us
  local copies, waits for them, and re-layouts: 107 us -> 17.5 us
  matrix products: 26.7 us -> 0 us
  other arithmetic: 24.8 us -> 0.08 us
  Pallas kernels: 0 us -> 21.8 us
  between operations: 16.1 us -> 0.19 us
    psum x2 -> x0, waiting for transfers between devices: 433 us -> none  [coarse_values(): corner_sums = lax.psum(partial_sums, ('blk', 'cross'))]
    psum x3 -> x0, blocking collectives: 240 us -> none  [the longest x2 158 us: inner_progress(): return lax.psum(jnp.sum(residual * smoothed, axis=(0, 1)), ('blk', 'cross'))]
    gather x37 -> x0, local copies, waits for them, and re-layouts: 77.5 us -> none  [the longest x32 74.4 us: rows_by(): jnp.take(block, chosen, axis=0)]
    all_gather x0 -> x3, blocking collectives: none -> 51.1 us  [the longest x2 35.4 us: coarse(): near = lax.all_gather(message, NEAR)]
    ppermute x16, waiting for transfers between devices: 53.3 us -> 24.9 us  [moved(): lax.ppermute(block, axes, [(i, (i + distance) % count) for i in range(cou...]
    dot_general x12 -> x0, matrix products: 26.7 us -> none  [the longest x2 7.3 us: on_device(): jnp.einsum('kmn,knr->kmr', inverse_blocks, spread_field.astype(jnp.bfloat...]
    all_to_all x0 -> x2, blocking collectives: none -> 22.6 us  [the longest x1 11.4 us: coarse(): return lax.all_to_all(partial, FAR, 0, 0)]
    pallas_call x0 -> x13, Pallas kernels: none -> 21.8 us  [call(): pl.pallas_call(kernel, out_shape=[jax.ShapeDtypeStruct(s, d) for s, d in...]
  transfers between devices with their start and end apart: 18 -> 17, of which waited for: 11 -> 6; matrix products, arithmetic and copies ran while one was open for 8% -> 0% of each run, Pallas kernels for 0% -> 4%
where the time goes in v1:
time: 167 us
  blocking collectives  73.7 us (44%)
  waiting for transfers between devices  26.9 us (16%)
  starting transfers between devices  26.7 us (16%)
  Pallas kernels  21.8 us (13%)
  local copies, waits for them, and re-layouts  17.5 us (10%)
    all_gather x2, blocking collectives, coarse(): near = lax.all_gather(message, NEAR)  35.4 us
    ppermute x16, waiting for transfers between devices, moved(): lax.ppermute(block, axes, [(i, (i + distance) % count) for i in range(cou...  24.9 us
    ppermute x16, starting transfers between devices, moved(): lax.ppermute(block, axes, [(i, (i + distance) % count) for i in range(cou...  23 us
    pallas_call x13, Pallas kernels, call(): pl.pallas_call(kernel, out_shape=[jax.ShapeDtypeStruct(s, d) for s, d in...  21.8 us
    unnamed x34, local copies, waits for them, and re-layouts  17.5 us
    all_gather x1, blocking collectives, on_device(): near = lax.all_gather(message, NEAR)  15.7 us
    all_to_all x1, blocking collectives, coarse(): return lax.all_to_all(partial, FAR, 0, 0)  11.4 us
    all_to_all x1, blocking collectives, on_device(): sums = lax.all_to_all(spread_sums, FAR, 0, 0)  11.2 us
  transfers between devices with their start and end apart: 17, of which 6 were waited for; matrix products, arithmetic and copies ran while one was open for 0% of the time, Pallas kernels for 4%

profile of v1, /device:TPU:1, one launch (start us, length us, event | category | flops | bytes accessed | tf_op | source)
XLA Modules:
  0.0 166.8 jit_solution(2243202819417518835)
XLA Ops:
  0.7 1.2 copy-done.3
  2.7 3.1 %collective-permute-start.2 = (f32[2,256,256]{2,1,0:T(8,128)S(1)}, f32[2,256,256]{2,1,0:T(8,128)S(1)}, u32[]{:S(2)}, u32[]{:S(2)}) collective-permute-start(f32[2,256,256]{2,1,0:T(8,128)S(1)} %get-tuple-element.39), channel_id=1, source_target_pairs={{0,1},{1,2},{2,3},{3,4},{4,5},{5,6},{6,7},{7,8},{8,9},{9,10},{10,1... | collective-permute-start | bytes 1572872 | tf_op jit(solution)/shard_map/ppermute | solution.py:416
  7.4 1.3 collective-permute-start.3
  10.5 1.6 collective-permute-done.from_left_ref
  12.8 2.2 %copy-done.15 = bf16[2,1,1024,1024]{3,2,1,0:T(8,128)(2,1)S(1)} copy-done((bf16[2,1,1024,1024]{3,2,1,0:T(8,128)(2,1)S(1)}, bf16[2,1,1024,1024]{3,2,1,0:T(8,128)(2,1)}, u32[]{:S(2)}) %copy-start.15) | copy-done | bytes 4194328
  15.0 1.6 shard_map.93
  16.7 6.4 %collective-permute-done.3.from_down_ref.r_down_ref = f32[256,256]{1,0:T(8,128)S(1)} collective-permute-done((f32[256,256]{1,0:T(8,128)S(1)}, f32[256,256]{1,0:T(8,128)S(1)}, u32[]{:S(2)}, u32[]{:S(2)}) %collective-permute-start.3) | collective-permute-done | bytes 262176 | tf_op jit(solution)/shard_map/ppermute | solution.py:416
  23.1 2.1 %shard_map.97 = (f32[2,256,256]{2,1,0:T(8,128)}, f32[2,256,256]{2,1,0:T(8,128)}, f32[256,256]{1,0:T(8,128)S(1)}, f32[256,256]{1,0:T(8,128)}, f32[256,256]{1,0:T(8,128)S(1)}) custom-call(bf16[2,1024,1024]{2,1,0:T(8,128)(2,1)S(1)} %get-tuple-element.38.s_ref, f32[2,512,256]{2,1,0:T(8,128)S(1)} %bitcast.22, ...), custom_call_target="tpu_custom_call" | custom-call | flops 1073741824 | bytes 7864320 | tf_op jit(solution)/shard_map/pallas_call | solution.py:44
  25.1 2.0 %copy-done.5 = bf16[2,1024,1024]{2,1,0:T(8,128)(2,1)} copy-done((bf16[2,1024,1024]{2,1,0:T(8,128)(2,1)}, bf16[2,1024,1024]{2,1,0:T(8,128)(2,1)S(1)}, u32[]{:S(2)}) %copy-start.5) | copy-done | bytes 4194328
  30.1 19.5 %all-gather = f32[256,256]{1,0:T(8,128)S(1)} all-gather(f32[16,256]{1,0:T(8,128)S(1)} %shard_map.95), channel_id=2, replica_groups=mesh['y'=4,'xl'=2,'xh'=2,'z'=8,'c'=2] {'z','c'}, dimensions={0}, use_global_device_ids=true | all-gather | bytes 278528 | tf_op jit(solution)/shard_map/all_gather | solution.py:457
  49.6 3.6 %collective-permute-start.6 = (f32[256,256]{1,0:T(8,128)}, f32[256,256]{1,0:T(8,128)}, u32[]{:S(2)}, u32[]{:S(2)}) collective-permute-start(f32[256,256]{1,0:T(8,128)} %get-tuple-element.44.d_ref), channel_id=1, source_target_pairs={{0,224},{32,0},{64,32},{96,64},{128,96},{160,128},{192,160},{224,1... | collective-permute-start | bytes 786440 | tf_op jit(solution)/shard_map/ppermute | solution.py:416
  53.3 2.2 %shard_map.94.block_ref = f32[256,256]{1,0:T(8,128)S(1)} custom-call(s32[3]{0:T(128)S(1)} %pad_add_fusion.place_ref, s32[1,512]{1,0:T(1,128)S(1)} %bitcast.35, f32[512,512]{1,0:T(8,128)S(1)} %copy-done.8), custom_call_target="tpu_custom_call" | custom-call | bytes 1312780 | tf_op jit(solution)/shard_map/pallas_call | solution.py:44
  56.5 3.7 %all-to-all-start = ((f32[16,16,256]{2,1,0:T(8,128)}), f32[16,16,256]{2,1,0:T(8,128)S(1)}, u32[]{:S(2)}, u32[]{:S(2)}) async-start(f32[16,16,256]{2,1,0:T(8,128)} %shard_map.96), calls=%async_computation | async-start | bytes 524288 | tf_op jit(solution)/shard_map/all_to_all | solution.py:459
  60.3 2.2 %copy-done.7 = bf16[2,1,1024,1024]{3,2,1,0:T(8,128)(2,1)S(1)} copy-done((bf16[2,1,1024,1024]{3,2,1,0:T(8,128)(2,1)S(1)}, bf16[2,1,1024,1024]{3,2,1,0:T(8,128)(2,1)}, u32[]{:S(2)}) %copy-start.7) | copy-done | bytes 4194328
  62.5 1.4 shard_map.91.s_ref
  63.9 2.0 %copy-done = bf16[2,1024,1024]{2,1,0:T(8,128)(2,1)} copy-done((bf16[2,1024,1024]{2,1,0:T(8,128)(2,1)}, bf16[2,1024,1024]{2,1,0:T(8,128)(2,1)S(1)}, u32[]{:S(2)}) %copy-start) | copy-done | bytes 4194328
  65.9 2.0 %all-to-all-done.values_ref = f32[16,16,256]{2,1,0:T(8,128)S(1)} async-done(((f32[16,16,256]{2,1,0:T(8,128)}), f32[16,16,256]{2,1,0:T(8,128)S(1)}, u32[]{:S(2)}, u32[]{:S(2)}) %all-to-all-start) | async-done | bytes 262176 | tf_op jit(solution)/shard_map/all_to_all | solution.py:459
  67.9 2.2 %copy-done.1 = bf16[2,1024,1024]{2,1,0:T(8,128)(2,1)S(1)} copy-done((bf16[2,1024,1024]{2,1,0:T(8,128)(2,1)S(1)}, bf16[2,1024,1024]{2,1,0:T(8,128)(2,1)}, u32[]{:S(2)}) %copy-start.1) | copy-done | bytes 4194328
  70.1 6.4 %shard_map.98 = (f32[7,256,256]{2,1,0:T(8,128)S(1)}, f32[2,256,256]{2,1,0:T(8,128)S(1)}, f32[2,256,256]{2,1,0:T(8,128)S(1)}, f32[256,256]{1,0:T(8,128)S(1)}, f32...) custom-call(bf16[2,1024,1024]{2,1,0:T(8,128)(2,1)S(1)} %copy-done.1, ...), custom_call_target="tpu_custom_call" | custom-call | flops 1073741824 | bytes 12730368 | tf_op jit(solution)/shard_map/pallas_call | solution.py:44
  76.5 1.6 collective-permute-start.9
  78.4 3.5 %collective-permute-start.10 = (f32[256,256]{1,0:T(8,128)S(1)}, f32[256,256]{1,0:T(8,128)S(1)}, u32[]{:S(2)}, u32[]{:S(2)}) collective-permute-start(f32[256,256]{1,0:T(8,128)S(1)} %get-tuple-element.52.d_ref), channel_id=1, source_target_pairs={{0,224},{32,0},{64,32},{96,64},{128,96},{160,128},{192,160},{224,1... | collective-permute-start | bytes 786440 | tf_op jit(solution)/shard_map/ppermute | solution.py:416
  81.9 15.9 %all-gather.1 = f32[256,256]{1,0:T(8,128)S(1)} all-gather(f32[16,256]{1,0:T(8,128)S(1)} %get-tuple-element.47), channel_id=3, replica_groups=mesh['y'=4,'xl'=2,'xh'=2,'z'=8,'c'=2] {'z','c'}, dimensions={0}, use_global_device_ids=true | all-gather | bytes 278528 | tf_op jit(solution)/shard_map/all_gather | solution.py:457
  98.2 11.4 %all_to_all.15.values_ref = f32[16,16,256]{2,1,0:T(8,128)S(1)} all-to-all(f32[16,16,256]{2,1,0:T(8,128)S(1)} %shard_map.99), channel_id=1, replica_groups=mesh['y'=4,'xl'=2,'xh'=2,'z'=8,'c'=2] {'y','xl','xh'}, dimensions={0} | all-to-all | bytes 524288 | tf_op jit(solution)/shard_map/all_to_all | solution.py:459
  109.6 2.2 %copy-done.6 = bf16[2,1024,1024]{2,1,0:T(8,128)(2,1)S(1)} copy-done((bf16[2,1024,1024]{2,1,0:T(8,128)(2,1)S(1)}, bf16[2,1024,1024]{2,1,0:T(8,128)(2,1)}, u32[]{:S(2)}) %copy-start.6) | copy-done | bytes 4194328
  111.8 1.3 shard_map.100
  113.2 2.0 %collective-permute-start.13 = (f32[2,256,256]{2,1,0:T(8,128)S(1)}, f32[2,256,256]{2,1,0:T(8,128)S(1)}, u32[]{:S(2)}, u32[]{:S(2)}) collective-permute-start(f32[2,256,256]{2,1,0:T(8,128)S(1)} %get-tuple-element.57.l_ref), channel_id=1, source_target_pairs={{0,31},{1,0},{2,1},{3,2},{4,3},{5,4},{6,5},{7,6},{8,7},{9,8},{10,9... | collective-permute-start | bytes 1572872 | tf_op jit(solution)/shard_map/ppermute | solution.py:416
  116.2 3.3 %collective-permute-start.14 = (f32[256,256]{1,0:T(8,128)S(1)}, f32[256,256]{1,0:T(8,128)S(1)}, u32[]{:S(2)}, u32[]{:S(2)}) collective-permute-start(f32[256,256]{1,0:T(8,128)S(1)} %get-tuple-element.60.d_ref), channel_id=1, source_target_pairs={{0,224},{32,0},{64,32},{96,64},{128,96},{160,128},{192,160},{224,1... | collective-permute-start | bytes 786440 | tf_op jit(solution)/shard_map/ppermute | solution.py:416
  119.5 12.1 %collective-permute-done.15.fd_ref = f32[256,256]{1,0:T(8,128)S(1)} collective-permute-done((f32[256,256]{1,0:T(8,128)S(1)}, f32[256,256]{1,0:T(8,128)S(1)}, u32[]{:S(2)}, u32[]{:S(2)}) %collective-permute-start.15) | collective-permute-done | bytes 262176 | tf_op jit(solution)/shard_map/ppermute | solution.py:416
  131.6 3.6 %collective-permute-done.14.fu_ref = f32[256,256]{1,0:T(8,128)S(1)} collective-permute-done((f32[256,256]{1,0:T(8,128)S(1)}, f32[256,256]{1,0:T(8,128)S(1)}, u32[]{:S(2)}, u32[]{:S(2)}) %collective-permute-start.14) | collective-permute-done | bytes 262176 | tf_op jit(solution)/shard_map/ppermute | solution.py:416
  135.2 3.5 %shard_map.101 = (f32[4,256,256]{2,1,0:T(8,128)S(1)}, f32[8,256]{1,0:T(8,128)S(1)}) custom-call(bf16[2,1024,1024]{2,1,0:T(8,128)(2,1)S(1)} %copy-done.2, f32[7,16,256]{2,1,0:T(8,128)S(1)} %get-tuple-element.37.basis_ref, f32[16,256]{1,0:T(8,128)S(1)} %get-tuple-element.54.corners_ref, f32[7,256,256]{2,1,0:T(8,128)S(1)} %get-tuple-element.46.z0_ref, ...), custom_call_target="tpu_custom_call" | custom-call | flops 1073741824 | bytes 12722176 | tf_op jit(solution)/shard_map/pallas_call | solution.py:44
  138.7 15.7 %all-gather.2 = f32[128,256]{1,0:T(8,128)S(1)} all-gather(f32[8,256]{1,0:T(8,128)S(1)} %get-tuple-element.64), channel_id=4, replica_groups=mesh['y'=4,'xl'=2,'xh'=2,'z'=8,'c'=2] {'z','c'}, dimensions={0}, use_global_device_ids=true | all-gather | bytes 139264 | tf_op jit(solution)/shard_map/all_gather | solution.py:492
  154.5 11.2 %all_to_all.16.sums_ref = f32[16,8,256]{2,1,0:T(8,128)S(1)} all-to-all(f32[16,8,256]{2,1,0:T(8,128)S(1)} %shard_map.102), channel_id=1, replica_groups=mesh['y'=4,'xl'=2,'xh'=2,'z'=8,'c'=2] {'y','xl','xh'}, dimensions={0} | all-to-all | bytes 262144 | tf_op jit(solution)/shard_map/all_to_all | solution.py:494
  (55 shorter events, 12.7 us)
Async XLA Ops:
  0.7 1.2 copy-start.3
  1.9 0.7 copy-start.11
  2.7 20.4 %copy-start.4 = (f32[2,1,512,256]{3,2,1,0:T(8,128)S(1)}, f32[2,1,512,256]{3,2,1,0:T(8,128)}, u32[]{:S(2)}) copy-start(f32[2,1,512,256]{3,2,1,0:T(8,128)} %param.9) | copy-start | bytes 3145732
  2.7 20.4 %collective-permute-start.2 = (f32[2,256,256]{2,1,0:T(8,128)S(1)}, f32[2,256,256]{2,1,0:T(8,128)S(1)}, u32[]{:S(2)}, u32[]{:S(2)}) collective-permute-start(f32[2,256,256]{2,1,0:T(8,128)S(1)} %get-tuple-element.39), channel_id=1, source_target_pairs={{0,1},{1,2},{2,3},{3,4},{4,5},{5,6},{6,7},{7,8},{8,9},{9,10},{10,1... | collective-permute-start | bytes 1572872 | tf_op jit(solution)/shard_map/ppermute | solution.py:416
  5.8 4.7 %collective-permute-start.1 = (f32[8,256]{1,0:T(8,128)S(1)}, f32[8,256]{1,0:T(8,128)S(1)}, u32[]{:S(2)}, u32[]{:S(2)}) collective-permute-start(f32[8,256]{1,0:T(8,128)S(1)} %get-tuple-element.36), channel_id=1, source_target_pairs={{0,32},{32,64},{64,96},{96,128},{128,160},{160,192},{192,224},{224... | collective-permute-start | bytes 24584 | tf_op jit(solution)/shard_map/ppermute | solution.py:416
  7.0 5.1 %collective-permute-start = (f32[2,8,256]{2,1,0:T(8,128)S(1)}, f32[2,8,256]{2,1,0:T(8,128)S(1)}, u32[]{:S(2)}, u32[]{:S(2)}) collective-permute-start(f32[2,8,256]{2,1,0:T(8,128)S(1)} %get-tuple-element.35), channel_id=1, source_target_pairs={{0,1},{1,2},{2,3},{3,4},{4,5},{5,6},{6,7},{7,8},{8,9},{9,10},{10,1... | collective-permute-start | bytes 49160 | tf_op jit(solution)/shard_map/ppermute | solution.py:416
  7.4 15.7 %collective-permute-start.3 = (f32[256,256]{1,0:T(8,128)S(1)}, f32[256,256]{1,0:T(8,128)S(1)}, u32[]{:S(2)}, u32[]{:S(2)}) collective-permute-start(f32[256,256]{1,0:T(8,128)S(1)} %get-tuple-element.40), channel_id=1, source_target_pairs={{0,32},{32,64},{64,96},{96,128},{128,160},{160,192},{192,224},{224... | collective-permute-start | bytes 786440 | tf_op jit(solution)/shard_map/ppermute | solution.py:416
  12.1 0.7 copy-start.12
  12.8 2.2 %copy-start.15 = (bf16[2,1,1024,1024]{3,2,1,0:T(8,128)(2,1)S(1)}, bf16[2,1,1024,1024]{3,2,1,0:T(8,128)(2,1)}, u32[]{:S(2)}) copy-start(bf16[2,1,1024,1024]{3,2,1,0:T(8,128)(2,1)} %param.11) | copy-start | bytes 12582916
  16.7 12.9 %copy-start.13 = (f32[2,1,4,512]{3,2,1,0:T(4,128)S(1)}, f32[2,1,4,512]{3,2,1,0:T(4,128)}, u32[]{:S(2)}) copy-start(f32[2,1,4,512]{3,2,1,0:T(4,128)} %param.12) | copy-start | bytes 49156
  16.7 36.6 %copy-start.8 = (f32[512,512]{1,0:T(8,128)S(1)}, f32[512,512]{1,0:T(8,128)}, u32[]{:S(2)}) copy-start(f32[512,512]{1,0:T(8,128)} %inverse_ref.1) | copy-start | bytes 3145732
  16.7 36.6 %copy-start.14 = (s32[512]{0:T(512)S(1)}, s32[512]{0:T(512)}, u32[]{:S(2)}) copy-start(s32[512]{0:T(512)} %param.16) | copy-start | bytes 6148
  25.1 2.0 %copy-start.5 = (bf16[2,1024,1024]{2,1,0:T(8,128)(2,1)}, bf16[2,1024,1024]{2,1,0:T(8,128)(2,1)S(1)}, u32[]{:S(2)}) copy-start(bf16[2,1024,1024]{2,1,0:T(8,128)(2,1)S(1)} %get-tuple-element.38.s_ref) | copy-start | bytes 12582916
  27.8 40.1 %collective-permute-start.5 = (f32[2,256,256]{2,1,0:T(8,128)}, f32[2,256,256]{2,1,0:T(8,128)}, u32[]{:S(2)}, u32[]{:S(2)}) collective-permute-start(f32[2,256,256]{2,1,0:T(8,128)} %get-tuple-element.41.l_ref), channel_id=1, source_target_pairs={{0,31},{1,0},{2,1},{3,2},{4,3},{5,4},{6,5},{7,6},{8,7},{9,8},{10,9... | collective-permute-start | bytes 1572872 | tf_op jit(solution)/shard_map/ppermute | solution.py:416
  28.8 39.1 %collective-permute-start.4 = (f32[2,256,256]{2,1,0:T(8,128)}, f32[2,256,256]{2,1,0:T(8,128)}, u32[]{:S(2)}, u32[]{:S(2)}) collective-permute-start(f32[2,256,256]{2,1,0:T(8,128)} %get-tuple-element.42.r2_ref), channel_id=1, source_target_pairs={{0,1},{1,2},{2,3},{3,4},{4,5},{5,6},{6,7},{7,8},{8,9},{9,10},{10,1... | collective-permute-start | bytes 1572872 | tf_op jit(solution)/shard_map/ppermute | solution.py:416
  49.6 18.3 %collective-permute-start.7 = (f32[256,256]{1,0:T(8,128)S(1)}, f32[256,256]{1,0:T(8,128)}, u32[]{:S(2)}, u32[]{:S(2)}) collective-permute-start(f32[256,256]{1,0:T(8,128)S(1)} %get-tuple-element.43.u_ref), channel_id=1, source_target_pairs={{0,32},{32,64},{64,96},{96,128},{128,160},{160,192},{192,224},{224... | collective-permute-start | bytes 786440 | tf_op jit(solution)/shard_map/ppermute | solution.py:416
  49.6 18.3 %collective-permute-start.6 = (f32[256,256]{1,0:T(8,128)}, f32[256,256]{1,0:T(8,128)}, u32[]{:S(2)}, u32[]{:S(2)}) collective-permute-start(f32[256,256]{1,0:T(8,128)} %get-tuple-element.44.d_ref), channel_id=1, source_target_pairs={{0,224},{32,0},{64,32},{96,64},{128,96},{160,128},{192,160},{224,1... | collective-permute-start | bytes 786440 | tf_op jit(solution)/shard_map/ppermute | solution.py:416
  56.5 11.4 %all-to-all-start = ((f32[16,16,256]{2,1,0:T(8,128)}), f32[16,16,256]{2,1,0:T(8,128)S(1)}, u32[]{:S(2)}, u32[]{:S(2)}) async-start(f32[16,16,256]{2,1,0:T(8,128)} %shard_map.96), calls=%async_computation | async-start | bytes 524288 | tf_op jit(solution)/shard_map/all_to_all | solution.py:459
  60.3 2.2 %copy-start.7 = (bf16[2,1,1024,1024]{3,2,1,0:T(8,128)(2,1)S(1)}, bf16[2,1,1024,1024]{3,2,1,0:T(8,128)(2,1)}, u32[]{:S(2)}) copy-start(bf16[2,1,1024,1024]{3,2,1,0:T(8,128)(2,1)} %param.10) | copy-start | bytes 12582916
  62.5 5.5 %copy-start.10 = (f32[256,256]{1,0:T(8,128)S(1)}, f32[256,256]{1,0:T(8,128)}, u32[]{:S(2)}) copy-start(f32[256,256]{1,0:T(8,128)} %copy-done.9) | copy-start | bytes 786436
  63.9 2.0 %copy-start = (bf16[2,1024,1024]{2,1,0:T(8,128)(2,1)}, bf16[2,1024,1024]{2,1,0:T(8,128)(2,1)S(1)}, u32[]{:S(2)}) copy-start(bf16[2,1024,1024]{2,1,0:T(8,128)(2,1)S(1)} %shard_map.91.s_ref) | copy-start | bytes 12582916
  67.9 2.2 %copy-start.1 = (bf16[2,1024,1024]{2,1,0:T(8,128)(2,1)S(1)}, bf16[2,1024,1024]{2,1,0:T(8,128)(2,1)}, u32[]{:S(2)}) copy-start(bf16[2,1024,1024]{2,1,0:T(8,128)(2,1)} %copy-done) | copy-start | bytes 12582916
  76.5 33.1 %collective-permute-start.9 = (f32[2,256,256]{2,1,0:T(8,128)S(1)}, f32[2,256,256]{2,1,0:T(8,128)S(1)}, u32[]{:S(2)}, u32[]{:S(2)}) collective-permute-start(f32[2,256,256]{2,1,0:T(8,128)S(1)} %get-tuple-element.49.l_ref), channel_id=1, source_target_pairs={{0,31},{1,0},{2,1},{3,2},{4,3},{5,4},{6,5},{7,6},{8,7},{9,8},{10,9... | collective-permute-start | bytes 1572872 | tf_op jit(solution)/shard_map/ppermute | solution.py:416
  78.1 31.5 %collective-permute-start.8 = (f32[2,256,256]{2,1,0:T(8,128)S(1)}, f32[2,256,256]{2,1,0:T(8,128)S(1)}, u32[]{:S(2)}, u32[]{:S(2)}) collective-permute-start(f32[2,256,256]{2,1,0:T(8,128)S(1)} %get-tuple-element.50.r2_ref), channel_id=1, source_target_pairs={{0,1},{1,2},{2,3},{3,4},{4,5},{5,6},{6,7},{7,8},{8,9},{9,10},{10,1... | collective-permute-start | bytes 1572872 | tf_op jit(solution)/shard_map/ppermute | solution.py:416
  78.3 31.3 %collective-permute-start.11 = (f32[256,256]{1,0:T(8,128)S(1)}, f32[256,256]{1,0:T(8,128)S(1)}, u32[]{:S(2)}, u32[]{:S(2)}) collective-permute-start(f32[256,256]{1,0:T(8,128)S(1)} %get-tuple-element.51.u_ref), channel_id=1, source_target_pairs={{0,32},{32,64},{64,96},{96,128},{128,160},{160,192},{192,224},{224... | collective-permute-start | bytes 786440 | tf_op jit(solution)/shard_map/ppermute | solution.py:416
  78.4 31.2 %collective-permute-start.10 = (f32[256,256]{1,0:T(8,128)S(1)}, f32[256,256]{1,0:T(8,128)S(1)}, u32[]{:S(2)}, u32[]{:S(2)}) collective-permute-start(f32[256,256]{1,0:T(8,128)S(1)} %get-tuple-element.52.d_ref), channel_id=1, source_target_pairs={{0,224},{32,0},{64,32},{96,64},{128,96},{160,128},{192,160},{224,1... | collective-permute-start | bytes 786440 | tf_op jit(solution)/shard_map/ppermute | solution.py:416
  109.6 2.2 %copy-start.6 = (bf16[2,1024,1024]{2,1,0:T(8,128)(2,1)S(1)}, bf16[2,1024,1024]{2,1,0:T(8,128)(2,1)}, u32[]{:S(2)}) copy-start(bf16[2,1024,1024]{2,1,0:T(8,128)(2,1)} %copy-done.5) | copy-start | bytes 12582916
  111.8 23.4 %copy-start.2 = (bf16[2,1024,1024]{2,1,0:T(8,128)(2,1)S(1)}, bf16[2,1024,1024]{2,1,0:T(8,128)(2,1)}, u32[]{:S(2)}) copy-start(bf16[2,1024,1024]{2,1,0:T(8,128)(2,1)} %copy-done) | copy-start | bytes 12582916
  113.2 22.1 %collective-permute-start.13 = (f32[2,256,256]{2,1,0:T(8,128)S(1)}, f32[2,256,256]{2,1,0:T(8,128)S(1)}, u32[]{:S(2)}, u32[]{:S(2)}) collective-permute-start(f32[2,256,256]{2,1,0:T(8,128)S(1)} %get-tuple-element.57.l_ref), channel_id=1, source_target_pairs={{0,31},{1,0},{2,1},{3,2},{4,3},{5,4},{6,5},{7,6},{8,7},{9,8},{10,9... | collective-permute-start | bytes 1572872 | tf_op jit(solution)/shard_map/ppermute | solution.py:416
  115.2 20.0 %collective-permute-start.12 = (f32[2,256,256]{2,1,0:T(8,128)S(1)}, f32[2,256,256]{2,1,0:T(8,128)S(1)}, u32[]{:S(2)}, u32[]{:S(2)}) collective-permute-start(f32[2,256,256]{2,1,0:T(8,128)S(1)} %get-tuple-element.58.r2_ref), channel_id=1, source_target_pairs={{0,1},{1,2},{2,3},{3,4},{4,5},{5,6},{6,7},{7,8},{8,9},{9,10},{10,1... | collective-permute-start | bytes 1572872 | tf_op jit(solution)/shard_map/ppermute | solution.py:416
  115.9 15.7 %collective-permute-start.15 = (f32[256,256]{1,0:T(8,128)S(1)}, f32[256,256]{1,0:T(8,128)S(1)}, u32[]{:S(2)}, u32[]{:S(2)}) collective-permute-start(f32[256,256]{1,0:T(8,128)S(1)} %get-tuple-element.59.u_ref), channel_id=1, source_target_pairs={{0,32},{32,64},{64,96},{96,128},{128,160},{160,192},{192,224},{224... | collective-permute-start | bytes 786440 | tf_op jit(solution)/shard_map/ppermute | solution.py:416
  116.2 19.0 %collective-permute-start.14 = (f32[256,256]{1,0:T(8,128)S(1)}, f32[256,256]{1,0:T(8,128)S(1)}, u32[]{:S(2)}, u32[]{:S(2)}) collective-permute-start(f32[256,256]{1,0:T(8,128)S(1)} %get-tuple-element.60.d_ref), channel_id=1, source_target_pairs={{0,224},{32,0},{64,32},{96,64},{128,96},{160,128},{192,160},{224,1... | collective-permute-start | bytes 786440 | tf_op jit(solution)/shard_map/ppermute | solution.py:416
  (1 other events, 0.7 us)

commit v2 on v0

v2 whole, which is shorter than its diff:
```python
import jax
import jax.numpy as jnp
import numpy as np
from jax import lax
from jax.experimental import pallas as pl
from jax.experimental.pallas import tpu as pltpu
from jax.sharding import Mesh
from jax.sharding import PartitionSpec as P

SPLIT = {"y": 4, "xl": 2, "xh": 2, "z": 8, "c": 2}
BLK = ("y", "xl")
CROSS = ("xh", "z", "c")
NEAR = ("z", "c")
FAR = ("y", "xl", "xh")
F = 256
R = 256
CORNERS = 512
EXACT = lax.Precision.HIGHEST
F32 = jnp.float32
BF16 = jnp.bfloat16

FACES = 7
PACK = F + 8
WEIGHT = F + 4
SIDES = ((4, 0, 6, 2), (5, 1, 2, 3))
OWNER = ((0, 0), (1, 0), (0, 0), (1, 0), (0, -1), (1, -1), (-1, 0))


def slot(axial, sector):
    return (axial + 1) * 3 + sector + 1


SLOTS = 16


def face_slots(face):
    axial, sector = OWNER[face]
    return [slot(axial + da, sector + ds) for da in (0, 1) for ds in (0, 1)]


class Fetched:
    def __init__(self, source, held, sems, pieces):
        self.held = held
        self.copies = {
            str(piece): pltpu.make_async_copy(source.at[piece], held.at[piece], sem)
            for piece, sem in zip(pieces, sems)
        }
        self.waited = set()

    def start(self):
        for copy in self.copies.values():
            copy.start()

    def get(self, piece=()):
        if str(piece) not in self.waited:
            self.waited.add(str(piece))
            self.copies[str(piece)].wait()
        return self.held.at[piece] if piece else self.held

    def finish(self):
        for piece, copy in self.copies.items():
            if piece not in self.waited:
                copy.wait()


class Stored:
    def __init__(self, held, target, sems, pieces):
        self.held = held
        self.copies = {
            str(piece): pltpu.make_async_copy(held.at[piece], target.at[piece], sem)
            for piece, sem in zip(pieces, sems)
        }

    def put(self, value, piece=()):
        self.held[piece if piece else ...] = value
        self.copies[str(piece)].start()

    def send(self, piece=()):
        self.copies[str(piece)].start()

    def finish(self):
        for copy in self.copies.values():
            copy.wait()


BLOCK_PIECES = [(k, slice(side * F, (side + 1) * F)) for k in range(2) for side in range(4)]


HALF_PIECES = [(k, slice(side * F, (side + 1) * F)) for k in range(2) for side in range(2)]


def pieces_of(shape):
    if shape == (2, 4 * F, 4 * F):
        return BLOCK_PIECES
    if shape == (2, 2 * F, R):
        return HALF_PIECES
    if len(shape) == 3 and shape[1:] in ((F, R), (PACK, R)):
        return [(k,) for k in range(shape[0])]
    return [()]


def block_piece(k, side):
    return BLOCK_PIECES[k * 4 + side]


class Here:
    def __init__(self, held):
        self.held = held

    def start(self):
        pass

    def get(self, piece=()):
        return self.held.at[piece] if piece else self.held

    def put(self, value, piece=()):
        self.held[piece if piece else ...] = value

    def send(self, piece=()):
        pass

    def finish(self):
        pass


def call(kernel, outs, *args, flops=0, smem=(), near=(), near_out=(), parts=None, scratch=()):
    size = sum(int(np.prod(a.shape)) * a.dtype.itemsize for a in args)
    size += sum(int(np.prod(s)) * jnp.dtype(d).itemsize for s, d in outs)
    inputs = [i for i in range(len(args)) if i not in smem]
    shapes = [(args[i].shape, args[i].dtype) for i in inputs] + list(outs)
    here = [i in near for i in inputs] + [i in near_out for i in range(len(outs))]
    pieces = [[] if there else pieces_of(shape) for (shape, _), there in zip(shapes, here)]
    for i, count in (parts or {}).items():
        pieces[i] = pieces[i][:count]
    staged = [shape for shape, there in zip(shapes, here) if not there]

    def body(*refs):
        operands, results = refs[: len(args)], refs[len(args) : len(args) + len(outs)]
        rest = list(refs[len(args) + len(outs) :])
        held, sems, rest = rest[: len(staged)], rest[len(staged)], rest[len(staged) + 1 :]
        made, at = [], 0
        for i, (ref, there) in enumerate(zip([operands[i] for i in inputs] + list(results), here)):
            if there:
                made.append(Here(ref))
                continue
            own = [sems.at[at + j] for j in range(len(pieces[i]))]
            at += len(own)
            vmem = held.pop(0)
            fetch = i < len(inputs)
            made.append(Fetched(ref, vmem, own, pieces[i]) if fetch else Stored(vmem, ref, own, pieces[i]))
        for operand in made[: len(inputs)]:
            operand.start()
        kernel(*[operands[i] for i in smem], *made, *rest)
        for array in made:
            array.finish()

    args = [a if i in smem or i in near else pltpu.with_memory_space_constraint(a, pltpu.HBM) for i, a in enumerate(args)]

    def space(there):
        return pl.BlockSpec(memory_space=pltpu.VMEM if there else pltpu.HBM)

    return pl.pallas_call(
        body,
        out_shape=[
            jax.ShapeDtypeStruct(s, d) if i in near_out else pltpu.HBM(s, d) for i, (s, d) in enumerate(outs)
        ],
        in_specs=[pl.BlockSpec(memory_space=pltpu.SMEM) if i in smem else space(i in near) for i in range(len(args))],
        out_specs=[space(i in near_out) for i in range(len(outs))],
        scratch_shapes=[pltpu.VMEM(s, d) for s, d in staged]
        + [pltpu.SemaphoreType.DMA((max(1, sum(len(p) for p in pieces)),)), *scratch],
        compiler_params=pltpu.CompilerParams(vmem_limit_bytes=32 * 1024 * 1024),
        cost_estimate=pl.CostEstimate(flops=flops, bytes_accessed=size, transcendentals=0),
    )(*args)


def thirds(value):
    high = value.astype(BF16)
    rest = value - high.astype(F32)
    middle = rest.astype(BF16)
    return high, middle, (rest - middle.astype(F32)).astype(BF16)


def nt(left, right):
    return lax.dot_general(left, right, (((1,), (1,)), ((), ())), preferred_element_type=F32)


def nn(left, right):
    return lax.dot_general(left, right, (((1,), (0,)), ((), ())), preferred_element_type=F32)


def weights_of(occ_ref, k):
    return 1.0 / (1.0 + occ_ref[k].astype(F32))


def pack_kernel(r, occ, basis, right, up):
    basis_ref, occ_ref = basis.get(), occ.get()

    def tail(k, part):
        spare = jnp.zeros((3, R), F32)
        return jnp.concatenate([basis_ref[k, :, part], weights_of(occ_ref, k)[:, part], spare], axis=0)

    first, last = slice(0, F), slice(F, 2 * F)
    right.held[0, F:, :] = tail(0, first)
    right.held[1, F:, :] = tail(1, first)
    up.held[F:, :] = tail(1, last)
    for k in range(2):
        right.held[k, :F, :] = own_face(r, k)
        right.send((k,))
    up.held[:F, :] = own_face(r, 3)
    up.send()


def loads_kernel(r, basis, out):
    basis_ref = basis.get()
    for piece in HALF_PIECES:
        r.get(piece)
    first = jnp.dot(basis_ref[0], r.held[0], precision=EXACT, preferred_element_type=F32)
    second = jnp.dot(basis_ref[1], r.held[1], precision=EXACT, preferred_element_type=F32)
    for peer in range(16):
        out.held[peer, 0:2, :] = first[0:2]
        out.held[peer, 2:4, :] = first[2:4] + second[0:2]
        out.held[peer, 4:6, :] = second[2:4]
        out.held[peer, 6:8, :] = jnp.zeros((2, R), F32)
    out.send()


def scale_column(row):
    eye = lax.broadcasted_iota(jnp.int32, (F, F), 1) == lax.broadcasted_iota(jnp.int32, (F, F), 0)
    return jnp.sum(jnp.where(eye, row, 0.0), axis=1, keepdims=True)


def placed(order_row):
    rows = lax.broadcasted_iota(jnp.int32, (F, F), 0)
    return jnp.where(order_row == rows, -1.0, 0.0).astype(BF16)


def reorder_block(s, out, work_ref, k, orders, weights):
    for row in range(4):
        rows = s.get(block_piece(k, row))
        for side in range(4):
            part = rows[:, side * F : (side + 1) * F]
            if orders[side] is not None:
                part = nt(part, orders[side])
            if weights[side] is not None:
                part = part.astype(F32) * weights[side]
            work_ref[:, side * F : (side + 1) * F] = part.astype(BF16)
        part = work_ref[...]
        if orders[row] is not None:
            part = nn(orders[row], part)
        if weights[row] is not None:
            part = part.astype(F32) * scale_column(weights[row])
        out.put(part.astype(BF16), block_piece(k, row))


def reorder_plain_kernel(s, left, down, out, work_ref):
    left_ref, down_ref = left.get(), down.get()
    for k in range(2):
        orders = (placed(left_ref[k]), None, placed(down_ref[k]), None)
        reorder_block(s, out, work_ref, k, orders, (None,) * 4)


def reorder_weighted_kernel(s, left, down, occ, out, work_ref):
    left_ref, down_ref, occ_ref = left.get(), down.get(), occ.get()
    first, second = weights_of(occ_ref, 0), weights_of(occ_ref, 1)
    for k, weight in enumerate((first, second)):
        orders = (placed(left_ref[k]), None, placed(down_ref[k]), None)
        below = None if k == 0 else first[:, F:]
        reorder_block(s, out, work_ref, k, orders, (None, weight[:, :F], below, weight[:, F:]))


def basis_kernel(basis, from_left, from_down, rows, columns, flat_ref):
    basis_ref, from_down_ref = basis.get(), from_down.get()
    sources = (
        basis_ref[0, :, :F],
        basis_ref[1, :, :F],
        basis_ref[0, :, F:],
        basis_ref[1, :, F:],
        from_left.get((0,))[F : F + 4, :],
        from_left.get((1,))[F : F + 4, :],
        from_down_ref[F : F + 4, :],
    )
    for face in range(FACES):
        flat_ref[...] = jnp.zeros_like(flat_ref)
        for k, row in enumerate(face_slots(face)):
            flat_ref[row : row + 1, :] = sources[face][k : k + 1, :]
        high, middle, low = thirds(flat_ref[...])
        rows.held[face, 0:16, :] = high
        rows.held[face, 16:32, :] = middle
        rows.held[face, 32:48, :] = low
        parts = [p.astype(F32) for p in (high, high, high, middle, middle, low)]
        parts.append(jnp.zeros((32, F), F32))
        columns.held[face] = jnp.concatenate(parts, axis=0).T.astype(BF16)
    rows.send()
    columns.send()


def corner_onehot(numbers_t, axial, sector, spare):
    wanted = (axial & 15) * 32 + (sector & 31)
    columns = lax.broadcasted_iota(jnp.int32, (wanted.shape[0], CORNERS), 1)
    picks = jnp.where((columns == wanted) & jnp.logical_not(spare), 1.0, 0.0).astype(BF16)
    return nt(picks, numbers_t).astype(BF16)


def coarse_block_kernel(place_ref, numbers, inverse, first, later):
    blk, xh, near = place_ref[0], place_ref[1], place_ref[2]
    ids = lax.broadcasted_iota(jnp.int32, (CORNERS, CORNERS), 0)
    numbers_t = jnp.where(numbers.get()[...] == ids, 1.0, 0.0).astype(BF16)
    rows = lax.broadcasted_iota(jnp.int32, (16 * SLOTS, 1), 0)
    peer = rows >> 4
    entry = rows & 15
    third = (entry >= 3).astype(jnp.int32) + (entry >= 6).astype(jnp.int32) + (entry >= 9).astype(jnp.int32)
    da = third - 1
    ds = entry - 3 * third - 1
    spare = entry >= 12
    far_rows = corner_onehot(numbers_t, 2 * (peer >> 1) + da, (peer & 1) * 16 + near + ds, spare)
    near_rows = corner_onehot(numbers_t, 2 * blk + da, xh * 16 + peer + ds, spare)
    few = lax.broadcasted_iota(jnp.int32, (16 * 8, 1), 0)
    own = few & 7
    own_rows = corner_onehot(numbers_t, 2 * blk + (own >> 1), xh * 16 + (few >> 3) + (own & 1), own >= 6)
    picked = thirds(sum(nn(far_rows, part) for part in thirds(inverse.get()[...])[::-1]))[::-1]
    first.put(sum(nt(part, own_rows) for part in picked))
    block = sum(nt(part, near_rows) for part in picked)
    columns = lax.broadcasted_iota(jnp.int32, (16 * SLOTS, 16 * SLOTS), 1) & 15
    passed = (columns == entry) & spare
    later.put(jnp.where(passed, 1.0, block))


HALVES = [((2, F, R), F32), ((2, F, R), F32), ((F, R), F32), ((F, R), F32), ((F, R), F32)]


def apply_block(s, operand_ref, left, right, up, down, mid, weights=None):
    def outer(value, which):
        return value if weights is None else value * weights[which]

    for k in range(2):
        sides = [nn(s.get(block_piece(k, side))[...], operand_ref[k]) for side in range(4)]
        left.put(outer(sides[0], k), (k,))
        right.put(sides[1], (k,))
        if k == 0:
            down.put(outer(sides[2], 2))
            shared = sides[3]
        else:
            mid.put(shared + sides[2])
            up.put(sides[3])


def set_operand(operand_ref, face, value):
    value = value.astype(BF16)
    for k in range(2):
        for side in range(4):
            if SIDES[k][side] == face:
                operand_ref[k, side * F : (side + 1) * F, :] = value


def outer_weights(from_left, from_down):
    rows = [from_left.get((k,))[WEIGHT : WEIGHT + 1, :] for k in range(2)]
    rows.append(from_down.get()[WEIGHT : WEIGHT + 1, :])
    return [scale_column(row) for row in rows]


def first_kernel(
    left_order, down_order, occ, s, r, from_left, from_down,
    block, left, right, up, down, mid, operand_ref, strip_ref,
):
    reorder_weighted_kernel(s, left_order, down_order, occ, block, strip_ref)
    weights = outer_weights(from_left, from_down)
    for k in range(2):
        set_operand(operand_ref, k, own_face(r, k))
        set_operand(operand_ref, 2 + k, own_face(r, 2 + k))
        set_operand(operand_ref, 4 + k, from_left.get((k,))[:F, :] * weights[k])
    set_operand(operand_ref, 6, from_down.get()[:F, :] * weights[2])
    apply_block(Here(block.held), operand_ref, left, right, up, down, mid, weights)


PLACES = ((1, (0,)), (1, (1,)), (4, ()), (2, ()), (0, (0,)), (0, (1,)), (3, ()))


def own_share(halves, face):
    which, piece = PLACES[face]
    return halves[which].get(piece)[...]


def own_image(halves, face):
    which, piece = PLACES[face]
    return halves[which].held[piece if piece else ...]


def assembled(halves, others, face):
    which, piece = PLACES[face]
    if which == 4:
        return own_share(halves, face)
    return own_share(halves, face) + others[which].get(piece)[...]


def stacked(values):
    high, middle, low = thirds(values)
    parts = [high, middle, low, high, middle, high, jnp.zeros((32, R), BF16)]
    return jnp.concatenate(parts, axis=0)


def face_loads(rows_ref, face, image):
    out = sum(nn(rows_ref[face], part) for part in thirds(image)[1::-1])
    return out[32:48] + out[16:32] + out[0:16]


def face_piece(face):
    return HALF_PIECES[(face % 2) * 2 + face // 2]


def own_face(r, face):
    return r.get(face_piece(face))[...]


def total(value):
    return jnp.sum(value, axis=0, keepdims=True)


def operate_first_kernel(
    values, columns, l0, r0, u0, d0, m0, fl, fr, fu, fd, r, s, rows,
    z, left, right, up, down, mid, message, corners_out, operand_ref,
):
    corners = jnp.sum(values.get()[...], axis=0)
    corners_out.put(corners)
    terms = stacked(corners)
    columns_ref = columns.get()
    before, others = (l0, r0, u0, d0, m0), (fl, fr, fu, fd)
    images = (left, right, up, down, mid)
    progress = jnp.zeros((1, R), F32)
    for face in range(FACES):
        value = assembled(before, others, face) + nn(columns_ref[face], terms)
        z.put(value, (face,))
        set_operand(operand_ref, face, value)
        if face < 4:
            progress = progress + total(own_face(r, face) * value)
    apply_block(s, operand_ref, *images)
    rows_ref = rows.get()
    loads = jnp.zeros((SLOTS, R), F32)
    curvature = jnp.zeros((1, R), F32)
    for face in range(FACES):
        image = own_image(images, face)
        loads = loads + face_loads(rows_ref, face, image)
        curvature = curvature + total(z.held[face] * image)
    for peer in range(16):
        message.held[peer] = loads
        message.held[peer, 12:13, :] = progress
        message.held[peer, 13:14, :] = curvature
    message.send()


def second_kernel(
    values, corners_before, r_left, r_down, r, l0, r0, u0, d0, m0, fl, fr, fu, fd, s,
    residual, image_out, left, right, up, down, mid, corners_out, scalars, operand_ref,
):
    sums = jnp.sum(values.get()[...], axis=0)
    progress, curvature = sums[12:13, :], sums[13:14, :]
    alpha = progress / curvature
    corners_out.put(corners_before.get()[...] - alpha * sums)
    scalars.held[...] = jnp.zeros((8, R), F32)
    scalars.held[0:1, :] = progress
    scalars.held[1:2, :] = curvature
    scalars.held[2:3, :] = alpha
    scalars.send()
    before, others = (l0, r0, u0, d0, m0), (fl, fr, fu, fd)
    weights = outer_weights(r_left, r_down)
    for face in range(FACES):
        image = assembled(before, others, face)
        if face < 4:
            start = own_face(r, face)
        elif face < 6:
            start = r_left.get((face - 4,))[:F, :]
        else:
            start = r_down.get()[:F, :]
        value = start - alpha * image
        if face < 4:
            image_out.put(image, (face,))
            residual.put(value, (face,))
        else:
            value = value * weights[face - 4]
        set_operand(operand_ref, face, value)
    apply_block(s, operand_ref, left, right, up, down, mid, weights)


def operate_last_kernel(
    corners_in, columns, l0, r0, u0, d0, m0, fl, fr, fu, fd, residual, image_in, s, z0,
    z, message, operand_ref, z_ref,
):
    corners = corners_in.get()[...]
    terms = stacked(jnp.where(lax.broadcasted_iota(jnp.int32, corners.shape, 0) < 12, corners, 0.0))
    columns_ref = columns.get()
    before, others = (l0, r0, u0, d0, m0), (fl, fr, fu, fd)
    progress = jnp.zeros((1, R), F32)
    mixed = jnp.zeros((1, R), F32)
    for face in range(FACES):
        value = assembled(before, others, face) + nn(columns_ref[face], terms)
        z_ref[face] = value
        set_operand(operand_ref, face, value)
        if face < 4:
            z.put(value, (face,))
            progress = progress + total(residual.get((face,))[...] * value)
            mixed = mixed + total(image_in.get((face,))[...] * value)
    curvature = jnp.zeros((1, R), F32)
    for k in range(2):
        for side in range(4):
            image = nn(s.get(block_piece(k, side))[...], operand_ref[k])
            face = SIDES[k][side]
            curvature = curvature + total(z_ref[face] * image)
            mixed = mixed + total(z0.get((face,))[...] * image)
    for peer in range(16):
        message.held[peer, 0:1, :] = progress
        message.held[peer, 1:2, :] = curvature
        message.held[peer, 2:3, :] = mixed
        message.held[peer, 3:4, :] = jnp.zeros((1, R), F32)
    message.send()


def finish_kernel(sums_in, scalars, z0, z1, out):
    sums = jnp.sum(sums_in.get()[...], axis=0)
    progress, curvature, mixed = sums[0:1, :], sums[1:2, :], sums[2:3, :]
    before = scalars.get()[...]
    first_progress, first_curvature, alpha = before[0:1, :], before[1:2, :], before[2:3, :]
    ratio = progress / first_progress
    last = progress / (curvature + ratio * (mixed + ratio * first_curvature))
    scale0 = alpha + last * ratio
    for face in (0, 2, 1, 3):
        out.put(scale0 * z0.get((face,))[...] + last * z1.get((face,))[...], face_piece(face))


def partial_kernel(message, block, out):
    flat = jnp.concatenate([message.get()[i] for i in range(16)], axis=0)
    values = jnp.dot(block.get()[...], flat, precision=EXACT, preferred_element_type=F32)
    for i in range(16):
        out.held[i] = values[i * SLOTS : (i + 1) * SLOTS]
    out.send()


def sum_kernel(near, out):
    sums = jnp.sum(near.get()[...], axis=0)
    for i in range(16):
        out.held[i] = sums
    out.send()


def moved(block, axes, count, distance):
    return lax.ppermute(block, axes, [(i, (i + distance) % count) for i in range(count)])


def exchanged(left, right, up, down):
    return (
        moved(right, CROSS, 32, 1),
        moved(left, CROSS, 32, -1),
        moved(down, BLK, 8, -1),
        moved(up, BLK, 8, 1),
    )


MATMUL_FLOPS = 2 * 2 * (4 * F) * (4 * F) * R


def on_device(r, s_inverse, s, basis, occ, left_order, down_order, numbers, coarse_inverse):
    r, s_inverse, s, basis = r[:, 0], s_inverse[:, 0], s[:, 0], basis[:, 0]
    place = jnp.stack([lax.axis_index(BLK), lax.axis_index("xh"), lax.axis_index(NEAR)]).astype(jnp.int32)
    operand = pltpu.VMEM((2, 4 * F, R), BF16)
    strip = pltpu.VMEM((F, 4 * F), BF16)

    right, up = call(pack_kernel, [((2, PACK, R), F32), ((PACK, R), F32)], r, occ, basis)
    r_left = moved(right, CROSS, 32, 1)
    r_down = moved(up, BLK, 8, 1)
    (loads,) = call(loads_kernel, [((16, 8, R), F32)], r, basis)
    near = lax.all_to_all(loads, NEAR, 0, 0)
    first_block, later_block = call(
        coarse_block_kernel,
        [((16 * SLOTS, 16 * 8), F32), ((16 * SLOTS, 16 * SLOTS), F32)],
        place, numbers[None, :], coarse_inverse,
        smem=(0,),
    )
    (inverse_block,) = call(
        reorder_plain_kernel,
        [(s_inverse.shape, BF16)],
        s_inverse, left_order, down_order,
        flops=2 * MATMUL_FLOPS, scratch=[strip],
    )
    r_left, r_down, first_block, later_block, inverse_block = lax.optimization_barrier(
        (r_left, r_down, first_block, later_block, inverse_block)
    )

    schur_block, *halves = call(
        first_kernel,
        [(s.shape, BF16), *HALVES],
        left_order, down_order, occ, s, r, r_left, r_down,
        flops=3 * MATMUL_FLOPS, near=(5, 6), scratch=[operand, strip],
    )
    near, *halves = lax.optimization_barrier((near, *halves))
    others = exchanged(*halves[:4])
    (partial,) = call(partial_kernel, [((16, SLOTS, R), F32)], near, first_block, near=(0,))
    values = lax.all_to_all(partial, FAR, 0, 0)
    rows, columns = call(
        basis_kernel,
        [((FACES, 48, F), BF16), ((FACES, F, 128), BF16)],
        basis, r_left, r_down,
        scratch=[pltpu.VMEM((SLOTS, F), F32)],
    )
    z0, *halves, message, corners = call(
        operate_first_kernel,
        [((FACES, F, R), F32), *HALVES, ((16, SLOTS, R), F32), ((SLOTS, R), F32)],
        values, columns, *halves, *others, r, inverse_block, rows,
        flops=MATMUL_FLOPS, near=(0, 7, 8, 9, 10), scratch=[operand],
    )
    others = exchanged(*halves[:4])
    near = lax.all_to_all(message, NEAR, 0, 0)
    (partial,) = call(partial_kernel, [((16, SLOTS, R), F32)], near, later_block, near=(0,))
    values = lax.all_to_all(partial, FAR, 0, 0)
    residual, image, *halves, corners, scalars = call(
        second_kernel,
        [((4, F, R), F32), ((4, F, R), F32), *HALVES, ((SLOTS, R), F32), ((8, R), F32)],
        values, corners, r_left, r_down, r, *halves, *others, schur_block,
        flops=MATMUL_FLOPS, near=(0, 10, 11, 12, 13), near_out=(0, 1, 2, 3, 4, 5, 6, 7), scratch=[operand],
    )
    others = exchanged(*halves[:4])
    z1, message = call(
        operate_last_kernel,
        [((4, F, R), F32), ((16, 4, R), F32)],
        corners, columns, *halves, *others, residual, image, inverse_block, z0,
        flops=MATMUL_FLOPS, near=tuple(range(15)), scratch=[operand, pltpu.VMEM((FACES, F, R), F32)],
    )
    near = lax.all_to_all(message, NEAR, 0, 0)
    (spread_sums,) = call(sum_kernel, [((16, 4, R), F32)], near, near=(0,))
    sums = lax.all_to_all(spread_sums, FAR, 0, 0)
    (out,) = call(finish_kernel, [((2, 2 * F, R), F32)], sums, scalars, z0, z1, near=(0,), parts={2: 4})
    return out[:, None]


def solution(mesh):
    split = Mesh(mesh.devices.reshape(tuple(SPLIT.values())), tuple(SPLIT))
    four = P(BLK, CROSS, None, None)
    three = P(BLK, CROSS, None)
    return jax.shard_map(
        on_device,
        mesh=split,
        in_specs=(four, four, four, four, three, three, three, P(), P()),
        out_specs=four,
        check_vma=False,
    )
```

time: 936 us -> 159 us (0.17)
  waiting for transfers between devices: 486 us -> 39.7 us
  blocking collectives: 240 us -> 25.8 us
  local copies, waits for them, and re-layouts: 107 us -> 0.02 us
  Pallas kernels: 0 us -> 46.8 us
  matrix products: 26.7 us -> 0 us
  other arithmetic: 24.8 us -> 0.08 us
  starting transfers between devices: 26 us -> 44.7 us
  between operations: 16.1 us -> 0.4 us
    psum x2 -> x0, waiting for transfers between devices: 433 us -> none  [coarse_values(): corner_sums = lax.psum(partial_sums, ('blk', 'cross'))]
    psum x3 -> x0, blocking collectives: 240 us -> none  [the longest x2 158 us: inner_progress(): return lax.psum(jnp.sum(residual * smoothed, axis=(0, 1)), ('blk', 'cross'))]
    gather x37 -> x0, local copies, waits for them, and re-layouts: 77.5 us -> none  [the longest x32 74.4 us: rows_by(): jnp.take(block, chosen, axis=0)]
    pallas_call x0 -> x13, Pallas kernels: none -> 46.8 us  [call(): pl.pallas_call(body, out_shape=[jax.ShapeDtypeStruct(s, d) if i in near_o...]
    ppermute x16 -> x14, waiting for transfers between devices: 53.3 us -> 16.1 us  [moved(): lax.ppermute(block, axes, [(i, (i + distance) % count) for i in range(cou...]
    dot_general x12 -> x0, matrix products: 26.7 us -> none  [the longest x2 7.3 us: on_device(): jnp.einsum('kmn,knr->kmr', inverse_blocks, spread_field.astype(jnp.bfloat...]
    all_to_all x0 -> x2, blocking collectives: none -> 25.8 us  [the longest x1 13.9 us: on_device(): near = lax.all_to_all(message, NEAR, 0, 0)]
    all_to_all x0 -> x4, starting transfers between devices: none -> 24 us  [the longest x2 8.82 us: on_device(): values = lax.all_to_all(partial, FAR, 0, 0)]
  transfers between devices with their start and end apart: 18 -> 18, of which waited for: 11 -> 6; matrix products, arithmetic and copies ran while one was open for 8% -> 0% of each run, Pallas kernels for 0% -> 16%
where the time goes in v2:
time: 159 us; the launch traced here: 157 us
  Pallas kernels  46.8 us (29%)
  starting transfers between devices  44.7 us (28%)
  waiting for transfers between devices  39.7 us (25%)
  blocking collectives  25.8 us (16%)
    pallas_call x13, Pallas kernels, call(): pl.pallas_call(body, out_shape=[jax.ShapeDtypeStruct(s, d) if i in near_o...  46.8 us
    ppermute x14, starting transfers between devices, moved(): lax.ppermute(block, axes, [(i, (i + distance) % count) for i in range(cou...  20.7 us
    all_to_all x2, waiting for transfers between devices, on_device(): values = lax.all_to_all(partial, FAR, 0, 0)  16.7 us
    ppermute x14, waiting for transfers between devices, moved(): lax.ppermute(block, axes, [(i, (i + distance) % count) for i in range(cou...  16.1 us
    all_to_all x1, blocking collectives, on_device(): near = lax.all_to_all(message, NEAR, 0, 0)  13.9 us
    all_to_all x1, blocking collectives, on_device(): sums = lax.all_to_all(spread_sums, FAR, 0, 0)  12 us
    all_to_all x2, starting transfers between devices, on_device(): values = lax.all_to_all(partial, FAR, 0, 0)  8.82 us
    all_to_all x1, starting transfers between devices, on_device(): near = lax.all_to_all(loads, NEAR, 0, 0)  7.71 us
  transfers between devices with their start and end apart: 18, of which 6 were waited for; matrix products, arithmetic and copies ran while one was open for 0% of the time, Pallas kernels for 16%

profile of v2, /device:TPU:1, one launch (start us, length us, event | category | flops | bytes accessed | tf_op | source)
XLA Modules:
  0.0 157.5 jit_solution(15197999065369323221)
XLA Ops:
  0.0 2.0 %shard_map.92 = (f32[2,264,256]{2,1,0:T(8,128)}, f32[264,256]{1,0:T(8,128)}) custom-call(f32[2,512,256]{2,1,0:T(8,128)} %bitcast.11, s32[2,1,512]{2,1,0:T(1,128)} %refs_2_.5, f32[2,4,512]{2,1,0:T(4,128)} %bitcast.17), custom_call_target="tpu_custom_call" | custom-call | bytes 1880064 | tf_op jit(solution)/shard_map/pallas_call | solution.py:162
  2.1 3.1 %collective-permute-start = (f32[2,264,256]{2,1,0:T(8,128)}, f32[2,264,256]{2,1,0:T(8,128)S(1)}, u32[]{:S(2)}, u32[]{:S(2)}) collective-permute-start(f32[2,264,256]{2,1,0:T(8,128)} %get-tuple-element.47), channel_id=1, source_target_pairs={{0,1},{1,2},{2,3},{3,4},{4,5},{5,6},{6,7},{7,8},{8,9},{9,10},{10,1... | collective-permute-start | bytes 1622024 | tf_op jit(solution)/shard_map/ppermute | solution.py:544
  5.2 2.5 %shard_map.91 = f32[16,8,256]{2,1,0:T(8,128)} custom-call(f32[2,512,256]{2,1,0:T(8,128)} %bitcast.12, f32[2,4,512]{2,1,0:T(4,128)} %bitcast.18), custom_call_target="tpu_custom_call" | custom-call | bytes 1196032 | tf_op jit(solution)/shard_map/pallas_call | solution.py:162
  7.7 7.7 %all-to-all-start = ((f32[16,8,256]{2,1,0:T(8,128)}), f32[16,8,256]{2,1,0:T(8,128)S(1)}, u32[]{:S(2)}, u32[]{:S(2)}) async-start(f32[16,8,256]{2,1,0:T(8,128)} %shard_map.91), calls=%async_computation | async-start | bytes 262144 | tf_op jit(solution)/shard_map/all_to_all | solution.py:569
  15.4 1.2 collective-permute-start.1
  16.6 3.9 %shard_map.93 = (f32[256,128]{1,0:T(8,128)}, f32[256,256]{1,0:T(8,128)}) custom-call(s32[3]{0:T(128)S(1)} %pad_add_fusion.refs_0_, s32[1,512]{1,0:T(1,128)} %bitcast.20, f32[512,512]{1,0:T(8,128)} %refs_2_.3), custom_call_target="tpu_custom_call" | custom-call | bytes 1443852 | tf_op jit(solution)/shard_map/pallas_call | solution.py:162
  20.5 6.2 %shard_map.94.refs_12_.refs_13_ = bf16[2,1024,1024]{2,1,0:T(8,128)(2,1)} custom-call(bf16[2,1024,1024]{2,1,0:T(8,128)(2,1)} %bitcast.16, s32[2,1,256]{2,1,0:T(1,128)} %refs_0_.1, s32[2,1,256]{2,1,0:T(1,128)} %refs_1_.5), custom_call_target="tpu_custom_call" | custom-call | flops 2147483648 | bytes 8392704 | tf_op jit(solution)/shard_map/pallas_call | solution.py:162
  26.8 7.1 %shard_map.95 = (bf16[2,1024,1024]{2,1,0:T(8,128)(2,1)}, f32[2,256,256]{2,1,0:T(8,128)}, f32[2,256,256]{2,1,0:T(8,128)}, f32[256,256]{1,0:T(8,128)}, f32[256,256]{1,0:T(8,128)}, /*index=5*/f32[256,256]{1,0:T(8,128)}) custom-call(s32[2,1,256]{2,1,0:T(1,128)} %refs_0_.1, s32[2,1,256]{2,1,0:T(1,128)} %refs_1_.5, s32[2,1,512]{2,1,0:T(1,128)} %refs_2_.5, ...), custom_call_target="tpu_custom_call" | custom-call | flops 3221225472 | bytes 12091392 | tf_op jit(solution)/shard_map/pallas_call | solution.py:162
  34.4 1.5 collective-permute-start.2
  36.0 1.3 collective-permute-start.5
  37.2 2.3 %collective-permute-start.4 = (f32[256,256]{1,0:T(8,128)}, f32[256,256]{1,0:T(8,128)S(1)}, u32[]{:S(2)}, u32[]{:S(2)}) collective-permute-start(f32[256,256]{1,0:T(8,128)} %get-tuple-element.64.refs_5_), channel_id=1, source_target_pairs={{0,224},{32,0},{64,32},{96,64},{128,96},{160,128},{192,160},{224,1... | collective-permute-start | bytes 786440 | tf_op jit(solution)/shard_map/ppermute | solution.py:544
  39.5 2.0 %shard_map.96 = f32[16,16,256]{2,1,0:T(8,128)} custom-call(f32[16,8,256]{2,1,0:T(8,128)S(1)} %all-to-all-done.refs_0_, f32[256,128]{1,0:T(8,128)} %get-tuple-element.59.refs_1_), custom_call_target="tpu_custom_call" | custom-call | bytes 524288 | tf_op jit(solution)/shard_map/pallas_call | solution.py:162
  41.5 5.3 %all-to-all-start.1 = ((f32[16,16,256]{2,1,0:T(8,128)}), f32[16,16,256]{2,1,0:T(8,128)S(1)}, u32[]{:S(2)}, u32[]{:S(2)}) async-start(f32[16,16,256]{2,1,0:T(8,128)} %shard_map.96), calls=%async_computation.1 | async-start | bytes 524288 | tf_op jit(solution)/shard_map/all_to_all | solution.py:595
  46.8 2.2 %shard_map.97 = (bf16[7,48,256]{2,1,0:T(8,128)(2,1)}, bf16[7,256,128]{2,1,0:T(8,128)(2,1)}) custom-call(f32[2,4,512]{2,1,0:T(4,128)} %bitcast.19, f32[2,264,256]{2,1,0:T(8,128)} %copy-done.2, f32[264,256]{1,0:T(8,128)} %copy-done.4), custom_call_target="tpu_custom_call" | custom-call | bytes 1458176 | tf_op jit(solution)/shard_map/pallas_call | solution.py:162
  49.0 11.1 %all-to-all-done.1.refs_0_ = f32[16,16,256]{2,1,0:T(8,128)S(1)} async-done(((f32[16,16,256]{2,1,0:T(8,128)}), f32[16,16,256]{2,1,0:T(8,128)S(1)}, u32[]{:S(2)}, u32[]{:S(2)}) %all-to-all-start.1) | async-done | bytes 262176 | tf_op jit(solution)/shard_map/all_to_all | solution.py:595
  60.1 7.6 %shard_map.98 = (f32[7,256,256]{2,1,0:T(8,128)}, f32[2,256,256]{2,1,0:T(8,128)}, f32[2,256,256]{2,1,0:T(8,128)}, f32[256,256]{1,0:T(8,128)}, f32[256,256]{1,0:T(...) custom-call(f32[16,16,256]{2,1,0:T(8,128)S(1)} %all-to-all-done.1.refs_0_, ...), custom_call_target="tpu_custom_call" | custom-call | flops 1073741824 | bytes 13492224 | tf_op jit(solution)/shard_map/pallas_call | solution.py:162
  67.7 7.5 %all-to-all-start.2 = ((f32[16,16,256]{2,1,0:T(8,128)}), f32[16,16,256]{2,1,0:T(8,128)S(1)}, u32[]{:S(2)}, u32[]{:S(2)}) async-start(f32[16,16,256]{2,1,0:T(8,128)} %get-tuple-element.68), calls=%async_computation.2 | async-start | bytes 524288 | tf_op jit(solution)/shard_map/all_to_all | solution.py:609
  75.4 1.6 collective-permute-start.6
  77.0 3.6 %collective-permute-start.8 = (f32[256,256]{1,0:T(8,128)}, f32[256,256]{1,0:T(8,128)S(1)}, u32[]{:S(2)}, u32[]{:S(2)}) collective-permute-start(f32[256,256]{1,0:T(8,128)} %get-tuple-element.74.refs_8_), channel_id=1, source_target_pairs={{0,224},{32,0},{64,32},{96,64},{128,96},{160,128},{192,160},{224,1... | collective-permute-start | bytes 786440 | tf_op jit(solution)/shard_map/ppermute | solution.py:544
  80.5 6.9 %all-to-all-done.2.refs_0_ = f32[16,16,256]{2,1,0:T(8,128)S(1)} async-done(((f32[16,16,256]{2,1,0:T(8,128)}), f32[16,16,256]{2,1,0:T(8,128)S(1)}, u32[]{:S(2)}, u32[]{:S(2)}) %all-to-all-start.2) | async-done | bytes 262176 | tf_op jit(solution)/shard_map/all_to_all | solution.py:609
  87.5 2.0 %shard_map.99 = f32[16,16,256]{2,1,0:T(8,128)} custom-call(f32[16,16,256]{2,1,0:T(8,128)S(1)} %all-to-all-done.2.refs_0_, f32[256,256]{1,0:T(8,128)} %get-tuple-element.69.refs_1_), custom_call_target="tpu_custom_call" | custom-call | bytes 786432 | tf_op jit(solution)/shard_map/pallas_call | solution.py:162
  89.5 3.5 %all-to-all-start.3 = ((f32[16,16,256]{2,1,0:T(8,128)}), f32[16,16,256]{2,1,0:T(8,128)S(1)}, u32[]{:S(2)}, u32[]{:S(2)}) async-start(f32[16,16,256]{2,1,0:T(8,128)} %shard_map.99), calls=%async_computation.3 | async-start | bytes 524288 | tf_op jit(solution)/shard_map/all_to_all | solution.py:611
  93.1 2.4 %collective-permute-done.8.refs_12_ = f32[256,256]{1,0:T(8,128)S(1)} collective-permute-done((f32[256,256]{1,0:T(8,128)}, f32[256,256]{1,0:T(8,128)S(1)}, u32[]{:S(2)}, u32[]{:S(2)}) %collective-permute-start.8) | collective-permute-done | bytes 262176 | tf_op jit(solution)/shard_map/ppermute | solution.py:544
  95.4 5.7 %all-to-all-done.3.refs_0_ = f32[16,16,256]{2,1,0:T(8,128)S(1)} async-done(((f32[16,16,256]{2,1,0:T(8,128)}), f32[16,16,256]{2,1,0:T(8,128)S(1)}, u32[]{:S(2)}, u32[]{:S(2)}) %all-to-all-start.3) | async-done | bytes 262176 | tf_op jit(solution)/shard_map/all_to_all | solution.py:611
  101.1 5.7 %shard_map.100 = (f32[4,256,256]{2,1,0:T(8,128)S(1)}, f32[4,256,256]{2,1,0:T(8,128)S(1)}, f32[2,256,256]{2,1,0:T(8,128)S(1)}, f32[2,256,256]{2,1,0:T(8,128)S(1)}...) custom-call(f32[16,16,256]{2,1,0:T(8,128)S(1)} %all-to-all-done.3.re, ...), custom_call_target="tpu_custom_call" | custom-call | flops 1073741824 | bytes 13697024 | tf_op jit(solution)/shard_map/pallas_call | solution.py:162
  108.9 3.3 %collective-permute-start.12 = (f32[256,256]{1,0:T(8,128)S(1)}, f32[256,256]{1,0:T(8,128)S(1)}, u32[]{:S(2)}, u32[]{:S(2)}) collective-permute-start(f32[256,256]{1,0:T(8,128)S(1)} %get-tuple-element.81.refs_5_), channel_id=1, source_target_pairs={{0,224},{32,0},{64,32},{96,64},{128,96},{160,128},{192,160},{224,1... | collective-permute-start | bytes 786440 | tf_op jit(solution)/shard_map/ppermute | solution.py:544
  112.2 10.6 %collective-permute-done.13.refs_10_ = f32[256,256]{1,0:T(8,128)S(1)} collective-permute-done((f32[256,256]{1,0:T(8,128)S(1)}, f32[256,256]{1,0:T(8,128)S(1)}, u32[]{:S(2)}, u32[]{:S(2)}) %collective-permute-start.13) | collective-permute-done | bytes 262176 | tf_op jit(solution)/shard_map/ppermute | solution.py:544
  122.8 3.1 %collective-permute-done.12.refs_9_ = f32[256,256]{1,0:T(8,128)S(1)} collective-permute-done((f32[256,256]{1,0:T(8,128)S(1)}, f32[256,256]{1,0:T(8,128)S(1)}, u32[]{:S(2)}, u32[]{:S(2)}) %collective-permute-start.12) | collective-permute-done | bytes 262176 | tf_op jit(solution)/shard_map/ppermute | solution.py:544
  125.9 2.5 %shard_map.101 = (f32[4,256,256]{2,1,0:T(8,128)}, f32[16,4,256]{2,1,0:T(4,128)}) custom-call(f32[16,256]{1,0:T(8,128)S(1)} %get-tuple-element.77.refs_0_, bf16[7,256,128]{2,1,0:T(8,128)(2,1)S(1)} %copy-done.3, f32[2,256,256]{2,1,0:T(8,128)S(1)} %get-tuple-element.78.refs_2_, f32[2,256,256]{2,1,0:T(8,128)S(1)} %get-tuple-element.79.refs_3_, ...), custom_call_target="tpu_custom_call" | custom-call | flops 1073741824 | bytes 13123584 | tf_op jit(solution)/shard_map/pallas_call | solution.py:162
  128.4 13.9 %all_to_all.30.refs_0_ = f32[16,4,256]{2,1,0:T(4,128)S(1)} all-to-all(f32[16,4,256]{2,1,0:T(4,128)} %get-tuple-element.86), channel_id=1, replica_groups=mesh['y'=4,'xl'=2,'xh'=2,'z'=8,'c'=2] {'z','c'}, dimensions={0} | all-to-all | bytes 131072 | tf_op jit(solution)/shard_map/all_to_all | solution.py:625
  142.9 12.0 %all_to_all.31.refs_0_ = f32[16,4,256]{2,1,0:T(4,128)S(1)} all-to-all(f32[16,4,256]{2,1,0:T(4,128)} %shard_map.102), channel_id=1, replica_groups=mesh['y'=4,'xl'=2,'xh'=2,'z'=8,'c'=2] {'y','xl','xh'}, dimensions={0} | all-to-all | bytes 131072 | tf_op jit(solution)/shard_map/all_to_all | solution.py:627
  154.8 2.4 %shard_map.103 = f32[2,512,256]{2,1,0:T(8,128)} custom-call(f32[16,4,256]{2,1,0:T(4,128)S(1)} %all_to_all.31.refs_0_, f32[8,256]{1,0:T(8,128)} %get-tuple-element.87.refs_1_, f32[7,256,256]{2,1,0:T(8,128)} %get-tuple-element.85.refs_14_.refs_2_, f32[4,256,256]{2,1,0:T(8,128)} %get-tuple-element.88.refs_3_), custom_call_target="tpu_custom_call" | custom-call | bytes 4005888 | tf_op jit(solution)/shard_map/pallas_call | solution.py:162
  (30 shorter events, 3.6 us)
Async XLA Ops:
  2.1 24.7 %collective-permute-start = (f32[2,264,256]{2,1,0:T(8,128)}, f32[2,264,256]{2,1,0:T(8,128)S(1)}, u32[]{:S(2)}, u32[]{:S(2)}) collective-permute-start(f32[2,264,256]{2,1,0:T(8,128)} %get-tuple-element.47), channel_id=1, source_target_pairs={{0,1},{1,2},{2,3},{3,4},{4,5},{5,6},{6,7},{7,8},{8,9},{9,10},{10,1... | collective-permute-start | bytes 1622024 | tf_op jit(solution)/shard_map/ppermute | solution.py:544
  7.7 26.2 %all-to-all-start = ((f32[16,8,256]{2,1,0:T(8,128)}), f32[16,8,256]{2,1,0:T(8,128)S(1)}, u32[]{:S(2)}, u32[]{:S(2)}) async-start(f32[16,8,256]{2,1,0:T(8,128)} %shard_map.91), calls=%async_computation | async-start | bytes 262144 | tf_op jit(solution)/shard_map/all_to_all | solution.py:569
  15.4 11.4 %collective-permute-start.1 = (f32[264,256]{1,0:T(8,128)}, f32[264,256]{1,0:T(8,128)S(1)}, u32[]{:S(2)}, u32[]{:S(2)}) collective-permute-start(f32[264,256]{1,0:T(8,128)} %get-tuple-element.48), channel_id=1, source_target_pairs={{0,32},{32,64},{64,96},{96,128},{128,160},{160,192},{192,224},{224... | collective-permute-start | bytes 811016 | tf_op jit(solution)/shard_map/ppermute | solution.py:544
  26.7 7.1 %copy-start.4 = (f32[264,256]{1,0:T(8,128)}, f32[264,256]{1,0:T(8,128)S(1)}, u32[]{:S(2)}) copy-start(f32[264,256]{1,0:T(8,128)S(1)} %collective-permute-done.1.refs_6_.refs_2_.refs_3_) | copy-start | bytes 811012
  26.8 7.1 %copy-start.2 = (f32[2,264,256]{2,1,0:T(8,128)}, f32[2,264,256]{2,1,0:T(8,128)S(1)}, u32[]{:S(2)}) copy-start(f32[2,264,256]{2,1,0:T(8,128)S(1)} %collective-permute-done.refs_5_.refs_1_.refs_2_) | copy-start | bytes 1622020
  33.9 26.2 %collective-permute-start.3 = (f32[2,256,256]{2,1,0:T(8,128)}, f32[2,256,256]{2,1,0:T(8,128)S(1)}, u32[]{:S(2)}, u32[]{:S(2)}) collective-permute-start(f32[2,256,256]{2,1,0:T(8,128)} %get-tuple-element.61.refs_2_), channel_id=1, source_target_pairs={{0,31},{1,0},{2,1},{3,2},{4,3},{5,4},{6,5},{7,6},{8,7},{9,8},{10,9... | collective-permute-start | bytes 1572872 | tf_op jit(solution)/shard_map/ppermute | solution.py:544
  34.4 25.7 %collective-permute-start.2 = (f32[2,256,256]{2,1,0:T(8,128)}, f32[2,256,256]{2,1,0:T(8,128)S(1)}, u32[]{:S(2)}, u32[]{:S(2)}) collective-permute-start(f32[2,256,256]{2,1,0:T(8,128)} %get-tuple-element.62.refs_3_), channel_id=1, source_target_pairs={{0,1},{1,2},{2,3},{3,4},{4,5},{5,6},{6,7},{7,8},{8,9},{9,10},{10,1... | collective-permute-start | bytes 1572872 | tf_op jit(solution)/shard_map/ppermute | solution.py:544
  36.0 24.1 %collective-permute-start.5 = (f32[256,256]{1,0:T(8,128)}, f32[256,256]{1,0:T(8,128)S(1)}, u32[]{:S(2)}, u32[]{:S(2)}) collective-permute-start(f32[256,256]{1,0:T(8,128)} %get-tuple-element.63.refs_4_), channel_id=1, source_target_pairs={{0,32},{32,64},{64,96},{96,128},{128,160},{160,192},{192,224},{224... | collective-permute-start | bytes 786440 | tf_op jit(solution)/shard_map/ppermute | solution.py:544
  37.2 22.9 %collective-permute-start.4 = (f32[256,256]{1,0:T(8,128)}, f32[256,256]{1,0:T(8,128)S(1)}, u32[]{:S(2)}, u32[]{:S(2)}) collective-permute-start(f32[256,256]{1,0:T(8,128)} %get-tuple-element.64.refs_5_), channel_id=1, source_target_pairs={{0,224},{32,0},{64,32},{96,64},{128,96},{160,128},{192,160},{224,1... | collective-permute-start | bytes 786440 | tf_op jit(solution)/shard_map/ppermute | solution.py:544
  41.5 18.6 %all-to-all-start.1 = ((f32[16,16,256]{2,1,0:T(8,128)}), f32[16,16,256]{2,1,0:T(8,128)S(1)}, u32[]{:S(2)}, u32[]{:S(2)}) async-start(f32[16,16,256]{2,1,0:T(8,128)} %shard_map.96), calls=%async_computation.1 | async-start | bytes 524288 | tf_op jit(solution)/shard_map/all_to_all | solution.py:595
  67.7 19.7 %all-to-all-start.2 = ((f32[16,16,256]{2,1,0:T(8,128)}), f32[16,16,256]{2,1,0:T(8,128)S(1)}, u32[]{:S(2)}, u32[]{:S(2)}) async-start(f32[16,16,256]{2,1,0:T(8,128)} %get-tuple-element.68), calls=%async_computation.2 | async-start | bytes 524288 | tf_op jit(solution)/shard_map/all_to_all | solution.py:609
  75.2 20.2 %collective-permute-start.7 = (f32[2,256,256]{2,1,0:T(8,128)}, f32[2,256,256]{2,1,0:T(8,128)S(1)}, u32[]{:S(2)}, u32[]{:S(2)}) collective-permute-start(f32[2,256,256]{2,1,0:T(8,128)} %get-tuple-element.71.refs_5_), channel_id=1, source_target_pairs={{0,31},{1,0},{2,1},{3,2},{4,3},{5,4},{6,5},{7,6},{8,7},{9,8},{10,9... | collective-permute-start | bytes 1572872 | tf_op jit(solution)/shard_map/ppermute | solution.py:544
  75.4 20.0 %collective-permute-start.6 = (f32[2,256,256]{2,1,0:T(8,128)}, f32[2,256,256]{2,1,0:T(8,128)S(1)}, u32[]{:S(2)}, u32[]{:S(2)}) collective-permute-start(f32[2,256,256]{2,1,0:T(8,128)} %get-tuple-element.72.refs_6_), channel_id=1, source_target_pairs={{0,1},{1,2},{2,3},{3,4},{4,5},{5,6},{6,7},{7,8},{8,9},{9,10},{10,1... | collective-permute-start | bytes 1572872 | tf_op jit(solution)/shard_map/ppermute | solution.py:544
  77.0 16.1 %collective-permute-start.9 = (f32[256,256]{1,0:T(8,128)}, f32[256,256]{1,0:T(8,128)S(1)}, u32[]{:S(2)}, u32[]{:S(2)}) collective-permute-start(f32[256,256]{1,0:T(8,128)} %get-tuple-element.73.refs_7_), channel_id=1, source_target_pairs={{0,32},{32,64},{64,96},{96,128},{128,160},{160,192},{192,224},{224... | collective-permute-start | bytes 786440 | tf_op jit(solution)/shard_map/ppermute | solution.py:544
  77.0 18.5 %collective-permute-start.8 = (f32[256,256]{1,0:T(8,128)}, f32[256,256]{1,0:T(8,128)S(1)}, u32[]{:S(2)}, u32[]{:S(2)}) collective-permute-start(f32[256,256]{1,0:T(8,128)} %get-tuple-element.74.refs_8_), channel_id=1, source_target_pairs={{0,224},{32,0},{64,32},{96,64},{128,96},{160,128},{192,160},{224,1... | collective-permute-start | bytes 786440 | tf_op jit(solution)/shard_map/ppermute | solution.py:544
  89.5 11.6 %all-to-all-start.3 = ((f32[16,16,256]{2,1,0:T(8,128)}), f32[16,16,256]{2,1,0:T(8,128)S(1)}, u32[]{:S(2)}, u32[]{:S(2)}) async-start(f32[16,16,256]{2,1,0:T(8,128)} %shard_map.99), calls=%async_computation.3 | async-start | bytes 524288 | tf_op jit(solution)/shard_map/all_to_all | solution.py:611
  101.1 24.8 %copy-start = (bf16[2,1024,1024]{2,1,0:T(8,128)(2,1)S(1)}, bf16[2,1024,1024]{2,1,0:T(8,128)(2,1)}, u32[]{:S(2)}) copy-start(bf16[2,1024,1024]{2,1,0:T(8,128)(2,1)} %shard_map.94.refs_12_.refs_13_) | copy-start | bytes 12582916
  101.1 24.8 %copy-start.1 = (f32[7,256,256]{2,1,0:T(8,128)S(1)}, f32[7,256,256]{2,1,0:T(8,128)}, u32[]{:S(2)}) copy-start(f32[7,256,256]{2,1,0:T(8,128)} %get-tuple-element.85.refs_14_.refs_2_) | copy-start | bytes 5505028
  101.1 24.8 %copy-start.3 = (bf16[7,256,128]{2,1,0:T(8,128)(2,1)S(1)}, bf16[7,256,128]{2,1,0:T(8,128)(2,1)}, u32[]{:S(2)}) copy-start(bf16[7,256,128]{2,1,0:T(8,128)(2,1)} %get-tuple-element.60.refs_1_) | copy-start | bytes 1376260
  106.8 19.1 %collective-permute-start.11 = (f32[2,256,256]{2,1,0:T(8,128)S(1)}, f32[2,256,256]{2,1,0:T(8,128)S(1)}, u32[]{:S(2)}, u32[]{:S(2)}) collective-permute-start(f32[2,256,256]{2,1,0:T(8,128)S(1)} %get-tuple-element.78.refs_2_), channel_id=1, source_target_pairs={{0,31},{1,0},{2,1},{3,2},{4,3},{5,4},{6,5},{7,6},{8,7},{9,8},{10,9... | collective-permute-start | bytes 1572872 | tf_op jit(solution)/shard_map/ppermute | solution.py:544
  107.8 18.1 %collective-permute-start.10 = (f32[2,256,256]{2,1,0:T(8,128)S(1)}, f32[2,256,256]{2,1,0:T(8,128)S(1)}, u32[]{:S(2)}, u32[]{:S(2)}) collective-permute-start(f32[2,256,256]{2,1,0:T(8,128)S(1)} %get-tuple-element.79.refs_3_), channel_id=1, source_target_pairs={{0,1},{1,2},{2,3},{3,4},{4,5},{5,6},{6,7},{7,8},{8,9},{9,10},{10,1... | collective-permute-start | bytes 1572872 | tf_op jit(solution)/shard_map/ppermute | solution.py:544
  108.6 14.2 %collective-permute-start.13 = (f32[256,256]{1,0:T(8,128)S(1)}, f32[256,256]{1,0:T(8,128)S(1)}, u32[]{:S(2)}, u32[]{:S(2)}) collective-permute-start(f32[256,256]{1,0:T(8,128)S(1)} %get-tuple-element.80.refs_4_), channel_id=1, source_target_pairs={{0,32},{32,64},{64,96},{96,128},{128,160},{160,192},{192,224},{224... | collective-permute-start | bytes 786440 | tf_op jit(solution)/shard_map/ppermute | solution.py:544
  108.9 17.0 %collective-permute-start.12 = (f32[256,256]{1,0:T(8,128)S(1)}, f32[256,256]{1,0:T(8,128)S(1)}, u32[]{:S(2)}, u32[]{:S(2)}) collective-permute-start(f32[256,256]{1,0:T(8,128)S(1)} %get-tuple-element.81.refs_5_), channel_id=1, source_target_pairs={{0,224},{32,0},{64,32},{96,64},{128,96},{160,128},{192,160},{224,1... | collective-permute-start | bytes 786440 | tf_op jit(solution)/shard_map/ppermute | solution.py:544

commit v3 on v2

--- a/solution.py
+++ b/solution.py
@@ -169,7 +169,7 @@
         scratch_shapes=[pltpu.VMEM(s, d) for s, d in staged]
         + [pltpu.SemaphoreType.DMA((max(1, sum(len(p) for p in pieces)),)), *scratch],
         compiler_params=pltpu.CompilerParams(vmem_limit_bytes=32 * 1024 * 1024),
-        cost_estimate=pl.CostEstimate(flops=flops, bytes_accessed=size, transcendentals=0),
+        cost_estimate=pl.CostEstimate(flops=0, bytes_accessed=0, transcendentals=0),
     )(*args)
 
 
@@ -234,7 +234,7 @@
     return jnp.where(order_row == rows, -1.0, 0.0).astype(BF16)
 
 
-def reorder_block(s, out, work_ref, k, orders, weights):
+def reorder_block(s, outs, work_ref, k, orders, weights):
     for row in range(4):
         rows = s.get(block_piece(k, row))
         for side in range(4):
@@ -249,23 +249,24 @@
             part = nn(orders[row], part)
         if weights[row] is not None:
             part = part.astype(F32) * scale_column(weights[row])
-        out.put(part.astype(BF16), block_piece(k, row))
+        for out in outs:
+            out.put(part.astype(BF16), block_piece(k, row))
 
 
 def reorder_plain_kernel(s, left, down, out, work_ref):
     left_ref, down_ref = left.get(), down.get()
     for k in range(2):
         orders = (placed(left_ref[k]), None, placed(down_ref[k]), None)
-        reorder_block(s, out, work_ref, k, orders, (None,) * 4)
-
-
-def reorder_weighted_kernel(s, left, down, occ, out, work_ref):
+        reorder_block(s, (out,), work_ref, k, orders, (None,) * 4)
+
+
+def reorder_weighted_kernel(s, left, down, occ, out, twin, work_ref):
     left_ref, down_ref, occ_ref = left.get(), down.get(), occ.get()
     first, second = weights_of(occ_ref, 0), weights_of(occ_ref, 1)
     for k, weight in enumerate((first, second)):
         orders = (placed(left_ref[k]), None, placed(down_ref[k]), None)
         below = None if k == 0 else first[:, F:]
-        reorder_block(s, out, work_ref, k, orders, (None, weight[:, :F], below, weight[:, F:]))
+        reorder_block(s, (out, twin), work_ref, k, orders, (None, weight[:, :F], below, weight[:, F:]))
 
 
 def basis_kernel(basis, from_left, from_down, rows, columns, flat_ref):
@@ -315,11 +316,14 @@
     far_rows = corner_onehot(numbers_t, 2 * (peer >> 1) + da, (peer & 1) * 16 + near + ds, spare)
     near_rows = corner_onehot(numbers_t, 2 * blk + da, xh * 16 + peer + ds, spare)
     few = lax.broadcasted_iota(jnp.int32, (16 * 8, 1), 0)
-    own = few & 7
-    own_rows = corner_onehot(numbers_t, 2 * blk + (own >> 1), xh * 16 + (few >> 3) + (own & 1), own >= 6)
-    picked = thirds(sum(nn(far_rows, part) for part in thirds(inverse.get()[...])[::-1]))[::-1]
+    source, own = few >> 3, few & 7
+    own_rows = corner_onehot(
+        numbers_t, 2 * (source >> 1) + (own >> 1), (source & 1) * 16 + near + (own & 1), own >= 6
+    )
+    terms = thirds(inverse.get()[...])[::-1]
+    picked = thirds(sum(nn(near_rows, part) for part in terms))[::-1]
     first.put(sum(nt(part, own_rows) for part in picked))
-    block = sum(nt(part, near_rows) for part in picked)
+    block = sum(nt(part, far_rows) for part in picked)
     columns = lax.broadcasted_iota(jnp.int32, (16 * SLOTS, 16 * SLOTS), 1) & 15
     passed = (columns == entry) & spare
     later.put(jnp.where(passed, 1.0, block))
@@ -328,20 +332,31 @@
 HALVES = [((2, F, R), F32), ((2, F, R), F32), ((F, R), F32), ((F, R), F32), ((F, R), F32)]
 
 
-def apply_block(s, operand_ref, left, right, up, down, mid, weights=None):
-    def outer(value, which):
-        return value if weights is None else value * weights[which]
-
+def apply_block(s, operand_ref, left, right, up, down, mid, weights=None, seen=None):
+    stores = {
+        0: lambda v: right.put(v, (0,)),
+        1: lambda v: right.put(v, (1,)),
+        2: mid.put,
+        3: up.put,
+        4: lambda v: left.put(v, (0,)),
+        5: lambda v: left.put(v, (1,)),
+        6: down.put,
+    }
+    shared = None
     for k in range(2):
-        sides = [nn(s.get(block_piece(k, side))[...], operand_ref[k]) for side in range(4)]
-        left.put(outer(sides[0], k), (k,))
-        right.put(sides[1], (k,))
-        if k == 0:
-            down.put(outer(sides[2], 2))
-            shared = sides[3]
-        else:
-            mid.put(shared + sides[2])
-            up.put(sides[3])
+        for side in range(4):
+            face = SIDES[k][side]
+            image = nn(s.get(block_piece(k, side))[...], operand_ref[k])
+            if face == 2:
+                if shared is None:
+                    shared = image
+                    continue
+                image = shared + image
+            if weights is not None and face >= 4:
+                image = image * weights[face - 4]
+            stores[face](image)
+            if seen is not None:
+                seen(face, image)
 
 
 def set_operand(operand_ref, face, value):
@@ -358,18 +373,14 @@
     return [scale_column(row) for row in rows]
 
 
-def first_kernel(
-    left_order, down_order, occ, s, r, from_left, from_down,
-    block, left, right, up, down, mid, operand_ref, strip_ref,
-):
-    reorder_weighted_kernel(s, left_order, down_order, occ, block, strip_ref)
+def first_kernel(r, from_left, from_down, s, left, right, up, down, mid, operand_ref):
     weights = outer_weights(from_left, from_down)
+    set_operand(operand_ref, 6, from_down.get()[:F, :] * weights[2])
     for k in range(2):
-        set_operand(operand_ref, k, own_face(r, k))
-        set_operand(operand_ref, 2 + k, own_face(r, 2 + k))
         set_operand(operand_ref, 4 + k, from_left.get((k,))[:F, :] * weights[k])
-    set_operand(operand_ref, 6, from_down.get()[:F, :] * weights[2])
-    apply_block(Here(block.held), operand_ref, left, right, up, down, mid, weights)
+    for face in range(4):
+        set_operand(operand_ref, face, own_face(r, face))
+    apply_block(s, operand_ref, left, right, up, down, mid, weights)
 
 
 PLACES = ((1, (0,)), (1, (1,)), (4, ()), (2, ()), (0, (0,)), (0, (1,)), (3, ()))
@@ -378,11 +389,6 @@
 def own_share(halves, face):
     which, piece = PLACES[face]
     return halves[which].get(piece)[...]
-
-
-def own_image(halves, face):
-    which, piece = PLACES[face]
-    return halves[which].held[piece if piece else ...]
 
 
 def assembled(halves, others, face):
@@ -416,7 +422,7 @@
 
 
 def operate_first_kernel(
-    values, columns, l0, r0, u0, d0, m0, fl, fr, fu, fd, r, s, rows,
+    values, columns, l0, r0, u0, d0, m0, fl, fr, fu, fd, r, rows, s,
     z, left, right, up, down, mid, message, corners_out, operand_ref,
 ):
     corners = jnp.sum(values.get()[...], axis=0)
@@ -432,14 +438,15 @@
         set_operand(operand_ref, face, value)
         if face < 4:
             progress = progress + total(own_face(r, face) * value)
-    apply_block(s, operand_ref, *images)
     rows_ref = rows.get()
-    loads = jnp.zeros((SLOTS, R), F32)
-    curvature = jnp.zeros((1, R), F32)
-    for face in range(FACES):
-        image = own_image(images, face)
-        loads = loads + face_loads(rows_ref, face, image)
-        curvature = curvature + total(z.held[face] * image)
+    sums = [jnp.zeros((SLOTS, R), F32), jnp.zeros((1, R), F32)]
+
+    def seen(face, image):
+        sums[0] = sums[0] + face_loads(rows_ref, face, image)
+        sums[1] = sums[1] + total(z.held[face] * image)
+
+    apply_block(s, operand_ref, *images, seen=seen)
+    loads, curvature = sums
     for peer in range(16):
         message.held[peer] = loads
         message.held[peer, 12:13, :] = progress
@@ -566,33 +573,37 @@
     r_left = moved(right, CROSS, 32, 1)
     r_down = moved(up, BLK, 8, 1)
     (loads,) = call(loads_kernel, [((16, 8, R), F32)], r, basis)
-    near = lax.all_to_all(loads, NEAR, 0, 0)
+    far = lax.all_to_all(loads, FAR, 0, 0)
     first_block, later_block = call(
         coarse_block_kernel,
         [((16 * SLOTS, 16 * 8), F32), ((16 * SLOTS, 16 * SLOTS), F32)],
         place, numbers[None, :], coarse_inverse,
-        smem=(0,),
-    )
+        smem=(0,), near_out=(0, 1),
+    )
+    schur_block, schur_here = call(
+        reorder_weighted_kernel,
+        [(s.shape, BF16), (s.shape, BF16)],
+        s, left_order, down_order, occ,
+        flops=2 * MATMUL_FLOPS, near_out=(1,), scratch=[strip],
+    )
+    r_left, r_down, first_block, later_block, schur_here = lax.optimization_barrier(
+        (r_left, r_down, first_block, later_block, schur_here)
+    )
+
+    halves = call(
+        first_kernel, HALVES, r, r_left, r_down, schur_here,
+        flops=MATMUL_FLOPS, near=(1, 2, 3), scratch=[operand],
+    )
+    far, s_inverse, *halves = lax.optimization_barrier((far, s_inverse, *halves))
+    others = exchanged(*halves[:4])
+    (partial,) = call(partial_kernel, [((16, SLOTS, R), F32)], far, first_block, near=(0, 1))
+    values = lax.all_to_all(partial, NEAR, 0, 0)
     (inverse_block,) = call(
         reorder_plain_kernel,
         [(s_inverse.shape, BF16)],
         s_inverse, left_order, down_order,
         flops=2 * MATMUL_FLOPS, scratch=[strip],
     )
-    r_left, r_down, first_block, later_block, inverse_block = lax.optimization_barrier(
-        (r_left, r_down, first_block, later_block, inverse_block)
-    )
-
-    schur_block, *halves = call(
-        first_kernel,
-        [(s.shape, BF16), *HALVES],
-        left_order, down_order, occ, s, r, r_left, r_down,
-        flops=3 * MATMUL_FLOPS, near=(5, 6), scratch=[operand, strip],
-    )
-    near, *halves = lax.optimization_barrier((near, *halves))
-    others = exchanged(*halves[:4])
-    (partial,) = call(partial_kernel, [((16, SLOTS, R), F32)], near, first_block, near=(0,))
-    values = lax.all_to_all(partial, FAR, 0, 0)
     rows, columns = call(
         basis_kernel,
         [((FACES, 48, F), BF16), ((FACES, F, 128), BF16)],
@@ -602,13 +613,13 @@
     z0, *halves, message, corners = call(
         operate_first_kernel,
         [((FACES, F, R), F32), *HALVES, ((16, SLOTS, R), F32), ((SLOTS, R), F32)],
-        values, columns, *halves, *others, r, inverse_block, rows,
+        values, columns, *halves, *others, r, rows, inverse_block,
         flops=MATMUL_FLOPS, near=(0, 7, 8, 9, 10), scratch=[operand],
     )
     others = exchanged(*halves[:4])
-    near = lax.all_to_all(message, NEAR, 0, 0)
-    (partial,) = call(partial_kernel, [((16, SLOTS, R), F32)], near, later_block, near=(0,))
-    values = lax.all_to_all(partial, FAR, 0, 0)
+    far = lax.all_to_all(message, FAR, 0, 0)
+    (partial,) = call(partial_kernel, [((16, SLOTS, R), F32)], far, later_block, near=(0, 1))
+    values = lax.all_to_all(partial, NEAR, 0, 0)
     residual, image, *halves, corners, scalars = call(
         second_kernel,
         [((4, F, R), F32), ((4, F, R), F32), *HALVES, ((SLOTS, R), F32), ((8, R), F32)],
@@ -620,12 +631,12 @@
         operate_last_kernel,
         [((4, F, R), F32), ((16, 4, R), F32)],
         corners, columns, *halves, *others, residual, image, inverse_block, z0,
-        flops=MATMUL_FLOPS, near=tuple(range(15)), scratch=[operand, pltpu.VMEM((FACES, F, R), F32)],
+        flops=MATMUL_FLOPS, near=tuple(range(15)), near_out=(0,), scratch=[operand, pltpu.VMEM((FACES, F, R), F32)],
     )
     near = lax.all_to_all(message, NEAR, 0, 0)
     (spread_sums,) = call(sum_kernel, [((16, 4, R), F32)], near, near=(0,))
     sums = lax.all_to_all(spread_sums, FAR, 0, 0)
-    (out,) = call(finish_kernel, [((2, 2 * F, R), F32)], sums, scalars, z0, z1, near=(0,), parts={2: 4})
+    (out,) = call(finish_kernel, [((2, 2 * F, R), F32)], sums, scalars, z0, z1, near=(0, 1, 2, 3))
     return out[:, None]
 
 

time: 159 us -> 158 us (level)
  waiting for transfers between devices: 39.7 us -> 33.2 us
  starting transfers between devices: 44.7 us -> 50.3 us
    all_to_all x4, waiting for transfers between devices: 23.6 us -> 5.54 us  [the longest x1 5.54 us: on_device(): far = lax.all_to_all(message, FAR, 0, 0)]
    ppermute x14, waiting for transfers between devices: 16.1 us -> 27.7 us  [moved(): lax.ppermute(block, axes, [(i, (i + distance) % count) for i in range(cou...]
    all_to_all x4, starting transfers between devices: 24 us -> 28.9 us  [the longest x2 16.1 us: on_device(): values = lax.all_to_all(partial, NEAR, 0, 0)]
    pallas_call x13 -> x14, Pallas kernels: 46.8 us -> 46.2 us  [call(): pl.pallas_call(body, out_shape=[jax.ShapeDtypeStruct(s, d) if i in near_o...]
  transfers between devices with their start and end apart: 18 -> 18, of which waited for: 6 -> 7; matrix products, arithmetic and copies ran while one was open for 0% -> 0% of each run, Pallas kernels for 16% -> 17%
where the time goes in v3:
time: 158 us; the launch traced here: 157 us
  starting transfers between devices  50.3 us (32%)
  Pallas kernels  46.2 us (29%)
  waiting for transfers between devices  33.2 us (21%)
  blocking collectives  26.8 us (17%)
    pallas_call x14, Pallas kernels, call(): pl.pallas_call(body, out_shape=[jax.ShapeDtypeStruct(s, d) if i in near_o...  46.2 us
    ppermute x14, waiting for transfers between devices, moved(): lax.ppermute(block, axes, [(i, (i + distance) % count) for i in range(cou...  27.7 us
    ppermute x14, starting transfers between devices, moved(): lax.ppermute(block, axes, [(i, (i + distance) % count) for i in range(cou...  21.5 us
    all_to_all x2, starting transfers between devices, on_device(): values = lax.all_to_all(partial, NEAR, 0, 0)  16.1 us
    all_to_all x1, blocking collectives, on_device(): near = lax.all_to_all(message, NEAR, 0, 0)  14.3 us
    all_to_all x1, blocking collectives, on_device(): sums = lax.all_to_all(spread_sums, FAR, 0, 0)  12.5 us
    all_to_all x1, starting transfers between devices, on_device(): far = lax.all_to_all(loads, FAR, 0, 0)  6.56 us
    all_to_all x1, starting transfers between devices, on_device(): far = lax.all_to_all(message, FAR, 0, 0)  6.19 us
  transfers between devices with their start and end apart: 18, of which 7 were waited for; matrix products, arithmetic and copies ran while one was open for 0% of the time, Pallas kernels for 17%

profile of v3, /device:TPU:1, one launch (start us, length us, event | category | flops | bytes accessed | tf_op | source)
XLA Modules:
  0.0 157.1 jit_solution(3129819998109690869)
XLA Ops:
  0.0 2.1 %shard_map.92 = (f32[2,264,256]{2,1,0:T(8,128)}, f32[264,256]{1,0:T(8,128)}) custom-call(f32[2,512,256]{2,1,0:T(8,128)} %bitcast.11, s32[2,1,512]{2,1,0:T(1,128)} %refs_3_.1, f32[2,4,512]{2,1,0:T(4,128)} %bitcast.18), custom_call_target="tpu_custom_call" | custom-call | tf_op jit(solution)/shard_map/pallas_call | solution.py:162
  2.1 3.1 %collective-permute-start = (f32[2,264,256]{2,1,0:T(8,128)}, f32[2,264,256]{2,1,0:T(8,128)S(1)}, u32[]{:S(2)}, u32[]{:S(2)}) collective-permute-start(f32[2,264,256]{2,1,0:T(8,128)} %get-tuple-element.49), channel_id=1, source_target_pairs={{0,1},{1,2},{2,3},{3,4},{4,5},{5,6},{6,7},{7,8},{8,9},{9,10},{10,1... | collective-permute-start | bytes 1622024 | tf_op jit(solution)/shard_map/ppermute | solution.py:551
  5.2 1.2 collective-permute-start.1
  6.4 2.5 %shard_map.91 = f32[16,8,256]{2,1,0:T(8,128)} custom-call(f32[2,512,256]{2,1,0:T(8,128)} %bitcast.12, f32[2,4,512]{2,1,0:T(4,128)} %bitcast.19), custom_call_target="tpu_custom_call" | custom-call | tf_op jit(solution)/shard_map/pallas_call | solution.py:162
  8.9 6.6 %all-to-all-start = ((f32[16,8,256]{2,1,0:T(8,128)}), f32[16,8,256]{2,1,0:T(8,128)S(1)}, u32[]{:S(2)}, u32[]{:S(2)}) async-start(f32[16,8,256]{2,1,0:T(8,128)} %shard_map.91), calls=%async_computation | async-start | bytes 262144 | tf_op jit(solution)/shard_map/all_to_all | solution.py:576
  15.6 3.1 %shard_map.93 = (f32[256,128]{1,0:T(8,128)S(1)}, f32[256,256]{1,0:T(8,128)S(1)}) custom-call(s32[3]{0:T(128)S(1)} %pad_add_fusion.refs_0_, s32[1,512]{1,0:T(1,128)} %bitcast.21, f32[512,512]{1,0:T(8,128)} %refs_2_.3), custom_call_target="tpu_custom_call" | custom-call | tf_op jit(solution)/shard_map/pallas_call | solution.py:162
  18.7 6.3 %shard_map.94 = (bf16[2,1024,1024]{2,1,0:T(8,128)(2,1)}, bf16[2,1024,1024]{2,1,0:T(8,128)(2,1)S(1)}) custom-call(bf16[2,1024,1024]{2,1,0:T(8,128)(2,1)} %bitcast.16, s32[2,1,256]{2,1,0:T(1,128)} %refs_1_.5, s32[2,1,256]{2,1,0:T(1,128)} %refs_2_.5, s32[2,1,512]{2,1,0:T(1,128)} %refs_3_.1), custom_call_target="tpu_custom_call" | custom-call | tf_op jit(solution)/shard_map/pallas_call | solution.py:162
  25.0 3.6 %shard_map.95 = (f32[2,256,256]{2,1,0:T(8,128)}, f32[2,256,256]{2,1,0:T(8,128)}, f32[256,256]{1,0:T(8,128)}, f32[256,256]{1,0:T(8,128)}, f32[256,256]{1,0:T(8,128)}) custom-call(f32[2,512,256]{2,1,0:T(8,128)} %bitcast.13, f32[2,264,256]{2,1,0:T(8,128)S(1)} %collective-permute-done.refs_1_.refs_2_, f32[264,256]{1,0:T(8,128)S(1)} %collective-permute-done.1.refs_2_.refs_3_, ...), custom_call_target="tpu_custom_call" | custom-call | tf_op jit(solution)/shard_map/pallas_call | solution.py:162
  28.8 1.7 %collective-permute-start.2 = (f32[2,256,256]{2,1,0:T(8,128)}, f32[2,256,256]{2,1,0:T(8,128)S(1)}, u32[]{:S(2)}, u32[]{:S(2)}) collective-permute-start(f32[2,256,256]{2,1,0:T(8,128)} %get-tuple-element.66.refs_3_), channel_id=1, source_target_pairs={{0,1},{1,2},{2,3},{3,4},{4,5},{5,6},{6,7},{7,8},{8,9},{9,10},{10,1... | collective-permute-start | bytes 1572872 | tf_op jit(solution)/shard_map/ppermute | solution.py:551
  31.6 8.8 %all-to-all-start.1 = ((f32[16,16,256]{2,1,0:T(8,128)}), f32[16,16,256]{2,1,0:T(8,128)S(1)}, u32[]{:S(2)}, u32[]{:S(2)}) async-start(f32[16,16,256]{2,1,0:T(8,128)} %shard_map.96), calls=%async_computation.1 | async-start | bytes 524288 | tf_op jit(solution)/shard_map/all_to_all | solution.py:600
  40.4 1.3 collective-permute-start.5
  41.7 2.4 %collective-permute-start.4 = (f32[256,256]{1,0:T(8,128)}, f32[256,256]{1,0:T(8,128)S(1)}, u32[]{:S(2)}, u32[]{:S(2)}) collective-permute-start(f32[256,256]{1,0:T(8,128)} %get-tuple-element.68.refs_5_), channel_id=1, source_target_pairs={{0,224},{32,0},{64,32},{96,64},{128,96},{160,128},{192,160},{224,1... | collective-permute-start | bytes 786440 | tf_op jit(solution)/shard_map/ppermute | solution.py:551
  44.1 2.2 %shard_map.97 = (bf16[7,48,256]{2,1,0:T(8,128)(2,1)}, bf16[7,256,128]{2,1,0:T(8,128)(2,1)}) custom-call(f32[2,4,512]{2,1,0:T(4,128)} %bitcast.20, f32[2,264,256]{2,1,0:T(8,128)} %copy-done.2, f32[264,256]{1,0:T(8,128)} %copy-done.3), custom_call_target="tpu_custom_call" | custom-call | tf_op jit(solution)/shard_map/pallas_call | solution.py:162
  46.3 6.3 %shard_map.98.refs_13_ = bf16[2,1024,1024]{2,1,0:T(8,128)(2,1)} custom-call(bf16[2,1024,1024]{2,1,0:T(8,128)(2,1)} %bitcast.17, s32[2,1,256]{2,1,0:T(1,128)} %refs_1_.5, s32[2,1,256]{2,1,0:T(1,128)} %refs_2_.5), custom_call_target="tpu_custom_call" | custom-call | tf_op jit(solution)/shard_map/pallas_call | solution.py:162
  53.4 3.5 %collective-permute-done.4.refs_9_ = f32[256,256]{1,0:T(8,128)S(1)} collective-permute-done((f32[256,256]{1,0:T(8,128)}, f32[256,256]{1,0:T(8,128)S(1)}, u32[]{:S(2)}, u32[]{:S(2)}) %collective-permute-start.4) | collective-permute-done | bytes 262176 | tf_op jit(solution)/shard_map/ppermute | solution.py:551
  56.9 7.8 %shard_map.99 = (f32[7,256,256]{2,1,0:T(8,128)}, f32[2,256,256]{2,1,0:T(8,128)}, f32[2,256,256]{2,1,0:T(8,128)}, f32[256,256]{1,0:T(8,128)}, f32[256,256]{1,0:T(...) custom-call(f32[16,16,256]{2,1,0:T(8,128)S(1)} %all-to-all-done.1.refs_0_, ...), custom_call_target="tpu_custom_call" | custom-call | tf_op jit(solution)/shard_map/pallas_call | solution.py:162
  64.7 6.2 %all-to-all-start.2 = ((f32[16,16,256]{2,1,0:T(8,128)}), f32[16,16,256]{2,1,0:T(8,128)S(1)}, u32[]{:S(2)}, u32[]{:S(2)}) async-start(f32[16,16,256]{2,1,0:T(8,128)} %get-tuple-element.72), calls=%async_computation.2 | async-start | bytes 524288 | tf_op jit(solution)/shard_map/all_to_all | solution.py:620
  72.7 5.5 %all-to-all-done.2.refs_0_ = f32[16,16,256]{2,1,0:T(8,128)S(1)} async-done(((f32[16,16,256]{2,1,0:T(8,128)}), f32[16,16,256]{2,1,0:T(8,128)S(1)}, u32[]{:S(2)}, u32[]{:S(2)}) %all-to-all-start.2) | async-done | bytes 262176 | tf_op jit(solution)/shard_map/all_to_all | solution.py:620
  78.3 1.1 shard_map.100
  79.4 7.3 %all-to-all-start.3 = ((f32[16,16,256]{2,1,0:T(8,128)}), f32[16,16,256]{2,1,0:T(8,128)S(1)}, u32[]{:S(2)}, u32[]{:S(2)}) async-start(f32[16,16,256]{2,1,0:T(8,128)} %shard_map.100), calls=%async_computation.3 | async-start | bytes 524288 | tf_op jit(solution)/shard_map/all_to_all | solution.py:622
  87.0 3.3 %collective-permute-start.8 = (f32[256,256]{1,0:T(8,128)}, f32[256,256]{1,0:T(8,128)S(1)}, u32[]{:S(2)}, u32[]{:S(2)}) collective-permute-start(f32[256,256]{1,0:T(8,128)} %get-tuple-element.78.refs_8_), channel_id=1, source_target_pairs={{0,224},{32,0},{64,32},{96,64},{128,96},{160,128},{192,160},{224,1... | collective-permute-start | bytes 786440 | tf_op jit(solution)/shard_map/ppermute | solution.py:551
  90.3 6.5 %collective-permute-done.9.refs_13_ = f32[256,256]{1,0:T(8,128)S(1)} collective-permute-done((f32[256,256]{1,0:T(8,128)}, f32[256,256]{1,0:T(8,128)S(1)}, u32[]{:S(2)}, u32[]{:S(2)}) %collective-permute-start.9) | collective-permute-done | bytes 262176 | tf_op jit(solution)/shard_map/ppermute | solution.py:551
  96.8 3.5 %collective-permute-done.8.refs_12_ = f32[256,256]{1,0:T(8,128)S(1)} collective-permute-done((f32[256,256]{1,0:T(8,128)}, f32[256,256]{1,0:T(8,128)S(1)}, u32[]{:S(2)}, u32[]{:S(2)}) %collective-permute-start.8) | collective-permute-done | bytes 262176 | tf_op jit(solution)/shard_map/ppermute | solution.py:551
  100.3 6.0 %shard_map.101 = (f32[4,256,256]{2,1,0:T(8,128)S(1)}, f32[4,256,256]{2,1,0:T(8,128)S(1)}, f32[2,256,256]{2,1,0:T(8,128)S(1)}, f32[2,256,256]{2,1,0:T(8,128)S(1)}...) custom-call(f32[16,16,256]{2,1,0:T(8,128)S(1)} %all-to-all-done.3.re, ...), custom_call_target="tpu_custom_call" | custom-call | tf_op jit(solution)/shard_map/pallas_call | solution.py:162
  106.3 1.3 collective-permute-start.11
  107.6 1.4 collective-permute-start.10
  109.3 3.3 %collective-permute-start.12 = (f32[256,256]{1,0:T(8,128)S(1)}, f32[256,256]{1,0:T(8,128)S(1)}, u32[]{:S(2)}, u32[]{:S(2)}) collective-permute-start(f32[256,256]{1,0:T(8,128)S(1)} %get-tuple-element.85.refs_5_), channel_id=1, source_target_pairs={{0,224},{32,0},{64,32},{96,64},{128,96},{160,128},{192,160},{224,1... | collective-permute-start | bytes 786440 | tf_op jit(solution)/shard_map/ppermute | solution.py:551
  112.5 4.8 %collective-permute-done.13.refs_10_ = f32[256,256]{1,0:T(8,128)S(1)} collective-permute-done((f32[256,256]{1,0:T(8,128)S(1)}, f32[256,256]{1,0:T(8,128)S(1)}, u32[]{:S(2)}, u32[]{:S(2)}) %collective-permute-start.13) | collective-permute-done | bytes 262176 | tf_op jit(solution)/shard_map/ppermute | solution.py:551
  117.4 8.6 %collective-permute-done.12.refs_9_ = f32[256,256]{1,0:T(8,128)S(1)} collective-permute-done((f32[256,256]{1,0:T(8,128)S(1)}, f32[256,256]{1,0:T(8,128)S(1)}, u32[]{:S(2)}, u32[]{:S(2)}) %collective-permute-start.12) | collective-permute-done | bytes 262176 | tf_op jit(solution)/shard_map/ppermute | solution.py:551
  126.0 2.4 %shard_map.102 = (f32[4,256,256]{2,1,0:T(8,128)S(1)}, f32[16,4,256]{2,1,0:T(4,128)}) custom-call(f32[16,256]{1,0:T(8,128)S(1)} %get-tuple-element.81.refs_0_, bf16[7,256,128]{2,1,0:T(8,128)(2,1)S(1)} %copy-done.4, f32[2,256,256]{2,1,0:T(8,128)S(1)} %get-tuple-element.82.refs_2_, f32[2,256,256]{2,1,0:T(8,128)S(1)} %get-tuple-element.83.refs_3_, ...), custom_call_target="tpu_custom_call" | custom-call | tf_op jit(solution)/shard_map/pallas_call | solution.py:162
  128.4 14.3 %all_to_all.30.refs_0_ = f32[16,4,256]{2,1,0:T(4,128)S(1)} all-to-all(f32[16,4,256]{2,1,0:T(4,128)} %get-tuple-element.90), channel_id=1, replica_groups=mesh['y'=4,'xl'=2,'xh'=2,'z'=8,'c'=2] {'z','c'}, dimensions={0} | all-to-all | bytes 131072 | tf_op jit(solution)/shard_map/all_to_all | solution.py:636
  143.3 12.5 %all_to_all.31.refs_0_ = f32[16,4,256]{2,1,0:T(4,128)S(1)} all-to-all(f32[16,4,256]{2,1,0:T(4,128)} %shard_map.103), channel_id=1, replica_groups=mesh['y'=4,'xl'=2,'xh'=2,'z'=8,'c'=2] {'y','xl','xh'}, dimensions={0} | all-to-all | bytes 131072 | tf_op jit(solution)/shard_map/all_to_all | solution.py:638
  (33 shorter events, 6.2 us)
Async XLA Ops:
  2.1 22.9 %collective-permute-start = (f32[2,264,256]{2,1,0:T(8,128)}, f32[2,264,256]{2,1,0:T(8,128)S(1)}, u32[]{:S(2)}, u32[]{:S(2)}) collective-permute-start(f32[2,264,256]{2,1,0:T(8,128)} %get-tuple-element.49), channel_id=1, source_target_pairs={{0,1},{1,2},{2,3},{3,4},{4,5},{5,6},{6,7},{7,8},{8,9},{9,10},{10,1... | collective-permute-start | bytes 1622024 | tf_op jit(solution)/shard_map/ppermute | solution.py:551
  5.2 19.8 %collective-permute-start.1 = (f32[264,256]{1,0:T(8,128)}, f32[264,256]{1,0:T(8,128)S(1)}, u32[]{:S(2)}, u32[]{:S(2)}) collective-permute-start(f32[264,256]{1,0:T(8,128)} %get-tuple-element.50), channel_id=1, source_target_pairs={{0,32},{32,64},{64,96},{96,128},{128,160},{160,192},{192,224},{224... | collective-permute-start | bytes 811016 | tf_op jit(solution)/shard_map/ppermute | solution.py:551
  8.9 19.8 %all-to-all-start = ((f32[16,8,256]{2,1,0:T(8,128)}), f32[16,8,256]{2,1,0:T(8,128)S(1)}, u32[]{:S(2)}, u32[]{:S(2)}) async-start(f32[16,8,256]{2,1,0:T(8,128)} %shard_map.91), calls=%async_computation | async-start | bytes 262144 | tf_op jit(solution)/shard_map/all_to_all | solution.py:576
  25.0 19.1 %copy-start.3 = (f32[264,256]{1,0:T(8,128)}, f32[264,256]{1,0:T(8,128)S(1)}, u32[]{:S(2)}) copy-start(f32[264,256]{1,0:T(8,128)S(1)} %collective-permute-done.1.refs_2_.refs_3_) | copy-start | bytes 811012
  25.0 19.1 %copy-start.2 = (f32[2,264,256]{2,1,0:T(8,128)}, f32[2,264,256]{2,1,0:T(8,128)S(1)}, u32[]{:S(2)}) copy-start(f32[2,264,256]{2,1,0:T(8,128)S(1)} %collective-permute-done.refs_1_.refs_2_) | copy-start | bytes 1622020
  28.7 28.2 %collective-permute-start.3 = (f32[2,256,256]{2,1,0:T(8,128)}, f32[2,256,256]{2,1,0:T(8,128)S(1)}, u32[]{:S(2)}, u32[]{:S(2)}) collective-permute-start(f32[2,256,256]{2,1,0:T(8,128)} %get-tuple-element.65.refs_2_), channel_id=1, source_target_pairs={{0,31},{1,0},{2,1},{3,2},{4,3},{5,4},{6,5},{7,6},{8,7},{9,8},{10,9... | collective-permute-start | bytes 1572872 | tf_op jit(solution)/shard_map/ppermute | solution.py:551
  28.8 28.1 %collective-permute-start.2 = (f32[2,256,256]{2,1,0:T(8,128)}, f32[2,256,256]{2,1,0:T(8,128)S(1)}, u32[]{:S(2)}, u32[]{:S(2)}) collective-permute-start(f32[2,256,256]{2,1,0:T(8,128)} %get-tuple-element.66.refs_3_), channel_id=1, source_target_pairs={{0,1},{1,2},{2,3},{3,4},{4,5},{5,6},{6,7},{7,8},{8,9},{9,10},{10,1... | collective-permute-start | bytes 1572872 | tf_op jit(solution)/shard_map/ppermute | solution.py:551
  31.6 25.3 %all-to-all-start.1 = ((f32[16,16,256]{2,1,0:T(8,128)}), f32[16,16,256]{2,1,0:T(8,128)S(1)}, u32[]{:S(2)}, u32[]{:S(2)}) async-start(f32[16,16,256]{2,1,0:T(8,128)} %shard_map.96), calls=%async_computation.1 | async-start | bytes 524288 | tf_op jit(solution)/shard_map/all_to_all | solution.py:600
  40.4 13.0 %collective-permute-start.5 = (f32[256,256]{1,0:T(8,128)}, f32[256,256]{1,0:T(8,128)S(1)}, u32[]{:S(2)}, u32[]{:S(2)}) collective-permute-start(f32[256,256]{1,0:T(8,128)} %get-tuple-element.67.refs_4_), channel_id=1, source_target_pairs={{0,32},{32,64},{64,96},{96,128},{128,160},{160,192},{192,224},{224... | collective-permute-start | bytes 786440 | tf_op jit(solution)/shard_map/ppermute | solution.py:551
  41.7 15.2 %collective-permute-start.4 = (f32[256,256]{1,0:T(8,128)}, f32[256,256]{1,0:T(8,128)S(1)}, u32[]{:S(2)}, u32[]{:S(2)}) collective-permute-start(f32[256,256]{1,0:T(8,128)} %get-tuple-element.68.refs_5_), channel_id=1, source_target_pairs={{0,224},{32,0},{64,32},{96,64},{128,96},{160,128},{192,160},{224,1... | collective-permute-start | bytes 786440 | tf_op jit(solution)/shard_map/ppermute | solution.py:551
  64.7 13.6 %all-to-all-start.2 = ((f32[16,16,256]{2,1,0:T(8,128)}), f32[16,16,256]{2,1,0:T(8,128)S(1)}, u32[]{:S(2)}, u32[]{:S(2)}) async-start(f32[16,16,256]{2,1,0:T(8,128)} %get-tuple-element.72), calls=%async_computation.2 | async-start | bytes 524288 | tf_op jit(solution)/shard_map/all_to_all | solution.py:620
  70.9 29.4 %collective-permute-start.7 = (f32[2,256,256]{2,1,0:T(8,128)}, f32[2,256,256]{2,1,0:T(8,128)S(1)}, u32[]{:S(2)}, u32[]{:S(2)}) collective-permute-start(f32[2,256,256]{2,1,0:T(8,128)} %get-tuple-element.75.refs_5_), channel_id=1, source_target_pairs={{0,31},{1,0},{2,1},{3,2},{4,3},{5,4},{6,5},{7,6},{8,7},{9,8},{10,9... | collective-permute-start | bytes 1572872 | tf_op jit(solution)/shard_map/ppermute | solution.py:551
  71.7 28.6 %collective-permute-start.6 = (f32[2,256,256]{2,1,0:T(8,128)}, f32[2,256,256]{2,1,0:T(8,128)S(1)}, u32[]{:S(2)}, u32[]{:S(2)}) collective-permute-start(f32[2,256,256]{2,1,0:T(8,128)} %get-tuple-element.76.refs_6_), channel_id=1, source_target_pairs={{0,1},{1,2},{2,3},{3,4},{4,5},{5,6},{6,7},{7,8},{8,9},{9,10},{10,1... | collective-permute-start | bytes 1572872 | tf_op jit(solution)/shard_map/ppermute | solution.py:551
  79.4 20.9 %all-to-all-start.3 = ((f32[16,16,256]{2,1,0:T(8,128)}), f32[16,16,256]{2,1,0:T(8,128)S(1)}, u32[]{:S(2)}, u32[]{:S(2)}) async-start(f32[16,16,256]{2,1,0:T(8,128)} %shard_map.100), calls=%async_computation.3 | async-start | bytes 524288 | tf_op jit(solution)/shard_map/all_to_all | solution.py:622
  86.7 10.1 %collective-permute-start.9 = (f32[256,256]{1,0:T(8,128)}, f32[256,256]{1,0:T(8,128)S(1)}, u32[]{:S(2)}, u32[]{:S(2)}) collective-permute-start(f32[256,256]{1,0:T(8,128)} %get-tuple-element.77.refs_7_), channel_id=1, source_target_pairs={{0,32},{32,64},{64,96},{96,128},{128,160},{160,192},{192,224},{224... | collective-permute-start | bytes 786440 | tf_op jit(solution)/shard_map/ppermute | solution.py:551
  87.0 13.3 %collective-permute-start.8 = (f32[256,256]{1,0:T(8,128)}, f32[256,256]{1,0:T(8,128)S(1)}, u32[]{:S(2)}, u32[]{:S(2)}) collective-permute-start(f32[256,256]{1,0:T(8,128)} %get-tuple-element.78.refs_8_), channel_id=1, source_target_pairs={{0,224},{32,0},{64,32},{96,64},{128,96},{160,128},{192,160},{224,1... | collective-permute-start | bytes 786440 | tf_op jit(solution)/shard_map/ppermute | solution.py:551
  100.3 25.7 %copy-start = (bf16[2,1024,1024]{2,1,0:T(8,128)(2,1)S(1)}, bf16[2,1024,1024]{2,1,0:T(8,128)(2,1)}, u32[]{:S(2)}) copy-start(bf16[2,1024,1024]{2,1,0:T(8,128)(2,1)} %shard_map.98.refs_13_) | copy-start | bytes 12582916
  100.3 25.7 %copy-start.1 = (f32[7,256,256]{2,1,0:T(8,128)S(1)}, f32[7,256,256]{2,1,0:T(8,128)}, u32[]{:S(2)}) copy-start(f32[7,256,256]{2,1,0:T(8,128)} %get-tuple-element.89.refs_14_.refs_2_) | copy-start | bytes 5505028
  100.3 25.7 %copy-start.4 = (bf16[7,256,128]{2,1,0:T(8,128)(2,1)S(1)}, bf16[7,256,128]{2,1,0:T(8,128)(2,1)}, u32[]{:S(2)}) copy-start(bf16[7,256,128]{2,1,0:T(8,128)(2,1)} %get-tuple-element.64.refs_1_) | copy-start | bytes 1376260
  106.3 19.6 %collective-permute-start.11 = (f32[2,256,256]{2,1,0:T(8,128)S(1)}, f32[2,256,256]{2,1,0:T(8,128)S(1)}, u32[]{:S(2)}, u32[]{:S(2)}) collective-permute-start(f32[2,256,256]{2,1,0:T(8,128)S(1)} %get-tuple-element.82.refs_2_), channel_id=1, source_target_pairs={{0,31},{1,0},{2,1},{3,2},{4,3},{5,4},{6,5},{7,6},{8,7},{9,8},{10,9... | collective-permute-start | bytes 1572872 | tf_op jit(solution)/shard_map/ppermute | solution.py:551
  107.6 18.3 %collective-permute-start.10 = (f32[2,256,256]{2,1,0:T(8,128)S(1)}, f32[2,256,256]{2,1,0:T(8,128)S(1)}, u32[]{:S(2)}, u32[]{:S(2)}) collective-permute-start(f32[2,256,256]{2,1,0:T(8,128)S(1)} %get-tuple-element.83.refs_3_), channel_id=1, source_target_pairs={{0,1},{1,2},{2,3},{3,4},{4,5},{5,6},{6,7},{7,8},{8,9},{9,10},{10,1... | collective-permute-start | bytes 1572872 | tf_op jit(solution)/shard_map/ppermute | solution.py:551
  109.0 8.4 %collective-permute-start.13 = (f32[256,256]{1,0:T(8,128)S(1)}, f32[256,256]{1,0:T(8,128)S(1)}, u32[]{:S(2)}, u32[]{:S(2)}) collective-permute-start(f32[256,256]{1,0:T(8,128)S(1)} %get-tuple-element.84.refs_4_), channel_id=1, source_target_pairs={{0,32},{32,64},{64,96},{96,128},{128,160},{160,192},{192,224},{224... | collective-permute-start | bytes 786440 | tf_op jit(solution)/shard_map/ppermute | solution.py:551
  109.3 16.7 %collective-permute-start.12 = (f32[256,256]{1,0:T(8,128)S(1)}, f32[256,256]{1,0:T(8,128)S(1)}, u32[]{:S(2)}, u32[]{:S(2)}) collective-permute-start(f32[256,256]{1,0:T(8,128)S(1)} %get-tuple-element.85.refs_5_), channel_id=1, source_target_pairs={{0,224},{32,0},{64,32},{96,64},{128,96},{160,128},{192,160},{224,1... | collective-permute-start | bytes 786440 | tf_op jit(solution)/shard_map/ppermute | solution.py:551
  126.0 29.8 %copy-start.5 = (f32[8,256]{1,0:T(8,128)S(1)}, f32[8,256]{1,0:T(8,128)}, u32[]{:S(2)}) copy-start(f32[8,256]{1,0:T(8,128)} %get-tuple-element.91.refs_1_) | copy-start | bytes 24580

commit v4 on v3

--- a/solution.py
+++ b/solution.py
@@ -1,6 +1,5 @@
 import jax
 import jax.numpy as jnp
-import numpy as np
 from jax import lax
 from jax.experimental import pallas as pl
 from jax.experimental.pallas import tpu as pltpu
@@ -123,9 +122,7 @@
         pass
 
 
-def call(kernel, outs, *args, flops=0, smem=(), near=(), near_out=(), parts=None, scratch=()):
-    size = sum(int(np.prod(a.shape)) * a.dtype.itemsize for a in args)
-    size += sum(int(np.prod(s)) * jnp.dtype(d).itemsize for s, d in outs)
+def call(kernel, outs, *args, smem=(), near=(), near_out=(), parts=None, scratch=()):
     inputs = [i for i in range(len(args)) if i not in smem]
     shapes = [(args[i].shape, args[i].dtype) for i in inputs] + list(outs)
     here = [i in near for i in inputs] + [i in near_out for i in range(len(outs))]
@@ -192,7 +189,7 @@
     return 1.0 / (1.0 + occ_ref[k].astype(F32))
 
 
-def pack_kernel(r, occ, basis, right, up):
+def open_kernel(r, occ, basis, right, up, loads):
     basis_ref, occ_ref = basis.get(), occ.get()
 
     def tail(k, part):
@@ -208,20 +205,13 @@
         right.send((k,))
     up.held[:F, :] = own_face(r, 3)
     up.send()
-
-
-def loads_kernel(r, basis, out):
-    basis_ref = basis.get()
-    for piece in HALF_PIECES:
-        r.get(piece)
-    first = jnp.dot(basis_ref[0], r.held[0], precision=EXACT, preferred_element_type=F32)
-    second = jnp.dot(basis_ref[1], r.held[1], precision=EXACT, preferred_element_type=F32)
+    own_face(r, 2)
+    one = jnp.dot(basis_ref[0], r.held[0], precision=EXACT, preferred_element_type=F32)
+    two = jnp.dot(basis_ref[1], r.held[1], precision=EXACT, preferred_element_type=F32)
+    rows = jnp.concatenate([one[0:2], one[2:4] + two[0:2], two[2:4], jnp.zeros((2, R), F32)], axis=0)
     for peer in range(16):
-        out.held[peer, 0:2, :] = first[0:2]
-        out.held[peer, 2:4, :] = first[2:4] + second[0:2]
-        out.held[peer, 4:6, :] = second[2:4]
-        out.held[peer, 6:8, :] = jnp.zeros((2, R), F32)
-    out.send()
+        loads.held[peer] = rows
+    loads.send()
 
 
 def scale_column(row):
@@ -323,7 +313,7 @@
     terms = thirds(inverse.get()[...])[::-1]
     picked = thirds(sum(nn(near_rows, part) for part in terms))[::-1]
     first.put(sum(nt(part, own_rows) for part in picked))
-    block = sum(nt(part, far_rows) for part in picked)
+    block = sum(nt(part, far_rows) for part in picked).T
     columns = lax.broadcasted_iota(jnp.int32, (16 * SLOTS, 16 * SLOTS), 1) & 15
     passed = (columns == entry) & spare
     later.put(jnp.where(passed, 1.0, block))
@@ -560,19 +550,17 @@
     )
 
 
-MATMUL_FLOPS = 2 * 2 * (4 * F) * (4 * F) * R
-
-
 def on_device(r, s_inverse, s, basis, occ, left_order, down_order, numbers, coarse_inverse):
     r, s_inverse, s, basis = r[:, 0], s_inverse[:, 0], s[:, 0], basis[:, 0]
     place = jnp.stack([lax.axis_index(BLK), lax.axis_index("xh"), lax.axis_index(NEAR)]).astype(jnp.int32)
     operand = pltpu.VMEM((2, 4 * F, R), BF16)
     strip = pltpu.VMEM((F, 4 * F), BF16)
 
-    right, up = call(pack_kernel, [((2, PACK, R), F32), ((PACK, R), F32)], r, occ, basis)
+    right, up, loads = call(
+        open_kernel, [((2, PACK, R), F32), ((PACK, R), F32), ((16, 8, R), F32)], r, occ, basis
+    )
     r_left = moved(right, CROSS, 32, 1)
     r_down = moved(up, BLK, 8, 1)
-    (loads,) = call(loads_kernel, [((16, 8, R), F32)], r, basis)
     far = lax.all_to_all(loads, FAR, 0, 0)
     first_block, later_block = call(
         coarse_block_kernel,
@@ -584,7 +572,7 @@
         reorder_weighted_kernel,
         [(s.shape, BF16), (s.shape, BF16)],
         s, left_order, down_order, occ,
-        flops=2 * MATMUL_FLOPS, near_out=(1,), scratch=[strip],
+        near_out=(1,), scratch=[strip],
     )
     r_left, r_down, first_block, later_block, schur_here = lax.optimization_barrier(
         (r_left, r_down, first_block, later_block, schur_here)
@@ -592,7 +580,7 @@
 
     halves = call(
         first_kernel, HALVES, r, r_left, r_down, schur_here,
-        flops=MATMUL_FLOPS, near=(1, 2, 3), scratch=[operand],
+        near=(1, 2, 3), scratch=[operand],
     )
     far, s_inverse, *halves = lax.optimization_barrier((far, s_inverse, *halves))
     others = exchanged(*halves[:4])
@@ -602,7 +590,7 @@
         reorder_plain_kernel,
         [(s_inverse.shape, BF16)],
         s_inverse, left_order, down_order,
-        flops=2 * MATMUL_FLOPS, scratch=[strip],
+        scratch=[strip],
     )
     rows, columns = call(
         basis_kernel,
@@ -614,24 +602,24 @@
         operate_first_kernel,
         [((FACES, F, R), F32), *HALVES, ((16, SLOTS, R), F32), ((SLOTS, R), F32)],
         values, columns, *halves, *others, r, rows, inverse_block,
-        flops=MATMUL_FLOPS, near=(0, 7, 8, 9, 10), scratch=[operand],
+        near=(0, 7, 8, 9, 10), scratch=[operand],
     )
     others = exchanged(*halves[:4])
-    far = lax.all_to_all(message, FAR, 0, 0)
-    (partial,) = call(partial_kernel, [((16, SLOTS, R), F32)], far, later_block, near=(0, 1))
-    values = lax.all_to_all(partial, NEAR, 0, 0)
+    near = lax.all_to_all(message, NEAR, 0, 0)
+    (partial,) = call(partial_kernel, [((16, SLOTS, R), F32)], near, later_block, near=(0, 1))
+    values = lax.all_to_all(partial, FAR, 0, 0)
     residual, image, *halves, corners, scalars = call(
         second_kernel,
         [((4, F, R), F32), ((4, F, R), F32), *HALVES, ((SLOTS, R), F32), ((8, R), F32)],
         values, corners, r_left, r_down, r, *halves, *others, schur_block,
-        flops=MATMUL_FLOPS, near=(0, 10, 11, 12, 13), near_out=(0, 1, 2, 3, 4, 5, 6, 7), scratch=[operand],
+        near=(0, 10, 11, 12, 13), near_out=(0, 1, 2, 3, 4, 5, 6, 7), scratch=[operand],
     )
     others = exchanged(*halves[:4])
     z1, message = call(
         operate_last_kernel,
         [((4, F, R), F32), ((16, 4, R), F32)],
         corners, columns, *halves, *others, residual, image, inverse_block, z0,
-        flops=MATMUL_FLOPS, near=tuple(range(15)), near_out=(0,), scratch=[operand, pltpu.VMEM((FACES, F, R), F32)],
+        near=tuple(range(15)), near_out=(0,), scratch=[operand, pltpu.VMEM((FACES, F, R), F32)],
     )
     near = lax.all_to_all(message, NEAR, 0, 0)
     (spread_sums,) = call(sum_kernel, [((16, 4, R), F32)], near, near=(0,))

time: 158 us -> 153 us (0.968)
  starting transfers between devices: 50.3 us -> 48 us
  Pallas kernels: 46.2 us -> 44.2 us
    ppermute x14, waiting for transfers between devices: 27.7 us -> 17.7 us  [moved(): lax.ppermute(block, axes, [(i, (i + distance) % count) for i in range(cou...]
    all_to_all x1 -> x2, waiting for transfers between devices: 5.54 us -> 15.3 us  [the longest x1 8.36 us: on_device(): values = lax.all_to_all(partial, FAR, 0, 0)]
    all_to_all x2 -> x1, starting transfers between devices: 16.1 us -> 8.77 us  [on_device(): values = lax.all_to_all(partial, NEAR, 0, 0)]
    all_to_all x1 -> x2, starting transfers between devices: 6.19 us -> 11.9 us  [the longest x1 5.94 us: on_device(): near = lax.all_to_all(message, NEAR, 0, 0)]
    pallas_call x14 -> x13, Pallas kernels: 46.2 us -> 44.2 us  [call(): pl.pallas_call(body, out_shape=[jax.ShapeDtypeStruct(s, d) if i in near_o...]
  transfers between devices with their start and end apart: 18 -> 18, of which waited for: 7 -> 6; matrix products, arithmetic and copies ran while one was open for 0% -> 0% of each run, Pallas kernels for 17% -> 16%
where the time goes in v4:
time: 153 us; the launch traced here: 152 us
  starting transfers between devices  48 us (31%)
  Pallas kernels  44.2 us (29%)
  waiting for transfers between devices  33 us (22%)
  blocking collectives  26 us (17%)
    pallas_call x13, Pallas kernels, call(): pl.pallas_call(body, out_shape=[jax.ShapeDtypeStruct(s, d) if i in near_o...  44.2 us
    ppermute x14, starting transfers between devices, moved(): lax.ppermute(block, axes, [(i, (i + distance) % count) for i in range(cou...  20.8 us
    ppermute x14, waiting for transfers between devices, moved(): lax.ppermute(block, axes, [(i, (i + distance) % count) for i in range(cou...  17.7 us
    all_to_all x1, blocking collectives, on_device(): near = lax.all_to_all(message, NEAR, 0, 0)  14.2 us
    all_to_all x1, blocking collectives, on_device(): sums = lax.all_to_all(spread_sums, FAR, 0, 0)  11.8 us
    all_to_all x1, starting transfers between devices, on_device(): values = lax.all_to_all(partial, NEAR, 0, 0)  8.77 us
    all_to_all x1, waiting for transfers between devices, on_device(): values = lax.all_to_all(partial, FAR, 0, 0)  8.36 us
    all_to_all x1, waiting for transfers between devices, on_device(): near = lax.all_to_all(message, NEAR, 0, 0)  6.92 us
  transfers between devices with their start and end apart: 18, of which 6 were waited for; matrix products, arithmetic and copies ran while one was open for 0% of the time, Pallas kernels for 16%

profile of v4, /device:TPU:1, one launch (start us, length us, event | category | flops | bytes accessed | tf_op | source)
XLA Modules:
  0.0 151.6 jit_solution(16007756276428062669)
XLA Ops:
  0.0 2.5 %shard_map.91 = (f32[2,264,256]{2,1,0:T(8,128)}, f32[264,256]{1,0:T(8,128)}, f32[16,8,256]{2,1,0:T(8,128)}) custom-call(f32[2,512,256]{2,1,0:T(8,128)} %bitcast.11, s32[2,1,512]{2,1,0:T(1,128)} %refs_3_.1, f32[2,4,512]{2,1,0:T(4,128)} %bitcast.17), custom_call_target="tpu_custom_call" | custom-call | tf_op jit(solution)/shard_map/pallas_call | solution.py:159
  2.5 3.1 %collective-permute-start = (f32[2,264,256]{2,1,0:T(8,128)}, f32[2,264,256]{2,1,0:T(8,128)S(1)}, u32[]{:S(2)}, u32[]{:S(2)}) collective-permute-start(f32[2,264,256]{2,1,0:T(8,128)} %get-tuple-element.51), channel_id=1, source_target_pairs={{0,1},{1,2},{2,3},{3,4},{4,5},{5,6},{6,7},{7,8},{8,9},{9,10},{10,1... | collective-permute-start | bytes 1622024 | tf_op jit(solution)/shard_map/ppermute | solution.py:541
  5.6 1.2 collective-permute-start.1
  6.9 6.5 %all-to-all-start = ((f32[16,8,256]{2,1,0:T(8,128)}), f32[16,8,256]{2,1,0:T(8,128)S(1)}, u32[]{:S(2)}, u32[]{:S(2)}) async-start(f32[16,8,256]{2,1,0:T(8,128)} %get-tuple-element.50), calls=%async_computation | async-start | bytes 262144 | tf_op jit(solution)/shard_map/all_to_all | solution.py:564
  13.5 3.2 %shard_map.92 = (f32[256,128]{1,0:T(8,128)S(1)}, f32[256,256]{1,0:T(8,128)S(1)}) custom-call(s32[3]{0:T(128)S(1)} %pad_add_fusion.refs_0_, s32[1,512]{1,0:T(1,128)} %bitcast.19, f32[512,512]{1,0:T(8,128)} %refs_2_.3), custom_call_target="tpu_custom_call" | custom-call | tf_op jit(solution)/shard_map/pallas_call | solution.py:159
  16.7 6.3 %shard_map.93 = (bf16[2,1024,1024]{2,1,0:T(8,128)(2,1)}, bf16[2,1024,1024]{2,1,0:T(8,128)(2,1)S(1)}) custom-call(bf16[2,1024,1024]{2,1,0:T(8,128)(2,1)} %bitcast.15, s32[2,1,256]{2,1,0:T(1,128)} %refs_1_.5, s32[2,1,256]{2,1,0:T(1,128)} %refs_2_.5, s32[2,1,512]{2,1,0:T(1,128)} %refs_3_.1), custom_call_target="tpu_custom_call" | custom-call | tf_op jit(solution)/shard_map/pallas_call | solution.py:159
  23.1 3.6 %shard_map.94 = (f32[2,256,256]{2,1,0:T(8,128)}, f32[2,256,256]{2,1,0:T(8,128)}, f32[256,256]{1,0:T(8,128)}, f32[256,256]{1,0:T(8,128)}, f32[256,256]{1,0:T(8,128)}) custom-call(f32[2,512,256]{2,1,0:T(8,128)} %bitcast.12, f32[2,264,256]{2,1,0:T(8,128)S(1)} %collective-permute-done.refs_1_.refs_2_, f32[264,256]{1,0:T(8,128)S(1)} %collective-permute-done.1.refs_2_.refs_3_, ...), custom_call_target="tpu_custom_call" | custom-call | tf_op jit(solution)/shard_map/pallas_call | solution.py:159
  27.1 1.4 collective-permute-start.2
  28.5 1.1 shard_map.95
  29.6 8.8 %all-to-all-start.1 = ((f32[16,16,256]{2,1,0:T(8,128)}), f32[16,16,256]{2,1,0:T(8,128)S(1)}, u32[]{:S(2)}, u32[]{:S(2)}) async-start(f32[16,16,256]{2,1,0:T(8,128)} %shard_map.95), calls=%async_computation.1 | async-start | bytes 524288 | tf_op jit(solution)/shard_map/all_to_all | solution.py:588
  38.4 1.4 collective-permute-start.5
  39.7 2.4 %collective-permute-start.4 = (f32[256,256]{1,0:T(8,128)}, f32[256,256]{1,0:T(8,128)S(1)}, u32[]{:S(2)}, u32[]{:S(2)}) collective-permute-start(f32[256,256]{1,0:T(8,128)} %get-tuple-element.70.refs_5_), channel_id=1, source_target_pairs={{0,224},{32,0},{64,32},{96,64},{128,96},{160,128},{192,160},{224,1... | collective-permute-start | bytes 786440 | tf_op jit(solution)/shard_map/ppermute | solution.py:541
  42.1 2.2 %shard_map.96 = (bf16[7,48,256]{2,1,0:T(8,128)(2,1)}, bf16[7,256,128]{2,1,0:T(8,128)(2,1)}) custom-call(f32[2,4,512]{2,1,0:T(4,128)} %bitcast.18, f32[2,264,256]{2,1,0:T(8,128)} %copy-done.2, f32[264,256]{1,0:T(8,128)} %copy-done.3), custom_call_target="tpu_custom_call" | custom-call | tf_op jit(solution)/shard_map/pallas_call | solution.py:159
  44.3 6.2 %shard_map.97.refs_13_ = bf16[2,1024,1024]{2,1,0:T(8,128)(2,1)} custom-call(bf16[2,1024,1024]{2,1,0:T(8,128)(2,1)} %bitcast.16, s32[2,1,256]{2,1,0:T(1,128)} %refs_1_.5, s32[2,1,256]{2,1,0:T(1,128)} %refs_2_.5), custom_call_target="tpu_custom_call" | custom-call | tf_op jit(solution)/shard_map/pallas_call | solution.py:159
  51.4 3.5 %collective-permute-done.4.refs_9_ = f32[256,256]{1,0:T(8,128)S(1)} collective-permute-done((f32[256,256]{1,0:T(8,128)}, f32[256,256]{1,0:T(8,128)S(1)}, u32[]{:S(2)}, u32[]{:S(2)}) %collective-permute-start.4) | collective-permute-done | bytes 262176 | tf_op jit(solution)/shard_map/ppermute | solution.py:541
  54.9 7.8 %shard_map.98 = (f32[7,256,256]{2,1,0:T(8,128)}, f32[2,256,256]{2,1,0:T(8,128)}, f32[2,256,256]{2,1,0:T(8,128)}, f32[256,256]{1,0:T(8,128)}, f32[256,256]{1,0:T(...) custom-call(f32[16,16,256]{2,1,0:T(8,128)S(1)} %all-to-all-done.1.refs_0_, ...), custom_call_target="tpu_custom_call" | custom-call | tf_op jit(solution)/shard_map/pallas_call | solution.py:159
  62.7 5.9 %all-to-all-start.2 = ((f32[16,16,256]{2,1,0:T(8,128)}), f32[16,16,256]{2,1,0:T(8,128)S(1)}, u32[]{:S(2)}, u32[]{:S(2)}) async-start(f32[16,16,256]{2,1,0:T(8,128)} %get-tuple-element.74), calls=%async_computation.2 | async-start | bytes 524288 | tf_op jit(solution)/shard_map/all_to_all | solution.py:608
  68.8 1.6 %collective-permute-start.6 = (f32[2,256,256]{2,1,0:T(8,128)}, f32[2,256,256]{2,1,0:T(8,128)S(1)}, u32[]{:S(2)}, u32[]{:S(2)}) collective-permute-start(f32[2,256,256]{2,1,0:T(8,128)} %get-tuple-element.78.refs_6_), channel_id=1, source_target_pairs={{0,1},{1,2},{2,3},{3,4},{4,5},{5,6},{6,7},{7,8},{8,9},{9,10},{10,1... | collective-permute-start | bytes 1572872 | tf_op jit(solution)/shard_map/ppermute | solution.py:541
  70.4 1.2 collective-permute-start.9
  71.6 2.4 %collective-permute-start.8 = (f32[256,256]{1,0:T(8,128)}, f32[256,256]{1,0:T(8,128)S(1)}, u32[]{:S(2)}, u32[]{:S(2)}) collective-permute-start(f32[256,256]{1,0:T(8,128)} %get-tuple-element.80.refs_8_), channel_id=1, source_target_pairs={{0,224},{32,0},{64,32},{96,64},{128,96},{160,128},{192,160},{224,1... | collective-permute-start | bytes 786440 | tf_op jit(solution)/shard_map/ppermute | solution.py:541
  74.0 6.9 %all-to-all-done.2.refs_0_ = f32[16,16,256]{2,1,0:T(8,128)S(1)} async-done(((f32[16,16,256]{2,1,0:T(8,128)}), f32[16,16,256]{2,1,0:T(8,128)S(1)}, u32[]{:S(2)}, u32[]{:S(2)}) %all-to-all-start.2) | async-done | bytes 262176 | tf_op jit(solution)/shard_map/all_to_all | solution.py:608
  80.9 1.1 shard_map.99
  82.0 5.9 %all-to-all-start.3 = ((f32[16,16,256]{2,1,0:T(8,128)}), f32[16,16,256]{2,1,0:T(8,128)S(1)}, u32[]{:S(2)}, u32[]{:S(2)}) async-start(f32[16,16,256]{2,1,0:T(8,128)} %shard_map.99), calls=%async_computation.3 | async-start | bytes 524288 | tf_op jit(solution)/shard_map/all_to_all | solution.py:610
  88.0 8.4 %all-to-all-done.3.refs_0_ = f32[16,16,256]{2,1,0:T(8,128)S(1)} async-done(((f32[16,16,256]{2,1,0:T(8,128)}), f32[16,16,256]{2,1,0:T(8,128)S(1)}, u32[]{:S(2)}, u32[]{:S(2)}) %all-to-all-start.3) | async-done | bytes 262176 | tf_op jit(solution)/shard_map/all_to_all | solution.py:610
  96.3 6.0 %shard_map.100 = (f32[4,256,256]{2,1,0:T(8,128)S(1)}, f32[4,256,256]{2,1,0:T(8,128)S(1)}, f32[2,256,256]{2,1,0:T(8,128)S(1)}, f32[2,256,256]{2,1,0:T(8,128)S(1)}...) custom-call(f32[16,16,256]{2,1,0:T(8,128)S(1)} %all-to-all-done.3.re, ...), custom_call_target="tpu_custom_call" | custom-call | tf_op jit(solution)/shard_map/pallas_call | solution.py:159
  104.7 3.3 %collective-permute-start.12 = (f32[256,256]{1,0:T(8,128)S(1)}, f32[256,256]{1,0:T(8,128)S(1)}, u32[]{:S(2)}, u32[]{:S(2)}) collective-permute-start(f32[256,256]{1,0:T(8,128)S(1)} %get-tuple-element.87.refs_5_), channel_id=1, source_target_pairs={{0,224},{32,0},{64,32},{96,64},{128,96},{160,128},{192,160},{224,1... | collective-permute-start | bytes 786440 | tf_op jit(solution)/shard_map/ppermute | solution.py:541
  108.0 3.8 %collective-permute-done.13.refs_10_ = f32[256,256]{1,0:T(8,128)S(1)} collective-permute-done((f32[256,256]{1,0:T(8,128)S(1)}, f32[256,256]{1,0:T(8,128)S(1)}, u32[]{:S(2)}, u32[]{:S(2)}) %collective-permute-start.13) | collective-permute-done | bytes 262176 | tf_op jit(solution)/shard_map/ppermute | solution.py:541
  111.7 9.6 %collective-permute-done.12.refs_9_ = f32[256,256]{1,0:T(8,128)S(1)} collective-permute-done((f32[256,256]{1,0:T(8,128)S(1)}, f32[256,256]{1,0:T(8,128)S(1)}, u32[]{:S(2)}, u32[]{:S(2)}) %collective-permute-start.12) | collective-permute-done | bytes 262176 | tf_op jit(solution)/shard_map/ppermute | solution.py:541
  121.4 2.4 %shard_map.101 = (f32[4,256,256]{2,1,0:T(8,128)S(1)}, f32[16,4,256]{2,1,0:T(4,128)}) custom-call(f32[16,256]{1,0:T(8,128)S(1)} %get-tuple-element.83.refs_0_, bf16[7,256,128]{2,1,0:T(8,128)(2,1)S(1)} %copy-done.4, f32[2,256,256]{2,1,0:T(8,128)S(1)} %get-tuple-element.84.refs_2_, f32[2,256,256]{2,1,0:T(8,128)S(1)} %get-tuple-element.85.refs_3_, ...), custom_call_target="tpu_custom_call" | custom-call | tf_op jit(solution)/shard_map/pallas_call | solution.py:159
  123.7 14.2 %all_to_all.30.refs_0_ = f32[16,4,256]{2,1,0:T(4,128)S(1)} all-to-all(f32[16,4,256]{2,1,0:T(4,128)} %get-tuple-element.92), channel_id=1, replica_groups=mesh['y'=4,'xl'=2,'xh'=2,'z'=8,'c'=2] {'z','c'}, dimensions={0} | all-to-all | bytes 131072 | tf_op jit(solution)/shard_map/all_to_all | solution.py:624
  138.6 11.8 %all_to_all.31.refs_0_ = f32[16,4,256]{2,1,0:T(4,128)S(1)} all-to-all(f32[16,4,256]{2,1,0:T(4,128)} %shard_map.102), channel_id=1, replica_groups=mesh['y'=4,'xl'=2,'xh'=2,'z'=8,'c'=2] {'y','xl','xh'}, dimensions={0} | all-to-all | bytes 131072 | tf_op jit(solution)/shard_map/all_to_all | solution.py:626
  150.4 1.1 shard_map.103
  (32 shorter events, 4.5 us)
Async XLA Ops:
  2.5 20.5 %collective-permute-start = (f32[2,264,256]{2,1,0:T(8,128)}, f32[2,264,256]{2,1,0:T(8,128)S(1)}, u32[]{:S(2)}, u32[]{:S(2)}) collective-permute-start(f32[2,264,256]{2,1,0:T(8,128)} %get-tuple-element.51), channel_id=1, source_target_pairs={{0,1},{1,2},{2,3},{3,4},{4,5},{5,6},{6,7},{7,8},{8,9},{9,10},{10,1... | collective-permute-start | bytes 1622024 | tf_op jit(solution)/shard_map/ppermute | solution.py:541
  5.6 17.4 %collective-permute-start.1 = (f32[264,256]{1,0:T(8,128)}, f32[264,256]{1,0:T(8,128)S(1)}, u32[]{:S(2)}, u32[]{:S(2)}) collective-permute-start(f32[264,256]{1,0:T(8,128)} %get-tuple-element.52), channel_id=1, source_target_pairs={{0,32},{32,64},{64,96},{96,128},{128,160},{160,192},{192,224},{224... | collective-permute-start | bytes 811016 | tf_op jit(solution)/shard_map/ppermute | solution.py:541
  6.9 19.8 %all-to-all-start = ((f32[16,8,256]{2,1,0:T(8,128)}), f32[16,8,256]{2,1,0:T(8,128)S(1)}, u32[]{:S(2)}, u32[]{:S(2)}) async-start(f32[16,8,256]{2,1,0:T(8,128)} %get-tuple-element.50), calls=%async_computation | async-start | bytes 262144 | tf_op jit(solution)/shard_map/all_to_all | solution.py:564
  23.0 19.1 %copy-start.3 = (f32[264,256]{1,0:T(8,128)}, f32[264,256]{1,0:T(8,128)S(1)}, u32[]{:S(2)}) copy-start(f32[264,256]{1,0:T(8,128)S(1)} %collective-permute-done.1.refs_2_.refs_3_) | copy-start | bytes 811012
  23.1 19.1 %copy-start.2 = (f32[2,264,256]{2,1,0:T(8,128)}, f32[2,264,256]{2,1,0:T(8,128)S(1)}, u32[]{:S(2)}) copy-start(f32[2,264,256]{2,1,0:T(8,128)S(1)} %collective-permute-done.refs_1_.refs_2_) | copy-start | bytes 1622020
  26.7 28.2 %collective-permute-start.3 = (f32[2,256,256]{2,1,0:T(8,128)}, f32[2,256,256]{2,1,0:T(8,128)S(1)}, u32[]{:S(2)}, u32[]{:S(2)}) collective-permute-start(f32[2,256,256]{2,1,0:T(8,128)} %get-tuple-element.67.refs_2_), channel_id=1, source_target_pairs={{0,31},{1,0},{2,1},{3,2},{4,3},{5,4},{6,5},{7,6},{8,7},{9,8},{10,9... | collective-permute-start | bytes 1572872 | tf_op jit(solution)/shard_map/ppermute | solution.py:541
  27.1 27.8 %collective-permute-start.2 = (f32[2,256,256]{2,1,0:T(8,128)}, f32[2,256,256]{2,1,0:T(8,128)S(1)}, u32[]{:S(2)}, u32[]{:S(2)}) collective-permute-start(f32[2,256,256]{2,1,0:T(8,128)} %get-tuple-element.68.refs_3_), channel_id=1, source_target_pairs={{0,1},{1,2},{2,3},{3,4},{4,5},{5,6},{6,7},{7,8},{8,9},{9,10},{10,1... | collective-permute-start | bytes 1572872 | tf_op jit(solution)/shard_map/ppermute | solution.py:541
  29.6 25.3 %all-to-all-start.1 = ((f32[16,16,256]{2,1,0:T(8,128)}), f32[16,16,256]{2,1,0:T(8,128)S(1)}, u32[]{:S(2)}, u32[]{:S(2)}) async-start(f32[16,16,256]{2,1,0:T(8,128)} %shard_map.95), calls=%async_computation.1 | async-start | bytes 524288 | tf_op jit(solution)/shard_map/all_to_all | solution.py:588
  38.4 13.0 %collective-permute-start.5 = (f32[256,256]{1,0:T(8,128)}, f32[256,256]{1,0:T(8,128)S(1)}, u32[]{:S(2)}, u32[]{:S(2)}) collective-permute-start(f32[256,256]{1,0:T(8,128)} %get-tuple-element.69.refs_4_), channel_id=1, source_target_pairs={{0,32},{32,64},{64,96},{96,128},{128,160},{160,192},{192,224},{224... | collective-permute-start | bytes 786440 | tf_op jit(solution)/shard_map/ppermute | solution.py:541
  39.7 15.2 %collective-permute-start.4 = (f32[256,256]{1,0:T(8,128)}, f32[256,256]{1,0:T(8,128)S(1)}, u32[]{:S(2)}, u32[]{:S(2)}) collective-permute-start(f32[256,256]{1,0:T(8,128)} %get-tuple-element.70.refs_5_), channel_id=1, source_target_pairs={{0,224},{32,0},{64,32},{96,64},{128,96},{160,128},{192,160},{224,1... | collective-permute-start | bytes 786440 | tf_op jit(solution)/shard_map/ppermute | solution.py:541
  62.7 18.2 %all-to-all-start.2 = ((f32[16,16,256]{2,1,0:T(8,128)}), f32[16,16,256]{2,1,0:T(8,128)S(1)}, u32[]{:S(2)}, u32[]{:S(2)}) async-start(f32[16,16,256]{2,1,0:T(8,128)} %get-tuple-element.74), calls=%async_computation.2 | async-start | bytes 524288 | tf_op jit(solution)/shard_map/all_to_all | solution.py:608
  68.7 19.3 %collective-permute-start.7 = (f32[2,256,256]{2,1,0:T(8,128)}, f32[2,256,256]{2,1,0:T(8,128)S(1)}, u32[]{:S(2)}, u32[]{:S(2)}) collective-permute-start(f32[2,256,256]{2,1,0:T(8,128)} %get-tuple-element.77.refs_5_), channel_id=1, source_target_pairs={{0,31},{1,0},{2,1},{3,2},{4,3},{5,4},{6,5},{7,6},{8,7},{9,8},{10,9... | collective-permute-start | bytes 1572872 | tf_op jit(solution)/shard_map/ppermute | solution.py:541
  68.8 19.1 %collective-permute-start.6 = (f32[2,256,256]{2,1,0:T(8,128)}, f32[2,256,256]{2,1,0:T(8,128)S(1)}, u32[]{:S(2)}, u32[]{:S(2)}) collective-permute-start(f32[2,256,256]{2,1,0:T(8,128)} %get-tuple-element.78.refs_6_), channel_id=1, source_target_pairs={{0,1},{1,2},{2,3},{3,4},{4,5},{5,6},{6,7},{7,8},{8,9},{9,10},{10,1... | collective-permute-start | bytes 1572872 | tf_op jit(solution)/shard_map/ppermute | solution.py:541
  70.4 17.5 %collective-permute-start.9 = (f32[256,256]{1,0:T(8,128)}, f32[256,256]{1,0:T(8,128)S(1)}, u32[]{:S(2)}, u32[]{:S(2)}) collective-permute-start(f32[256,256]{1,0:T(8,128)} %get-tuple-element.79.refs_7_), channel_id=1, source_target_pairs={{0,32},{32,64},{64,96},{96,128},{128,160},{160,192},{192,224},{224... | collective-permute-start | bytes 786440 | tf_op jit(solution)/shard_map/ppermute | solution.py:541
  71.6 16.4 %collective-permute-start.8 = (f32[256,256]{1,0:T(8,128)}, f32[256,256]{1,0:T(8,128)S(1)}, u32[]{:S(2)}, u32[]{:S(2)}) collective-permute-start(f32[256,256]{1,0:T(8,128)} %get-tuple-element.80.refs_8_), channel_id=1, source_target_pairs={{0,224},{32,0},{64,32},{96,64},{128,96},{160,128},{192,160},{224,1... | collective-permute-start | bytes 786440 | tf_op jit(solution)/shard_map/ppermute | solution.py:541
  82.0 14.3 %all-to-all-start.3 = ((f32[16,16,256]{2,1,0:T(8,128)}), f32[16,16,256]{2,1,0:T(8,128)S(1)}, u32[]{:S(2)}, u32[]{:S(2)}) async-start(f32[16,16,256]{2,1,0:T(8,128)} %shard_map.99), calls=%async_computation.3 | async-start | bytes 524288 | tf_op jit(solution)/shard_map/all_to_all | solution.py:610
  96.3 25.0 %copy-start = (bf16[2,1024,1024]{2,1,0:T(8,128)(2,1)S(1)}, bf16[2,1024,1024]{2,1,0:T(8,128)(2,1)}, u32[]{:S(2)}) copy-start(bf16[2,1024,1024]{2,1,0:T(8,128)(2,1)} %shard_map.97.refs_13_) | copy-start | bytes 12582916
  96.3 25.0 %copy-start.1 = (f32[7,256,256]{2,1,0:T(8,128)S(1)}, f32[7,256,256]{2,1,0:T(8,128)}, u32[]{:S(2)}) copy-start(f32[7,256,256]{2,1,0:T(8,128)} %get-tuple-element.91.refs_14_.refs_2_) | copy-start | bytes 5505028
  96.3 25.0 %copy-start.4 = (bf16[7,256,128]{2,1,0:T(8,128)(2,1)S(1)}, bf16[7,256,128]{2,1,0:T(8,128)(2,1)}, u32[]{:S(2)}) copy-start(bf16[7,256,128]{2,1,0:T(8,128)(2,1)} %get-tuple-element.66.refs_1_) | copy-start | bytes 1376260
  102.4 19.0 %collective-permute-start.11 = (f32[2,256,256]{2,1,0:T(8,128)S(1)}, f32[2,256,256]{2,1,0:T(8,128)S(1)}, u32[]{:S(2)}, u32[]{:S(2)}) collective-permute-start(f32[2,256,256]{2,1,0:T(8,128)S(1)} %get-tuple-element.84.refs_2_), channel_id=1, source_target_pairs={{0,31},{1,0},{2,1},{3,2},{4,3},{5,4},{6,5},{7,6},{8,7},{9,8},{10,9... | collective-permute-start | bytes 1572872 | tf_op jit(solution)/shard_map/ppermute | solution.py:541
  103.3 18.0 %collective-permute-start.10 = (f32[2,256,256]{2,1,0:T(8,128)S(1)}, f32[2,256,256]{2,1,0:T(8,128)S(1)}, u32[]{:S(2)}, u32[]{:S(2)}) collective-permute-start(f32[2,256,256]{2,1,0:T(8,128)S(1)} %get-tuple-element.85.refs_3_), channel_id=1, source_target_pairs={{0,1},{1,2},{2,3},{3,4},{4,5},{5,6},{6,7},{7,8},{8,9},{9,10},{10,1... | collective-permute-start | bytes 1572872 | tf_op jit(solution)/shard_map/ppermute | solution.py:541
  104.4 7.3 %collective-permute-start.13 = (f32[256,256]{1,0:T(8,128)S(1)}, f32[256,256]{1,0:T(8,128)S(1)}, u32[]{:S(2)}, u32[]{:S(2)}) collective-permute-start(f32[256,256]{1,0:T(8,128)S(1)} %get-tuple-element.86.refs_4_), channel_id=1, source_target_pairs={{0,32},{32,64},{64,96},{96,128},{128,160},{160,192},{192,224},{224... | collective-permute-start | bytes 786440 | tf_op jit(solution)/shard_map/ppermute | solution.py:541
  104.7 16.6 %collective-permute-start.12 = (f32[256,256]{1,0:T(8,128)S(1)}, f32[256,256]{1,0:T(8,128)S(1)}, u32[]{:S(2)}, u32[]{:S(2)}) collective-permute-start(f32[256,256]{1,0:T(8,128)S(1)} %get-tuple-element.87.refs_5_), channel_id=1, source_target_pairs={{0,224},{32,0},{64,32},{96,64},{128,96},{160,128},{192,160},{224,1... | collective-permute-start | bytes 786440 | tf_op jit(solution)/shard_map/ppermute | solution.py:541
  121.3 29.0 %copy-start.5 = (f32[8,256]{1,0:T(8,128)S(1)}, f32[8,256]{1,0:T(8,128)}, u32[]{:S(2)}) copy-start(f32[8,256]{1,0:T(8,128)} %get-tuple-element.93.refs_1_) | copy-start | bytes 24580

commit v5 on v4

--- a/solution.py
+++ b/solution.py
@@ -413,7 +413,7 @@
 
 def operate_first_kernel(
     values, columns, l0, r0, u0, d0, m0, fl, fr, fu, fd, r, rows, s,
-    z, left, right, up, down, mid, message, corners_out, operand_ref,
+    z, left, right, up, down, mid, message, corners_out, operand_ref, z_ref,
 ):
     corners = jnp.sum(values.get()[...], axis=0)
     corners_out.put(corners)
@@ -424,16 +424,17 @@
     progress = jnp.zeros((1, R), F32)
     for face in range(FACES):
         value = assembled(before, others, face) + nn(columns_ref[face], terms)
-        z.put(value, (face,))
+        z_ref[face] = value
         set_operand(operand_ref, face, value)
         if face < 4:
+            z.put(value, (face,))
             progress = progress + total(own_face(r, face) * value)
     rows_ref = rows.get()
     sums = [jnp.zeros((SLOTS, R), F32), jnp.zeros((1, R), F32)]
 
     def seen(face, image):
         sums[0] = sums[0] + face_loads(rows_ref, face, image)
-        sums[1] = sums[1] + total(z.held[face] * image)
+        sums[1] = sums[1] + total(z_ref[face] * image)
 
     apply_block(s, operand_ref, *images, seen=seen)
     loads, curvature = sums
@@ -478,7 +479,7 @@
 
 
 def operate_last_kernel(
-    corners_in, columns, l0, r0, u0, d0, m0, fl, fr, fu, fd, residual, image_in, s, z0,
+    corners_in, columns, l0, r0, u0, d0, m0, fl, fr, fu, fd, residual, image_in, s,
     z, message, operand_ref, z_ref,
 ):
     corners = corners_in.get()[...]
@@ -501,11 +502,10 @@
             image = nn(s.get(block_piece(k, side))[...], operand_ref[k])
             face = SIDES[k][side]
             curvature = curvature + total(z_ref[face] * image)
-            mixed = mixed + total(z0.get((face,))[...] * image)
     for peer in range(16):
         message.held[peer, 0:1, :] = progress
         message.held[peer, 1:2, :] = curvature
-        message.held[peer, 2:3, :] = mixed
+        message.held[peer, 2:3, :] = 2.0 * mixed
         message.held[peer, 3:4, :] = jnp.zeros((1, R), F32)
     message.send()
 
@@ -600,9 +600,9 @@
     )
     z0, *halves, message, corners = call(
         operate_first_kernel,
-        [((FACES, F, R), F32), *HALVES, ((16, SLOTS, R), F32), ((SLOTS, R), F32)],
+        [((4, F, R), F32), *HALVES, ((16, SLOTS, R), F32), ((SLOTS, R), F32)],
         values, columns, *halves, *others, r, rows, inverse_block,
-        near=(0, 7, 8, 9, 10), scratch=[operand],
+        near=(0, 7, 8, 9, 10), scratch=[operand, pltpu.VMEM((FACES, F, R), F32)],
     )
     others = exchanged(*halves[:4])
     near = lax.all_to_all(message, NEAR, 0, 0)
@@ -618,8 +618,8 @@
     z1, message = call(
         operate_last_kernel,
         [((4, F, R), F32), ((16, 4, R), F32)],
-        corners, columns, *halves, *others, residual, image, inverse_block, z0,
-        near=tuple(range(15)), near_out=(0,), scratch=[operand, pltpu.VMEM((FACES, F, R), F32)],
+        corners, columns, *halves, *others, residual, image, inverse_block,
+        near=tuple(range(14)), near_out=(0,), scratch=[operand, pltpu.VMEM((FACES, F, R), F32)],
     )
     near = lax.all_to_all(message, NEAR, 0, 0)
     (spread_sums,) = call(sum_kernel, [((16, 4, R), F32)], near, near=(0,))

time: 153 us -> 153 us (level)
  no operation moved by 1% of the time
where the time goes in v5:
time: 153 us; the launch traced here: 152 us
  starting transfers between devices  48 us (31%)
  Pallas kernels  44 us (29%)
  waiting for transfers between devices  33 us (22%)
  blocking collectives  26 us (17%)
    pallas_call x13, Pallas kernels, call(): pl.pallas_call(body, out_shape=[jax.ShapeDtypeStruct(s, d) if i in near_o...  44 us
    ppermute x14, starting transfers between devices, moved(): lax.ppermute(block, axes, [(i, (i + distance) % count) for i in range(cou...  20.8 us
    ppermute x14, waiting for transfers between devices, moved(): lax.ppermute(block, axes, [(i, (i + distance) % count) for i in range(cou...  17.7 us
    all_to_all x1, blocking collectives, on_device(): near = lax.all_to_all(message, NEAR, 0, 0)  14.2 us
    all_to_all x1, blocking collectives, on_device(): sums = lax.all_to_all(spread_sums, FAR, 0, 0)  11.8 us
    all_to_all x1, starting transfers between devices, on_device(): values = lax.all_to_all(partial, NEAR, 0, 0)  8.79 us
    all_to_all x1, waiting for transfers between devices, on_device(): values = lax.all_to_all(partial, FAR, 0, 0)  8.36 us
    all_to_all x1, waiting for transfers between devices, on_device(): near = lax.all_to_all(message, NEAR, 0, 0)  6.92 us
  transfers between devices with their start and end apart: 18, of which 6 were waited for; matrix products, arithmetic and copies ran while one was open for 0% of the time, Pallas kernels for 16%

profile of v5, /device:TPU:1, one launch (start us, length us, event | category | flops | bytes accessed | tf_op | source)
XLA Modules:
  0.0 151.5 jit_solution(18440123617166018353)
XLA Ops:
  0.0 2.5 %shard_map.91 = (f32[2,264,256]{2,1,0:T(8,128)}, f32[264,256]{1,0:T(8,128)}, f32[16,8,256]{2,1,0:T(8,128)}) custom-call(f32[2,512,256]{2,1,0:T(8,128)} %bitcast.11, s32[2,1,512]{2,1,0:T(1,128)} %refs_3_.1, f32[2,4,512]{2,1,0:T(4,128)} %bitcast.17), custom_call_target="tpu_custom_call" | custom-call | tf_op jit(solution)/shard_map/pallas_call | solution.py:159
  2.5 3.1 %collective-permute-start = (f32[2,264,256]{2,1,0:T(8,128)}, f32[2,264,256]{2,1,0:T(8,128)S(1)}, u32[]{:S(2)}, u32[]{:S(2)}) collective-permute-start(f32[2,264,256]{2,1,0:T(8,128)} %get-tuple-element.51), channel_id=1, source_target_pairs={{0,1},{1,2},{2,3},{3,4},{4,5},{5,6},{6,7},{7,8},{8,9},{9,10},{10,1... | collective-permute-start | bytes 1622024 | tf_op jit(solution)/shard_map/ppermute | solution.py:541
  5.6 1.2 collective-permute-start.1
  6.9 6.5 %all-to-all-start = ((f32[16,8,256]{2,1,0:T(8,128)}), f32[16,8,256]{2,1,0:T(8,128)S(1)}, u32[]{:S(2)}, u32[]{:S(2)}) async-start(f32[16,8,256]{2,1,0:T(8,128)} %get-tuple-element.50), calls=%async_computation | async-start | bytes 262144 | tf_op jit(solution)/shard_map/all_to_all | solution.py:564
  13.5 3.2 %shard_map.92 = (f32[256,128]{1,0:T(8,128)S(1)}, f32[256,256]{1,0:T(8,128)S(1)}) custom-call(s32[3]{0:T(128)S(1)} %pad_add_fusion.refs_0_, s32[1,512]{1,0:T(1,128)} %bitcast.19, f32[512,512]{1,0:T(8,128)} %refs_2_.3), custom_call_target="tpu_custom_call" | custom-call | tf_op jit(solution)/shard_map/pallas_call | solution.py:159
  16.7 6.3 %shard_map.93 = (bf16[2,1024,1024]{2,1,0:T(8,128)(2,1)}, bf16[2,1024,1024]{2,1,0:T(8,128)(2,1)S(1)}) custom-call(bf16[2,1024,1024]{2,1,0:T(8,128)(2,1)} %bitcast.15, s32[2,1,256]{2,1,0:T(1,128)} %refs_1_.5, s32[2,1,256]{2,1,0:T(1,128)} %refs_2_.5, s32[2,1,512]{2,1,0:T(1,128)} %refs_3_.1), custom_call_target="tpu_custom_call" | custom-call | tf_op jit(solution)/shard_map/pallas_call | solution.py:159
  23.0 3.6 %shard_map.94 = (f32[2,256,256]{2,1,0:T(8,128)}, f32[2,256,256]{2,1,0:T(8,128)}, f32[256,256]{1,0:T(8,128)}, f32[256,256]{1,0:T(8,128)}, f32[256,256]{1,0:T(8,128)}) custom-call(f32[2,512,256]{2,1,0:T(8,128)} %bitcast.12, f32[2,264,256]{2,1,0:T(8,128)S(1)} %collective-permute-done.refs_1_.refs_2_, f32[264,256]{1,0:T(8,128)S(1)} %collective-permute-done.1.refs_2_.refs_3_, ...), custom_call_target="tpu_custom_call" | custom-call | tf_op jit(solution)/shard_map/pallas_call | solution.py:159
  27.1 1.4 collective-permute-start.2
  28.5 1.1 shard_map.95
  29.6 8.8 %all-to-all-start.1 = ((f32[16,16,256]{2,1,0:T(8,128)}), f32[16,16,256]{2,1,0:T(8,128)S(1)}, u32[]{:S(2)}, u32[]{:S(2)}) async-start(f32[16,16,256]{2,1,0:T(8,128)} %shard_map.95), calls=%async_computation.1 | async-start | bytes 524288 | tf_op jit(solution)/shard_map/all_to_all | solution.py:588
  38.4 1.3 collective-permute-start.5
  39.7 2.4 %collective-permute-start.4 = (f32[256,256]{1,0:T(8,128)}, f32[256,256]{1,0:T(8,128)S(1)}, u32[]{:S(2)}, u32[]{:S(2)}) collective-permute-start(f32[256,256]{1,0:T(8,128)} %get-tuple-element.70.refs_5_), channel_id=1, source_target_pairs={{0,224},{32,0},{64,32},{96,64},{128,96},{160,128},{192,160},{224,1... | collective-permute-start | bytes 786440 | tf_op jit(solution)/shard_map/ppermute | solution.py:541
  42.1 2.2 %shard_map.96 = (bf16[7,48,256]{2,1,0:T(8,128)(2,1)}, bf16[7,256,128]{2,1,0:T(8,128)(2,1)}) custom-call(f32[2,4,512]{2,1,0:T(4,128)} %bitcast.18, f32[2,264,256]{2,1,0:T(8,128)} %copy-done.1, f32[264,256]{1,0:T(8,128)} %copy-done.2), custom_call_target="tpu_custom_call" | custom-call | tf_op jit(solution)/shard_map/pallas_call | solution.py:159
  44.3 6.3 %shard_map.97.refs_13_ = bf16[2,1024,1024]{2,1,0:T(8,128)(2,1)} custom-call(bf16[2,1024,1024]{2,1,0:T(8,128)(2,1)} %bitcast.16, s32[2,1,256]{2,1,0:T(1,128)} %refs_1_.5, s32[2,1,256]{2,1,0:T(1,128)} %refs_2_.5), custom_call_target="tpu_custom_call" | custom-call | tf_op jit(solution)/shard_map/pallas_call | solution.py:159
  51.4 3.5 %collective-permute-done.4.refs_9_ = f32[256,256]{1,0:T(8,128)S(1)} collective-permute-done((f32[256,256]{1,0:T(8,128)}, f32[256,256]{1,0:T(8,128)S(1)}, u32[]{:S(2)}, u32[]{:S(2)}) %collective-permute-start.4) | collective-permute-done | bytes 262176 | tf_op jit(solution)/shard_map/ppermute | solution.py:541
  54.9 7.7 %shard_map.98 = (f32[4,256,256]{2,1,0:T(8,128)}, f32[2,256,256]{2,1,0:T(8,128)}, f32[2,256,256]{2,1,0:T(8,128)}, f32[256,256]{1,0:T(8,128)}, f32[256,256]{1,0:T(...) custom-call(f32[16,16,256]{2,1,0:T(8,128)S(1)} %all-to-all-done.1.refs_0_, ...), custom_call_target="tpu_custom_call" | custom-call | tf_op jit(solution)/shard_map/pallas_call | solution.py:159
  62.7 6.0 %all-to-all-start.2 = ((f32[16,16,256]{2,1,0:T(8,128)}), f32[16,16,256]{2,1,0:T(8,128)S(1)}, u32[]{:S(2)}, u32[]{:S(2)}) async-start(f32[16,16,256]{2,1,0:T(8,128)} %get-tuple-element.74), calls=%async_computation.2 | async-start | bytes 524288 | tf_op jit(solution)/shard_map/all_to_all | solution.py:608
  68.8 1.6 %collective-permute-start.6 = (f32[2,256,256]{2,1,0:T(8,128)}, f32[2,256,256]{2,1,0:T(8,128)S(1)}, u32[]{:S(2)}, u32[]{:S(2)}) collective-permute-start(f32[2,256,256]{2,1,0:T(8,128)} %get-tuple-element.78.refs_6_), channel_id=1, source_target_pairs={{0,1},{1,2},{2,3},{3,4},{4,5},{5,6},{6,7},{7,8},{8,9},{9,10},{10,1... | collective-permute-start | bytes 1572872 | tf_op jit(solution)/shard_map/ppermute | solution.py:541
  70.4 1.2 collective-permute-start.9
  71.6 2.4 %collective-permute-start.8 = (f32[256,256]{1,0:T(8,128)}, f32[256,256]{1,0:T(8,128)S(1)}, u32[]{:S(2)}, u32[]{:S(2)}) collective-permute-start(f32[256,256]{1,0:T(8,128)} %get-tuple-element.80.refs_8_), channel_id=1, source_target_pairs={{0,224},{32,0},{64,32},{96,64},{128,96},{160,128},{192,160},{224,1... | collective-permute-start | bytes 786440 | tf_op jit(solution)/shard_map/ppermute | solution.py:541
  74.0 6.9 %all-to-all-done.2.refs_0_ = f32[16,16,256]{2,1,0:T(8,128)S(1)} async-done(((f32[16,16,256]{2,1,0:T(8,128)}), f32[16,16,256]{2,1,0:T(8,128)S(1)}, u32[]{:S(2)}, u32[]{:S(2)}) %all-to-all-start.2) | async-done | bytes 262176 | tf_op jit(solution)/shard_map/all_to_all | solution.py:608
  80.9 1.1 shard_map.99
  82.0 5.9 %all-to-all-start.3 = ((f32[16,16,256]{2,1,0:T(8,128)}), f32[16,16,256]{2,1,0:T(8,128)S(1)}, u32[]{:S(2)}, u32[]{:S(2)}) async-start(f32[16,16,256]{2,1,0:T(8,128)} %shard_map.99), calls=%async_computation.3 | async-start | bytes 524288 | tf_op jit(solution)/shard_map/all_to_all | solution.py:610
  87.9 8.4 %all-to-all-done.3.refs_0_ = f32[16,16,256]{2,1,0:T(8,128)S(1)} async-done(((f32[16,16,256]{2,1,0:T(8,128)}), f32[16,16,256]{2,1,0:T(8,128)S(1)}, u32[]{:S(2)}, u32[]{:S(2)}) %all-to-all-start.3) | async-done | bytes 262176 | tf_op jit(solution)/shard_map/all_to_all | solution.py:610
  96.3 6.0 %shard_map.100 = (f32[4,256,256]{2,1,0:T(8,128)S(1)}, f32[4,256,256]{2,1,0:T(8,128)S(1)}, f32[2,256,256]{2,1,0:T(8,128)S(1)}, f32[2,256,256]{2,1,0:T(8,128)S(1)}...) custom-call(f32[16,16,256]{2,1,0:T(8,128)S(1)} %all-to-all-done.3.re, ...), custom_call_target="tpu_custom_call" | custom-call | tf_op jit(solution)/shard_map/pallas_call | solution.py:159
  104.6 3.3 %collective-permute-start.12 = (f32[256,256]{1,0:T(8,128)S(1)}, f32[256,256]{1,0:T(8,128)S(1)}, u32[]{:S(2)}, u32[]{:S(2)}) collective-permute-start(f32[256,256]{1,0:T(8,128)S(1)} %get-tuple-element.87.refs_5_), channel_id=1, source_target_pairs={{0,224},{32,0},{64,32},{96,64},{128,96},{160,128},{192,160},{224,1... | collective-permute-start | bytes 786440 | tf_op jit(solution)/shard_map/ppermute | solution.py:541
  107.9 3.8 %collective-permute-done.13.refs_10_ = f32[256,256]{1,0:T(8,128)S(1)} collective-permute-done((f32[256,256]{1,0:T(8,128)S(1)}, f32[256,256]{1,0:T(8,128)S(1)}, u32[]{:S(2)}, u32[]{:S(2)}) %collective-permute-start.13) | collective-permute-done | bytes 262176 | tf_op jit(solution)/shard_map/ppermute | solution.py:541
  111.7 9.6 %collective-permute-done.12.refs_9_ = f32[256,256]{1,0:T(8,128)S(1)} collective-permute-done((f32[256,256]{1,0:T(8,128)S(1)}, f32[256,256]{1,0:T(8,128)S(1)}, u32[]{:S(2)}, u32[]{:S(2)}) %collective-permute-start.12) | collective-permute-done | bytes 262176 | tf_op jit(solution)/shard_map/ppermute | solution.py:541
  121.3 2.3 %shard_map.101 = (f32[4,256,256]{2,1,0:T(8,128)S(1)}, f32[16,4,256]{2,1,0:T(4,128)}) custom-call(f32[16,256]{1,0:T(8,128)S(1)} %get-tuple-element.83.refs_0_, bf16[7,256,128]{2,1,0:T(8,128)(2,1)S(1)} %copy-done.3, f32[2,256,256]{2,1,0:T(8,128)S(1)} %get-tuple-element.84.refs_2_, f32[2,256,256]{2,1,0:T(8,128)S(1)} %get-tuple-element.85.refs_3_, ...), custom_call_target="tpu_custom_call" | custom-call | tf_op jit(solution)/shard_map/pallas_call | solution.py:159
  123.6 14.2 %all_to_all.30.refs_0_ = f32[16,4,256]{2,1,0:T(4,128)S(1)} all-to-all(f32[16,4,256]{2,1,0:T(4,128)} %get-tuple-element.91), channel_id=1, replica_groups=mesh['y'=4,'xl'=2,'xh'=2,'z'=8,'c'=2] {'z','c'}, dimensions={0} | all-to-all | bytes 131072 | tf_op jit(solution)/shard_map/all_to_all | solution.py:624
  138.5 11.8 %all_to_all.31.refs_0_ = f32[16,4,256]{2,1,0:T(4,128)S(1)} all-to-all(f32[16,4,256]{2,1,0:T(4,128)} %shard_map.102), channel_id=1, replica_groups=mesh['y'=4,'xl'=2,'xh'=2,'z'=8,'c'=2] {'y','xl','xh'}, dimensions={0} | all-to-all | bytes 131072 | tf_op jit(solution)/shard_map/all_to_all | solution.py:626
  150.3 1.1 shard_map.103
  (32 shorter events, 4.6 us)
Async XLA Ops:
  2.5 20.5 %collective-permute-start = (f32[2,264,256]{2,1,0:T(8,128)}, f32[2,264,256]{2,1,0:T(8,128)S(1)}, u32[]{:S(2)}, u32[]{:S(2)}) collective-permute-start(f32[2,264,256]{2,1,0:T(8,128)} %get-tuple-element.51), channel_id=1, source_target_pairs={{0,1},{1,2},{2,3},{3,4},{4,5},{5,6},{6,7},{7,8},{8,9},{9,10},{10,1... | collective-permute-start | bytes 1622024 | tf_op jit(solution)/shard_map/ppermute | solution.py:541
  5.6 17.4 %collective-permute-start.1 = (f32[264,256]{1,0:T(8,128)}, f32[264,256]{1,0:T(8,128)S(1)}, u32[]{:S(2)}, u32[]{:S(2)}) collective-permute-start(f32[264,256]{1,0:T(8,128)} %get-tuple-element.52), channel_id=1, source_target_pairs={{0,32},{32,64},{64,96},{96,128},{128,160},{160,192},{192,224},{224... | collective-permute-start | bytes 811016 | tf_op jit(solution)/shard_map/ppermute | solution.py:541
  6.9 19.8 %all-to-all-start = ((f32[16,8,256]{2,1,0:T(8,128)}), f32[16,8,256]{2,1,0:T(8,128)S(1)}, u32[]{:S(2)}, u32[]{:S(2)}) async-start(f32[16,8,256]{2,1,0:T(8,128)} %get-tuple-element.50), calls=%async_computation | async-start | bytes 262144 | tf_op jit(solution)/shard_map/all_to_all | solution.py:564
  23.0 19.1 %copy-start.2 = (f32[264,256]{1,0:T(8,128)}, f32[264,256]{1,0:T(8,128)S(1)}, u32[]{:S(2)}) copy-start(f32[264,256]{1,0:T(8,128)S(1)} %collective-permute-done.1.refs_2_.refs_3_) | copy-start | bytes 811012
  23.0 19.1 %copy-start.1 = (f32[2,264,256]{2,1,0:T(8,128)}, f32[2,264,256]{2,1,0:T(8,128)S(1)}, u32[]{:S(2)}) copy-start(f32[2,264,256]{2,1,0:T(8,128)S(1)} %collective-permute-done.refs_1_.refs_2_) | copy-start | bytes 1622020
  26.7 28.2 %collective-permute-start.3 = (f32[2,256,256]{2,1,0:T(8,128)}, f32[2,256,256]{2,1,0:T(8,128)S(1)}, u32[]{:S(2)}, u32[]{:S(2)}) collective-permute-start(f32[2,256,256]{2,1,0:T(8,128)} %get-tuple-element.67.refs_2_), channel_id=1, source_target_pairs={{0,31},{1,0},{2,1},{3,2},{4,3},{5,4},{6,5},{7,6},{8,7},{9,8},{10,9... | collective-permute-start | bytes 1572872 | tf_op jit(solution)/shard_map/ppermute | solution.py:541
  27.1 27.8 %collective-permute-start.2 = (f32[2,256,256]{2,1,0:T(8,128)}, f32[2,256,256]{2,1,0:T(8,128)S(1)}, u32[]{:S(2)}, u32[]{:S(2)}) collective-permute-start(f32[2,256,256]{2,1,0:T(8,128)} %get-tuple-element.68.refs_3_), channel_id=1, source_target_pairs={{0,1},{1,2},{2,3},{3,4},{4,5},{5,6},{6,7},{7,8},{8,9},{9,10},{10,1... | collective-permute-start | bytes 1572872 | tf_op jit(solution)/shard_map/ppermute | solution.py:541
  29.6 25.3 %all-to-all-start.1 = ((f32[16,16,256]{2,1,0:T(8,128)}), f32[16,16,256]{2,1,0:T(8,128)S(1)}, u32[]{:S(2)}, u32[]{:S(2)}) async-start(f32[16,16,256]{2,1,0:T(8,128)} %shard_map.95), calls=%async_computation.1 | async-start | bytes 524288 | tf_op jit(solution)/shard_map/all_to_all | solution.py:588
  38.4 13.0 %collective-permute-start.5 = (f32[256,256]{1,0:T(8,128)}, f32[256,256]{1,0:T(8,128)S(1)}, u32[]{:S(2)}, u32[]{:S(2)}) collective-permute-start(f32[256,256]{1,0:T(8,128)} %get-tuple-element.69.refs_4_), channel_id=1, source_target_pairs={{0,32},{32,64},{64,96},{96,128},{128,160},{160,192},{192,224},{224... | collective-permute-start | bytes 786440 | tf_op jit(solution)/shard_map/ppermute | solution.py:541
  39.7 15.2 %collective-permute-start.4 = (f32[256,256]{1,0:T(8,128)}, f32[256,256]{1,0:T(8,128)S(1)}, u32[]{:S(2)}, u32[]{:S(2)}) collective-permute-start(f32[256,256]{1,0:T(8,128)} %get-tuple-element.70.refs_5_), channel_id=1, source_target_pairs={{0,224},{32,0},{64,32},{96,64},{128,96},{160,128},{192,160},{224,1... | collective-permute-start | bytes 786440 | tf_op jit(solution)/shard_map/ppermute | solution.py:541
  62.7 18.2 %all-to-all-start.2 = ((f32[16,16,256]{2,1,0:T(8,128)}), f32[16,16,256]{2,1,0:T(8,128)S(1)}, u32[]{:S(2)}, u32[]{:S(2)}) async-start(f32[16,16,256]{2,1,0:T(8,128)} %get-tuple-element.74), calls=%async_computation.2 | async-start | bytes 524288 | tf_op jit(solution)/shard_map/all_to_all | solution.py:608
  68.6 19.3 %collective-permute-start.7 = (f32[2,256,256]{2,1,0:T(8,128)}, f32[2,256,256]{2,1,0:T(8,128)S(1)}, u32[]{:S(2)}, u32[]{:S(2)}) collective-permute-start(f32[2,256,256]{2,1,0:T(8,128)} %get-tuple-element.77.refs_5_), channel_id=1, source_target_pairs={{0,31},{1,0},{2,1},{3,2},{4,3},{5,4},{6,5},{7,6},{8,7},{9,8},{10,9... | collective-permute-start | bytes 1572872 | tf_op jit(solution)/shard_map/ppermute | solution.py:541
  68.8 19.1 %collective-permute-start.6 = (f32[2,256,256]{2,1,0:T(8,128)}, f32[2,256,256]{2,1,0:T(8,128)S(1)}, u32[]{:S(2)}, u32[]{:S(2)}) collective-permute-start(f32[2,256,256]{2,1,0:T(8,128)} %get-tuple-element.78.refs_6_), channel_id=1, source_target_pairs={{0,1},{1,2},{2,3},{3,4},{4,5},{5,6},{6,7},{7,8},{8,9},{9,10},{10,1... | collective-permute-start | bytes 1572872 | tf_op jit(solution)/shard_map/ppermute | solution.py:541
  70.4 17.5 %collective-permute-start.9 = (f32[256,256]{1,0:T(8,128)}, f32[256,256]{1,0:T(8,128)S(1)}, u32[]{:S(2)}, u32[]{:S(2)}) collective-permute-start(f32[256,256]{1,0:T(8,128)} %get-tuple-element.79.refs_7_), channel_id=1, source_target_pairs={{0,32},{32,64},{64,96},{96,128},{128,160},{160,192},{192,224},{224... | collective-permute-start | bytes 786440 | tf_op jit(solution)/shard_map/ppermute | solution.py:541
  71.6 16.3 %collective-permute-start.8 = (f32[256,256]{1,0:T(8,128)}, f32[256,256]{1,0:T(8,128)S(1)}, u32[]{:S(2)}, u32[]{:S(2)}) collective-permute-start(f32[256,256]{1,0:T(8,128)} %get-tuple-element.80.refs_8_), channel_id=1, source_target_pairs={{0,224},{32,0},{64,32},{96,64},{128,96},{160,128},{192,160},{224,1... | collective-permute-start | bytes 786440 | tf_op jit(solution)/shard_map/ppermute | solution.py:541
  82.0 14.3 %all-to-all-start.3 = ((f32[16,16,256]{2,1,0:T(8,128)}), f32[16,16,256]{2,1,0:T(8,128)S(1)}, u32[]{:S(2)}, u32[]{:S(2)}) async-start(f32[16,16,256]{2,1,0:T(8,128)} %shard_map.99), calls=%async_computation.3 | async-start | bytes 524288 | tf_op jit(solution)/shard_map/all_to_all | solution.py:610
  96.3 25.0 %copy-start = (bf16[2,1024,1024]{2,1,0:T(8,128)(2,1)S(1)}, bf16[2,1024,1024]{2,1,0:T(8,128)(2,1)}, u32[]{:S(2)}) copy-start(bf16[2,1024,1024]{2,1,0:T(8,128)(2,1)} %shard_map.97.refs_13_) | copy-start | bytes 12582916
  96.3 25.0 %copy-start.3 = (bf16[7,256,128]{2,1,0:T(8,128)(2,1)S(1)}, bf16[7,256,128]{2,1,0:T(8,128)(2,1)}, u32[]{:S(2)}) copy-start(bf16[7,256,128]{2,1,0:T(8,128)(2,1)} %get-tuple-element.66.refs_1_) | copy-start | bytes 1376260
  102.3 19.0 %collective-permute-start.11 = (f32[2,256,256]{2,1,0:T(8,128)S(1)}, f32[2,256,256]{2,1,0:T(8,128)S(1)}, u32[]{:S(2)}, u32[]{:S(2)}) collective-permute-start(f32[2,256,256]{2,1,0:T(8,128)S(1)} %get-tuple-element.84.refs_2_), channel_id=1, source_target_pairs={{0,31},{1,0},{2,1},{3,2},{4,3},{5,4},{6,5},{7,6},{8,7},{9,8},{10,9... | collective-permute-start | bytes 1572872 | tf_op jit(solution)/shard_map/ppermute | solution.py:541
  103.3 18.0 %collective-permute-start.10 = (f32[2,256,256]{2,1,0:T(8,128)S(1)}, f32[2,256,256]{2,1,0:T(8,128)S(1)}, u32[]{:S(2)}, u32[]{:S(2)}) collective-permute-start(f32[2,256,256]{2,1,0:T(8,128)S(1)} %get-tuple-element.85.refs_3_), channel_id=1, source_target_pairs={{0,1},{1,2},{2,3},{3,4},{4,5},{5,6},{6,7},{7,8},{8,9},{9,10},{10,1... | collective-permute-start | bytes 1572872 | tf_op jit(solution)/shard_map/ppermute | solution.py:541
  104.3 7.3 %collective-permute-start.13 = (f32[256,256]{1,0:T(8,128)S(1)}, f32[256,256]{1,0:T(8,128)S(1)}, u32[]{:S(2)}, u32[]{:S(2)}) collective-permute-start(f32[256,256]{1,0:T(8,128)S(1)} %get-tuple-element.86.refs_4_), channel_id=1, source_target_pairs={{0,32},{32,64},{64,96},{96,128},{128,160},{160,192},{192,224},{224... | collective-permute-start | bytes 786440 | tf_op jit(solution)/shard_map/ppermute | solution.py:541
  104.6 16.6 %collective-permute-start.12 = (f32[256,256]{1,0:T(8,128)S(1)}, f32[256,256]{1,0:T(8,128)S(1)}, u32[]{:S(2)}, u32[]{:S(2)}) collective-permute-start(f32[256,256]{1,0:T(8,128)S(1)} %get-tuple-element.87.refs_5_), channel_id=1, source_target_pairs={{0,224},{32,0},{64,32},{96,64},{128,96},{160,128},{192,160},{224,1... | collective-permute-start | bytes 786440 | tf_op jit(solution)/shard_map/ppermute | solution.py:541
  121.3 29.0 %copy-start.4 = (f32[4,256,256]{2,1,0:T(8,128)S(1)}, f32[4,256,256]{2,1,0:T(8,128)}, u32[]{:S(2)}) copy-start(f32[4,256,256]{2,1,0:T(8,128)} %get-tuple-element.93.refs_2_) | copy-start | bytes 3145732
  121.3 29.0 %copy-start.5 = (f32[8,256]{1,0:T(8,128)S(1)}, f32[8,256]{1,0:T(8,128)}, u32[]{:S(2)}) copy-start(f32[8,256]{1,0:T(8,128)} %get-tuple-element.92.refs_1_) | copy-start | bytes 24580
